TPU v7x, 32 devices: a whole 2x2x4 slice. The times are simulated.
32 devices in a mesh: groups: 2 (over y), feat: 4 (over z), rows: 2 (over x), sub: 2 (over core).
Axes of the slice: x: 2, y: 2, z: 4, core: 2. Of those that a mesh axis runs over, the one named last changes fastest.
Arguments:
- acts: bfloat16 [256, 32, 8192], P(('groups', 'rows', 'sub'), None, 'feat'), parts along dimension 0, may hold values from -6 to 6
- out_grads: bfloat16 [256, 32, 8192], P(('groups', 'rows', 'sub'), None, 'feat'), parts along dimension 0, may hold values from -6 to 6
- proj_in: bfloat16 [8192, 128], P('feat'), may hold values from -0.0625 to 0.0625
- proj_out: bfloat16 [8192, 128], P('feat'), may hold values from -0.0625 to 0.0625
- store: float32 [5120, 16384], P(('groups', 'rows', 'sub'), 'feat'), parts along dimension 0, may hold values from -0.0084 to 0.0084
Outputs:
- scores: float32 [256, 2560], P(('groups', 'feat'), ('rows', 'sub')), parts along dimension 0
There are 2 independent parts, one for each index of `groups`. A program takes and returns all parts, laid end to end along the dimension named above; an argument that names none is the same for every part. Nothing has to cross between parts.
All inputs are finite; a program needn't handle non-finite values.
Results may differ from a plain program's by a relative error of at most 0.0003.
Values sent between devices are 32-bit elements; how exact they have to be, the bound alone decides.
No kernel may reach another device: no remote copies, remote signals or barrier semaphores. Data moves between devices by JAX's collectives and lax.ppermute only.
A program may use at most 64 MiB of HBM per device.

v0:
```python
import jax
import jax.numpy as jnp
from jax import lax
from jax.sharding import PartitionSpec as P


def score_block(grads_block, store):
    return lax.dot_general(
        grads_block,
        store,
        (((1,), (1,)), ((), ())),
        precision=lax.Precision.HIGHEST,
        preferred_element_type=jnp.float32,
    )


def local(acts, out_grads, proj_in, proj_out, store):
    queries_here = acts.shape[0]
    tokens = acts.shape[1]
    width_here = acts.shape[2]
    rank = proj_in.shape[1]
    in_part = jnp.dot(
        acts.reshape(queries_here * tokens, width_here), proj_in, preferred_element_type=jnp.float32
    )
    out_part = jnp.dot(
        out_grads.reshape(queries_here * tokens, width_here),
        proj_out,
        preferred_element_type=jnp.float32,
    )
    in_owned, out_owned = (
        lax.psum_scatter(
            in_part.reshape(queries_here, tokens, rank), "feat", scatter_dimension=0, tiled=True
        ),
        lax.psum_scatter(
            out_part.reshape(queries_here, tokens, rank), "feat", scatter_dimension=0, tiled=True
        ),
    )
    owned = in_owned.shape[0]
    full_grad = jnp.einsum(
        "qti,qtj->qij", out_owned, in_owned, precision=lax.Precision.HIGHEST
    ).reshape(owned, rank * rank)
    query_grad = lax.all_to_all(full_grad, "feat", split_axis=1, concat_axis=0, tiled=True)
    partial_scores = score_block(
        lax.all_gather(query_grad, ("rows", "sub"), axis=0, tiled=True), store
    )
    scores = lax.psum_scatter(partial_scores, "feat", scatter_dimension=0, tiled=True)
    return scores


def solution(mesh):
    return jax.shard_map(
        local,
        mesh=mesh,
        in_specs=(
            P(("groups", "rows", "sub"), None, "feat"),
            P(("groups", "rows", "sub"), None, "feat"),
            P("feat", None),
            P("feat", None),
            P(("groups", "rows", "sub"), "feat"),
        ),
        out_specs=P(("groups", "feat"), ("rows", "sub")),
        check_vma=False,
    )
```

profile of v0, /device:TPU:0, one launch (start us, length us, event | category | flops | bytes accessed | tf_op | source)
XLA Modules:
  0.0 141.3 jit_solution(16457488728892822400)
XLA Ops:
  6.5 0.0 copy-start
  6.5 0.0 copy-start.1
  6.5 0.0 reduce-scatter.6.cloned.1.call-start
  6.5 1.0 copy-done
  7.6 4.2 %fusion = f32[32,32,128]{2,1,0:T(8,128)} fusion(bf16[32,32,2048]{2,1,0:T(8,128)(2,1)} %param.5, bf16[2048,128]{1,0:T(8,128)(2,1)S(1)} %copy-done), kind=kOutput, calls=%fused_computation | convolution fusion | flops 536870912 | bytes 5242880 | tf_op jit(solution)/shard_map/dot_general | solution.py:22
  11.8 0.0 reduce-scatter.6.cloned.1.call-update
  11.8 0.0 reduce-scatter.4.cloned.1.call-start
  11.9 0.0 copy-done.1
  11.9 4.2 %fusion.2 = f32[32,32,128]{2,1,0:T(8,128)} fusion(bf16[32,32,2048]{2,1,0:T(8,128)(2,1)} %param.6, bf16[2048,128]{1,0:T(8,128)(2,1)S(1)} %copy-done.1), kind=kOutput, calls=%fused_computation.2 | convolution fusion | flops 536870912 | bytes 5242880 | tf_op jit(solution)/shard_map/dot_general | solution.py:25
  16.1 0.0 reduce-scatter.4.cloned.1.call-update
  16.1 0.0 all-gather.2.cloned.1.call-start
  16.2 20.1 %reduce-scatter.6.cloned.1.call-done = f32[8,32,128]{2,1,0:T(8,128)} async-done(((f32[32,32,128]{2,1,0:T(8,128)}), f32[8,32,128]{2,1,0:T(8,128)}) %reduce-scatter.6.cloned.1.call-update) | async-done | bytes 131088 | tf_op jit(solution)/shard_map/reduce_scatter | solution.py:31
  36.3 22.2 %reduce-scatter.4.cloned.1.call-done = f32[8,32,128]{2,1,0:T(8,128)} async-done(((f32[32,32,128]{2,1,0:T(8,128)}), f32[8,32,128]{2,1,0:T(8,128)}) %reduce-scatter.4.cloned.1.call-update) | async-done | bytes 131088 | tf_op jit(solution)/shard_map/reduce_scatter | solution.py:34
  58.6 2.0 %fusion.4 = f32[8,128,128]{2,1,0:T(8,128)S(1)} fusion(f32[8,32,128]{2,1,0:T(8,128)} %reduce-scatter.4.cloned.1.call-done, f32[8,32,128]{2,1,0:T(8,128)} %reduce-scatter.6.cloned.1.call-done), kind=kOutput, calls=%fused_computation.4 | convolution fusion | flops 50331648 | bytes 786432 | tf_op jit(solution)/shard_map/qti,qtj->qij/dot_general | solution.py:39
  60.5 0.2 all_to_all.14
  60.7 0.3 copy.6
  61.0 15.9 %all_to_all.19 = f32[8,4,4096]{2,0,1:T(8,128)} all-to-all(f32[8,4,4096]{2,0,1:T(8,128)S(1)} %copy.6), channel_id=1, replica_groups=mesh['groups'=2,'feat'=4,'rows'=2,'sub'=2] {'feat'}, dimensions={1} | all-to-all | bytes 1048576 | tf_op jit(solution)/shard_map/all_to_all | solution.py:42
  77.0 0.0 all-gather.2.cloned.1.call-update
  77.0 0.2 reduce-scatter.8.cloned.1.call-start
  77.3 21.7 %all-gather.2.cloned.1.call-done = f32[128,4096]{1,0:T(8,128)} async-done(((f32[32,4096]{1,0:T(8,128)}), f32[128,4096]{1,0:T(8,128)}) %all-gather.2.cloned.1.call-update) | async-done | bytes 2097168 | tf_op jit(solution)/shard_map/all_gather | solution.py:44
  99.0 15.5 %fusion.5 = f32[128,640]{1,0:T(8,128)} fusion(f32[128,4096]{1,0:T(8,128)} %all-gather.2.cloned.1.call-done, f32[640,4096]{1,0:T(8,128)} %param.9), kind=kOutput, calls=%fused_computation.5 | convolution fusion | flops 4026531840 | bytes 12910592 | tf_op jit(solution)/shard_map/dot_general | solution.py:8
  114.5 0.0 reduce-scatter.8.cloned.1.call-update
  114.6 20.2 %reduce-scatter.8.cloned.1.call-done = f32[32,640]{1,0:T(8,128)} async-done(((f32[128,640]{1,0:T(8,128)}), f32[32,640]{1,0:T(8,128)}) %reduce-scatter.8.cloned.1.call-update) | async-done | bytes 81936 | tf_op jit(solution)/shard_map/reduce_scatter | solution.py:46
Async XLA Ops:
  6.5 1.0 copy-start
  6.5 5.3 %copy-start.1 = (bf16[2048,128]{1,0:T(8,128)(2,1)S(1)}, bf16[2048,128]{1,0:T(8,128)(2,1)}, u32[]{:S(2)}) copy-start(bf16[2048,128]{1,0:T(8,128)(2,1)} %param.8) | copy-start | bytes 1572868
  6.5 29.8 %reduce-scatter.6.cloned.1.call-start = ((), (), s32[]{:S(2)}) async-start(), calls=%async_computation.5 | async-start | bytes 655360 | tf_op jit(solution)/shard_map/reduce_scatter | solution.py:31
  11.8 46.7 %reduce-scatter.4.cloned.1.call-start = ((), (), s32[]{:S(2)}) async-start(), calls=%async_computation.4 | async-start | bytes 655360 | tf_op jit(solution)/shard_map/reduce_scatter | solution.py:34
  16.1 82.8 %all-gather.2.cloned.1.call-start = ((), (), s32[]{:S(2)}) async-start(), calls=%async_computation.6 | async-start | bytes 2621440 | tf_op jit(solution)/shard_map/all_gather | solution.py:44
  77.0 57.7 %reduce-scatter.8.cloned.1.call-start = ((), (), s32[]{:S(2)}) async-start(), calls=%async_computation.7 | async-start | bytes 409600 | tf_op jit(solution)/shard_map/reduce_scatter | solution.py:46
Sparse Core Ops, SparseCore 0:
  12.0 24.3 reduce-scatter.5
  38.6 19.9 reduce-scatter.3
  77.1 21.8 all-gather.1
  114.7 20.0 reduce-scatter.7
where the time goes:
time: 142 us; the launch traced here: 141 us
  waiting for transfers between devices  84.4 us (59%)
  matrix products  26 us (18%)
  blocking collectives  15.9 us (11%)
  between operations  13.2 us (9%)
  local copies, waits for them, and re-layouts  1.53 us (1%)
    reduce_scatter x1, waiting for transfers between devices, local(): lax.psum_scatter(out_part.reshape(queries_here, tokens, rank), 'feat', sc...  22.2 us
    all_gather x1, waiting for transfers between devices, local(): lax.all_gather(query_grad, ('rows', 'sub'), axis=0, tiled=True)  21.7 us
    reduce_scatter x1, waiting for transfers between devices, local(): lax.psum_scatter(partial_scores, 'feat', scatter_dimension=0, tiled=True)  20.2 us
    reduce_scatter x1, waiting for transfers between devices, local(): lax.psum_scatter(in_part.reshape(queries_here, tokens, rank), 'feat', sca...  20.1 us
    all_to_all x1, blocking collectives, local(): lax.all_to_all(full_grad, 'feat', split_axis=1, concat_axis=0, tiled=True)  15.9 us
    dot_general x1, matrix products, score_block(): lax.dot_general(grads_block, store, (((1,), (1,)), ((), ())), precision=l...  15.5 us
    dot_general x1, matrix products, local(): jnp.dot(out_grads.reshape(queries_here * tokens, width_here), proj_out, p...  4.23 us
    dot_general x1, matrix products, local(): jnp.dot(acts.reshape(queries_here * tokens, width_here), proj_in, preferr...  4.23 us
  transfers between devices with their start and end apart: 4, of which 4 were waited for; matrix products, arithmetic and copies ran while one was open for 3% of the time, Pallas kernels for 0%

commit v1 on v0

v1 whole, which is shorter than its diff:
```python
import functools

import jax
import jax.numpy as jnp
from jax import lax
from jax.experimental import pallas as pl
from jax.experimental.pallas import tpu as pltpu
from jax.sharding import PartitionSpec as P

BF16, F32 = jnp.bfloat16, jnp.float32
NT = (((1,), (1,)), ((), ()))
NN = (((1,), (0,)), ((), ()))
VMEM_LIMIT = 48 * 1024 * 1024


def params(limit=VMEM_LIMIT):
    return pltpu.CompilerParams(vmem_limit_bytes=limit)


def whole(shape):
    return pl.BlockSpec(shape, lambda *_: (0,) * len(shape))


def in_vmem():
    return pl.BlockSpec(memory_space=pltpu.VMEM)


def gray(k):
    return k ^ (k >> 1)


def ungray(code):
    k = 0
    while code:
        k ^= code
        code >>= 1
    return k


def reversed_bits(value, bits):
    return sum(((value >> b) & 1) << (bits - 1 - b) for b in range(bits))


def exchange(x, axis, count, mask):
    return lax.ppermute(x, axis, [(k, k ^ mask) for k in range(count)])


def split(x):
    high = x.astype(BF16)
    return high, (x - high.astype(F32)).astype(BF16)


def in_kernel(tiles, x_ref, w_ref, keep_ref, send_ref):
    step = pl.program_id(0)
    rows = x_ref.shape[0]
    mine = gray(lax.axis_index("feat")) & 1
    half = tiles // 2
    product = jnp.dot(x_ref[...], w_ref[...], preferred_element_type=F32)
    place = pl.ds(pl.multiple_of(lax.rem(step, half) * rows, rows), rows)

    @pl.when(step // half == mine)
    def _():
        keep_ref[place, :] = product

    @pl.when(step // half != mine)
    def _():
        send_ref[place, :] = product


def project_in(x, w, tiles):
    rows, width = x.shape
    rank = w.shape[1]
    out = jax.ShapeDtypeStruct((rows // 2, rank), F32)
    return pl.pallas_call(
        functools.partial(in_kernel, tiles),
        grid=(tiles,),
        in_specs=[pl.BlockSpec((rows // tiles, width), lambda t: (t, 0)), whole(w.shape)],
        out_specs=[whole(out.shape)] * 2,
        out_shape=[out] * 2,
        compiler_params=params(),
        cost_estimate=pl.CostEstimate(
            flops=2 * rows * width * rank, bytes_accessed=2 * rows * width, transcendentals=0
        ),
        name="project_in",
    )(x, w)


def out_kernel(n, x_ref, w_ref, keep_ref, send_ref, turned):
    bits = n.bit_length() - 1
    here = lax.axis_index("feat")
    size = turned.shape[0] // n
    product = jnp.dot(x_ref[...], w_ref[...], preferred_element_type=F32)
    turned[...] = product.T
    for slot in range(n):
        chunk = here ^ ungray(reversed_bits(slot, bits))
        rows = turned[pl.ds(pl.multiple_of(chunk * size, size), size), :]
        ref = keep_ref if slot < n // 2 else send_ref
        ref[pl.ds(slot % (n // 2) * size, size), :] = rows


def project_out(x, w, tiles, n):
    rows, width = x.shape
    rank = w.shape[1]
    out = jax.ShapeDtypeStruct((rank // 2, rows), F32)
    columns = rows // tiles
    return pl.pallas_call(
        functools.partial(out_kernel, n),
        grid=(tiles,),
        in_specs=[pl.BlockSpec((columns, width), lambda t: (t, 0)), whole(w.shape)],
        out_specs=[pl.BlockSpec((rank // 2, columns), lambda t: (0, t))] * 2,
        out_shape=[out] * 2,
        scratch_shapes=[pltpu.VMEM((rank, columns), F32)],
        compiler_params=params(),
        cost_estimate=pl.CostEstimate(
            flops=2 * rows * width * rank, bytes_accessed=2 * rows * width, transcendentals=0
        ),
        name="project_out",
    )(x, w)


def outer_kernel(tokens, group, in_ref, out_ref, grad_ref):
    width = group * tokens
    features, rank = out_ref.shape[0], in_ref.shape[1]
    query = lax.broadcasted_iota(jnp.int32, (group, width), 0)
    token = lax.broadcasted_iota(jnp.int32, (group, width), 1)
    own = jnp.where(token // tokens == query, 1.0, 0.0).astype(F32)
    for g in range(in_ref.shape[0] // width):
        columns = out_ref[:, g * width : (g + 1) * width]
        spread = (columns[:, None, :] * own[None, :, :]).reshape(features * group, width)
        left, left_low = split(spread)
        right, right_low = split(in_ref[g * width : (g + 1) * width, :])
        total = jnp.dot(left, right, preferred_element_type=F32)
        total += jnp.dot(left_low, right, preferred_element_type=F32)
        total += jnp.dot(left, right_low, preferred_element_type=F32)
        grad_ref[:, g * group : (g + 1) * group, :] = total.reshape(features, group, rank)


def outer(in_rows, out_columns, tokens, group):
    rows, rank = in_rows.shape
    features = out_columns.shape[0]
    out = jax.ShapeDtypeStruct((features, rows // tokens, rank), F32)
    return pl.pallas_call(
        functools.partial(outer_kernel, tokens, group),
        in_specs=[in_vmem()] * 2,
        out_specs=in_vmem(),
        out_shape=out,
        compiler_params=params(),
        cost_estimate=pl.CostEstimate(
            flops=6 * rows * group * features * rank, bytes_accessed=8 * rows * rank, transcendentals=0
        ),
        name="outer",
    )(in_rows, out_columns)


def split_kernel(x_ref, high_ref, low_ref):
    high_ref[...], low_ref[...] = split(x_ref[...])


def split_store(store, tiles):
    rows, width = store.shape
    spec = pl.BlockSpec((rows // tiles, width), lambda t: (t, 0))
    out = jax.ShapeDtypeStruct(store.shape, BF16)
    return pl.pallas_call(
        split_kernel,
        grid=(tiles,),
        in_specs=[spec],
        out_specs=[spec] * 2,
        out_shape=[out] * 2,
        compiler_params=params(),
        cost_estimate=pl.CostEstimate(flops=rows * width, bytes_accessed=8 * rows * width, transcendentals=0),
        name="split_store",
    )(store)


def score_kernel(n, grads_ref, high_ref, low_ref, *rest):
    out_refs, (both,) = rest[:n], rest[n:]
    features, queries, rank = grads_ref.shape
    step = pl.program_id(0)
    here = lax.axis_index("feat")

    @pl.when(step == 0)
    def _():
        for i in range(features):
            high, low = split(grads_ref[i])
            both[:queries, i * rank : (i + 1) * rank] = high
            both[queries:, i * rank : (i + 1) * rank] = low

    total = lax.dot_general(high_ref[...], both[...], NT, preferred_element_type=F32)
    low = lax.dot_general(low_ref[...], both[:queries, :], NT, preferred_element_type=F32)
    total = total[:, :queries] + total[:, queries:] + low
    turned = total.T
    size = queries // n
    for slot in range(n):
        for k in range(n):
            @pl.when(here ^ slot == k)
            def _(slot=slot, k=k):
                out_refs[slot][...] = turned[k * size : (k + 1) * size, :]


def score(grads, high, low, n, tiles):
    features, queries, rank = grads.shape
    examples, width = high.shape
    spec = pl.BlockSpec((examples // tiles, width), lambda t: (t, 0))
    out = jax.ShapeDtypeStruct((queries // n, examples), F32)
    return pl.pallas_call(
        functools.partial(score_kernel, n),
        grid=(tiles,),
        in_specs=[whole(grads.shape), spec, spec],
        out_specs=[pl.BlockSpec((queries // n, examples // tiles), lambda t: (0, t))] * n,
        out_shape=[out] * n,
        scratch_shapes=[pltpu.VMEM((2 * queries, width), BF16)],
        compiler_params=params(),
        cost_estimate=pl.CostEstimate(
            flops=6 * queries * examples * width, bytes_accessed=4 * examples * width, transcendentals=0
        ),
        name="score",
    )(grads, high, low)


def tile_count(extent, unit, most):
    return next(t for t in range(most, 0, -1) if extent % (t * unit) == 0)


def local(sizes, acts, out_grads, proj_in, proj_out, store):
    n, rows, sub = sizes["feat"], sizes["rows"], sizes["sub"]
    bits = n.bit_length() - 1
    queries, tokens, width = acts.shape
    rank = proj_in.shape[1]
    here = gray(lax.axis_index("feat"))
    flat = queries * tokens

    in_keep, in_send = project_in(acts.reshape(flat, width), proj_in, 4)
    out_keep, out_send = project_out(out_grads.reshape(flat, width), proj_out, 4, n)

    in_sum = in_keep + exchange(in_send, "feat", n, 1)
    out_sum = out_keep + exchange(out_send, "feat", n, 1)
    for s in range(1, bits):
        mask = 2 ** (s + 1) - 1
        in_sum = in_sum + exchange(in_sum, "feat", n, mask)
        size = out_sum.shape[0] // 2
        out_sum = out_sum[:size] + exchange(out_sum[size:], "feat", n, mask)
    in_other = exchange(in_sum, "feat", n, 1)
    first = here & 1 == 0
    in_all = jnp.concatenate([jnp.where(first, in_sum, in_other), jnp.where(first, in_other, in_sum)])

    grads = outer(in_all, out_sum, tokens, 8)[None]
    for axis, count in (("rows", rows), ("sub", sub)):
        step = 1
        while step < count:
            other = exchange(grads, axis, count, step)
            low = lax.axis_index(axis) & step == 0
            grads = jnp.concatenate([jnp.where(low, grads, other), jnp.where(low, other, grads)])
            step *= 2
    features = grads.shape[1]
    grads = grads.reshape(sub, rows, features, queries, rank).transpose(2, 1, 0, 3, 4)
    grads = grads.reshape(features, rows * sub * queries, rank)
    high, low = split_store(store, tile_count(store.shape[0], 16, 5))
    parts = score(grads, high, low, n, tile_count(store.shape[0], 128, 5))
    total = parts[0]
    for mask in range(1, n):
        total = total + exchange(parts[mask], "feat", n, mask)
    return total


def solution(mesh):
    return jax.shard_map(
        functools.partial(local, dict(mesh.shape)),
        mesh=mesh,
        in_specs=(
            P(("groups", "rows", "sub"), None, "feat"),
            P(("groups", "rows", "sub"), None, "feat"),
            P("feat", None),
            P("feat", None),
            P(("groups", "rows", "sub"), "feat"),
        ),
        out_specs=P(("groups", "feat"), ("rows", "sub")),
        check_vma=False,
    )
```

time: 142 us -> 79.9 us (0.56)
  waiting for transfers between devices: 84.4 us -> 25.1 us
  matrix products: 26 us -> 0 us
  starting transfers between devices: 0.31 us -> 25.3 us
  Pallas kernels: 0 us -> 21.3 us
  blocking collectives: 15.9 us -> 0 us
  between operations: 13.2 us -> 0.11 us
  local copies, waits for them, and re-layouts: 1.53 us -> 5.21 us
  other arithmetic: 0 us -> 2.54 us
    reduce_scatter x3 -> x0, waiting for transfers between devices: 62.6 us -> none  [the longest x1 22.2 us: local(): lax.psum_scatter(out_part.reshape(queries_here, tokens, rank), 'feat', sc...]
    dot_general x4 -> x0, matrix products: 26 us -> none  [the longest x1 15.5 us: score_block(): lax.dot_general(grads_block, store, (((1,), (1,)), ((), ())), precision=l...]
    ppermute x0 -> x10, starting transfers between devices: none -> 25.3 us  [exchange(): return lax.ppermute(x, axis, [(k, k ^ mask) for k in range(count)])]
    ppermute x0 -> x10, waiting for transfers between devices: none -> 25.1 us  [exchange(): return lax.ppermute(x, axis, [(k, k ^ mask) for k in range(count)])]
    all_gather x1 -> x0, waiting for transfers between devices: 21.7 us -> none  [local(): lax.all_gather(query_grad, ('rows', 'sub'), axis=0, tiled=True)]
    pallas_call x0 -> x5, Pallas kernels: none -> 21.3 us  [the longest x1 8.79 us: score(): pl.pallas_call(functools.partial(score_kernel, n), grid=(tiles,), in_spec...]
    all_to_all x1 -> x0, blocking collectives: 15.9 us -> none  [local(): lax.all_to_all(full_grad, 'feat', split_axis=1, concat_axis=0, tiled=True)]
    unnamed x4 -> x10, local copies, waits for them, and re-layouts: 1.04 us -> 5.03 us
  transfers between devices with their start and end apart: 4 -> 10, of which waited for: 4 -> 7; matrix products, arithmetic and copies ran while one was open for 3% -> 0% of each run, Pallas kernels for 0% -> 13%
where the time goes in v1:
time: 79.9 us; the launch traced here: 79.5 us
  starting transfers between devices  25.3 us (32%)
  waiting for transfers between devices  25.1 us (31%)
  Pallas kernels  21.3 us (27%)
  local copies, waits for them, and re-layouts  5.21 us (7%)
  other arithmetic  2.54 us (3%)
    ppermute x10, starting transfers between devices, exchange(): return lax.ppermute(x, axis, [(k, k ^ mask) for k in range(count)])  25.3 us
    ppermute x10, waiting for transfers between devices, exchange(): return lax.ppermute(x, axis, [(k, k ^ mask) for k in range(count)])  25.1 us
    pallas_call x1, Pallas kernels, score(): pl.pallas_call(functools.partial(score_kernel, n), grid=(tiles,), in_spec...  8.79 us
    pallas_call x1, Pallas kernels, split_store(): pl.pallas_call(split_kernel, grid=(tiles,), in_specs=[spec], out_specs=[s...  8.07 us
    unnamed x10, local copies, waits for them, and re-layouts  5.03 us
    pallas_call x1, Pallas kernels, project_out(): pl.pallas_call(functools.partial(out_kernel, n), grid=(tiles,), in_specs=...  2.12 us
    pallas_call x1, Pallas kernels, project_in(): pl.pallas_call(functools.partial(in_kernel, tiles), grid=(tiles,), in_spe...  1.74 us
  transfers between devices with their start and end apart: 10, of which 7 were waited for; matrix products, arithmetic and copies ran while one was open for 0% of the time, Pallas kernels for 13%

profile of v1, /device:TPU:0, one launch (start us, length us, event | category | flops | bytes accessed | tf_op | source)
XLA Modules:
  0.0 79.5 jit_solution(17606836016775343456)
XLA Ops:
  0.0 0.0 copy-start.1
  0.0 2.2 %copy-done.1 = bf16[32,32,2048]{2,1,0:T(8,128)(2,1)S(1)} copy-done((bf16[32,32,2048]{2,1,0:T(8,128)(2,1)S(1)}, bf16[32,32,2048]{2,1,0:T(8,128)(2,1)}, u32[]{:S(2)}) %copy-start.1) | copy-done | bytes 4194328
  2.2 0.0 copy-start.3
  2.2 1.0 %copy-done.3 = bf16[2048,128]{1,0:T(8,128)(2,1)S(1)} copy-done((bf16[2048,128]{1,0:T(8,128)(2,1)S(1)}, bf16[2048,128]{1,0:T(8,128)(2,1)}, u32[]{:S(2)}) %copy-start.3) | copy-done | bytes 524312
  3.2 0.0 copy-start.2
  3.2 0.0 copy-start.4
  3.2 1.7 %project_in.1 = (f32[512,128]{1,0:T(8,128)S(1)}, f32[512,128]{1,0:T(8,128)S(1)}) custom-call(bf16[1024,2048]{1,0:T(8,128)(2,1)S(1)} %bitcast.10, bf16[2048,128]{1,0:T(8,128)(2,1)S(1)} %copy-done.3), custom_call_target="tpu_custom_call" | custom-call | flops 536870912 | bytes 4194304 | tf_op jit(solution)/shard_map/project_in/pallas_call | solution.py:74
  5.0 3.1 %collective-permute-start = (f32[512,128]{1,0:T(8,128)S(1)}, f32[512,128]{1,0:T(8,128)S(1)}, u32[]{:S(2)}, u32[]{:S(2)}) collective-permute-start(f32[512,128]{1,0:T(8,128)S(1)} %get-tuple-element.16), channel_id=1, source_target_pairs={{0,4},{4,0},{8,12},{12,8},{1,5},{5,1},{9,13},{13,9},{2,6},{6,2},{1... | collective-permute-start | bytes 786440 | tf_op jit(solution)/shard_map/ppermute | solution.py:45
  8.1 0.0 copy-done.2
  8.1 0.0 copy-done.4
  8.1 2.1 %project_out.1 = (f32[64,1024]{1,0:T(8,128)S(1)}, f32[64,1024]{1,0:T(8,128)S(1)}) custom-call(bf16[1024,2048]{1,0:T(8,128)(2,1)S(1)} %bitcast.11, bf16[2048,128]{1,0:T(8,128)(2,1)S(1)} %copy-done.4), custom_call_target="tpu_custom_call" | custom-call | flops 536870912 | bytes 4194304 | tf_op jit(solution)/shard_map/project_out/pallas_call | solution.py:106
  10.2 0.5 collective-permute-start.3
  10.7 4.5 %collective-permute-done = f32[512,128]{1,0:T(8,128)S(1)} collective-permute-done((f32[512,128]{1,0:T(8,128)S(1)}, f32[512,128]{1,0:T(8,128)S(1)}, u32[]{:S(2)}, u32[]{:S(2)}) %collective-permute-start) | collective-permute-done | bytes 262176 | tf_op jit(solution)/shard_map/ppermute | solution.py:45
  15.2 4.1 %collective-permute-start.1 = (f32[512,128]{1,0:T(8,128)S(1)}, f32[512,128]{1,0:T(8,128)S(1)}, u32[]{:S(2)}, u32[]{:S(2)}) collective-permute-start(f32[512,128]{1,0:T(8,128)S(1)} %add.21), channel_id=1, source_target_pairs={{0,12},{4,8},{8,4},{12,0},{1,13},{5,9},{9,5},{13,1},{2,14},{6,10},... | collective-permute-start | bytes 786440 | tf_op jit(solution)/shard_map/ppermute | solution.py:45
  19.4 1.0 %collective-permute-done.3 = f32[64,1024]{1,0:T(8,128)S(1)} collective-permute-done((f32[64,1024]{1,0:T(8,128)S(1)}, f32[64,1024]{1,0:T(8,128)S(1)}, u32[]{:S(2)}, u32[]{:S(2)}) %collective-permute-start.3) | collective-permute-done | bytes 262176 | tf_op jit(solution)/shard_map/ppermute | solution.py:45
  20.5 10.4 %collective-permute-start.4 = (f32[32,1024]{1,0:T(8,128)S(1)}, f32[32,1024]{1,0:T(8,128)S(1)}, u32[]{:S(2)}, u32[]{:S(2)}) collective-permute-start(f32[32,1024]{1,0:T(8,128)S(1)} %slice.9), channel_id=1, source_target_pairs={{0,12},{4,8},{8,4},{12,0},{1,13},{5,9},{9,5},{13,1},{2,14},{6,10},... | collective-permute-start | bytes 393224 | tf_op jit(solution)/shard_map/ppermute | solution.py:45
  30.9 0.0 collective-permute-done.1
  30.9 1.1 %collective-permute-start.2 = (f32[512,128]{1,0:T(8,128)S(1)}, f32[512,128]{1,0:T(8,128)S(1)}, u32[]{:S(2)}, u32[]{:S(2)}) collective-permute-start(f32[512,128]{1,0:T(8,128)S(1)} %add.22), channel_id=1, source_target_pairs={{0,4},{4,0},{8,12},{12,8},{1,5},{5,1},{9,13},{13,9},{2,6},{6,2},{1... | collective-permute-start | bytes 786440 | tf_op jit(solution)/shard_map/ppermute | solution.py:45
  32.0 1.9 %collective-permute-done.4 = f32[32,1024]{1,0:T(8,128)S(1)} collective-permute-done((f32[32,1024]{1,0:T(8,128)S(1)}, f32[32,1024]{1,0:T(8,128)S(1)}, u32[]{:S(2)}, u32[]{:S(2)}) %collective-permute-start.4) | collective-permute-done | bytes 131104 | tf_op jit(solution)/shard_map/ppermute | solution.py:45
  34.0 3.4 %collective-permute-done.2 = f32[512,128]{1,0:T(8,128)S(1)} collective-permute-done((f32[512,128]{1,0:T(8,128)S(1)}, f32[512,128]{1,0:T(8,128)S(1)}, u32[]{:S(2)}, u32[]{:S(2)}) %collective-permute-start.2) | collective-permute-done | bytes 262176 | tf_op jit(solution)/shard_map/ppermute | solution.py:45
  37.5 0.6 outer.1
  38.0 1.5 %collective-permute-start.5 = (f32[1,32,32,128]{3,2,1,0:T(8,128)S(1)}, f32[1,32,32,128]{3,2,1,0:T(8,128)S(1)}, u32[]{:S(2)}, u32[]{:S(2)}) collective-permute-start(f32[1,32,32,128]{3,2,1,0:T(8,128)S(1)} %bitcast.12), channel_id=1, source_target_pairs={{0,2},{2,0},{1,3},{3,1},{4,6},{6,4},{5,7},{7,5},{8,10},{10,8},{9,1... | collective-permute-start | bytes 1572872 | tf_op jit(solution)/shard_map/ppermute | solution.py:45
  39.6 7.7 %collective-permute-done.5 = f32[1,32,32,128]{3,2,1,0:T(8,128)S(1)} collective-permute-done((f32[1,32,32,128]{3,2,1,0:T(8,128)S(1)}, f32[1,32,32,128]{3,2,1,0:T(8,128)S(1)}, u32[]{:S(2)}, u32[]{:S(2)}) %collective-permute-start.5) | collective-permute-done | bytes 524320 | tf_op jit(solution)/shard_map/ppermute | solution.py:45
  47.3 0.1 broadcast_select_fusion.3
  47.4 1.0 %pad_maximum_fusion.1 = f32[2,32,32,128]{3,2,1,0:T(8,128)} fusion(f32[1,32,32,128]{3,2,1,0:T(8,128)S(1)} %get-tuple-element.28, f32[1,32,32,128]{3,2,1,0:T(8,128)S(1)} %get-tuple-element.27), kind=kLoop, calls=%fused_computation.1 | loop fusion | flops 262144 | bytes 2097152 | tf_op jit(solution)/shard_map/concatenate | solution.py:252
  48.4 0.0 collective-permute-start.6
  48.5 8.1 %split_store.1 = (bf16[640,4096]{1,0:T(8,128)(2,1)S(1)}, bf16[640,4096]{1,0:T(8,128)(2,1)}) custom-call(f32[640,4096]{1,0:T(8,128)} %x_ref.1), custom_call_target="tpu_custom_call" | custom-call | flops 2621440 | bytes 20971520 | tf_op jit(solution)/shard_map/split_store/pallas_call | solution.py:163
  56.5 0.0 copy-start
  56.5 0.0 collective-permute-done.6
  56.5 0.4 broadcast_select_fusion.1
  56.9 0.2 pad_maximum_fusion
  57.1 1.8 %copy-done = bf16[640,4096]{1,0:T(8,128)(2,1)} copy-done((bf16[640,4096]{1,0:T(8,128)(2,1)}, bf16[640,4096]{1,0:T(8,128)(2,1)S(1)}, u32[]{:S(2)}) %copy-start) | copy-done | bytes 5242904
  58.9 0.2 copy.6
  59.1 8.8 %score.1 = (f32[32,640]{1,0:T(8,128)S(1)}, f32[32,640]{1,0:T(8,128)S(1)}, f32[32,640]{1,0:T(8,128)S(1)}, f32[32,640]{1,0:T(8,128)S(1)}) custom-call(f32[32,128,128]{2,1,0:T(8,128)S(1)} %bitcast.9, bf16[640,4096]{1,0:T(8,128)(2,1)} %copy-done, bf16[640,4096]{1,0:T(8,128)(2,1)} %get-tuple-element.20.low_ref), custom_call_target="tpu_custom_call" | custom-call | flops 2013265920 | bytes 10485760 | tf_op jit(solution)/shard_map/score/pallas_call | solution.py:205
  67.9 1.3 %collective-permute-start.7 = (f32[32,640]{1,0:T(8,128)S(1)}, f32[32,640]{1,0:T(8,128)S(1)}, u32[]{:S(2)}, u32[]{:S(2)}) collective-permute-start(f32[32,640]{1,0:T(8,128)S(1)} %get-tuple-element.22), channel_id=1, source_target_pairs={{0,4},{4,0},{8,12},{12,8},{1,5},{5,1},{9,13},{13,9},{2,6},{6,2},{1... | collective-permute-start | bytes 245768 | tf_op jit(solution)/shard_map/ppermute | solution.py:45
  69.2 2.1 %collective-permute-start.8 = (f32[32,640]{1,0:T(8,128)S(1)}, f32[32,640]{1,0:T(8,128)S(1)}, u32[]{:S(2)}, u32[]{:S(2)}) collective-permute-start(f32[32,640]{1,0:T(8,128)S(1)} %get-tuple-element.23), channel_id=1, source_target_pairs={{0,8},{4,12},{8,0},{12,4},{1,9},{5,13},{9,1},{13,5},{2,10},{6,14},... | collective-permute-start | bytes 245768 | tf_op jit(solution)/shard_map/ppermute | solution.py:45
  71.3 1.0 %collective-permute-start.9 = (f32[32,640]{1,0:T(8,128)S(1)}, f32[32,640]{1,0:T(8,128)S(1)}, u32[]{:S(2)}, u32[]{:S(2)}) collective-permute-start(f32[32,640]{1,0:T(8,128)S(1)} %get-tuple-element.24), channel_id=1, source_target_pairs={{0,12},{4,8},{8,4},{12,0},{1,13},{5,9},{9,5},{13,1},{2,14},{6,10},... | collective-permute-start | bytes 245768 | tf_op jit(solution)/shard_map/ppermute | solution.py:45
  72.3 0.5 collective-permute-done.7
  72.8 6.1 %collective-permute-done.8 = f32[32,640]{1,0:T(8,128)S(1)} collective-permute-done((f32[32,640]{1,0:T(8,128)S(1)}, f32[32,640]{1,0:T(8,128)S(1)}, u32[]{:S(2)}, u32[]{:S(2)}) %collective-permute-start.8) | collective-permute-done | bytes 81952 | tf_op jit(solution)/shard_map/ppermute | solution.py:45
  78.9 0.0 collective-permute-done.9
  78.9 0.7 add_add_fusion
  (7 shorter events, 0.2 us)
Async XLA Ops:
  0.0 2.2 %copy-start.1 = (bf16[32,32,2048]{2,1,0:T(8,128)(2,1)S(1)}, bf16[32,32,2048]{2,1,0:T(8,128)(2,1)}, u32[]{:S(2)}) copy-start(bf16[32,32,2048]{2,1,0:T(8,128)(2,1)} %param.5) | copy-start | bytes 12582916
  2.2 1.0 %copy-start.3 = (bf16[2048,128]{1,0:T(8,128)(2,1)S(1)}, bf16[2048,128]{1,0:T(8,128)(2,1)}, u32[]{:S(2)}) copy-start(bf16[2048,128]{1,0:T(8,128)(2,1)} %w_ref.2) | copy-start | bytes 1572868
  3.2 4.8 %copy-start.2 = (bf16[32,32,2048]{2,1,0:T(8,128)(2,1)S(1)}, bf16[32,32,2048]{2,1,0:T(8,128)(2,1)}, u32[]{:S(2)}) copy-start(bf16[32,32,2048]{2,1,0:T(8,128)(2,1)} %param.6) | copy-start | bytes 12582916
  3.2 4.8 %copy-start.4 = (bf16[2048,128]{1,0:T(8,128)(2,1)S(1)}, bf16[2048,128]{1,0:T(8,128)(2,1)}, u32[]{:S(2)}) copy-start(bf16[2048,128]{1,0:T(8,128)(2,1)} %w_ref.3) | copy-start | bytes 1572868
  5.0 10.2 %collective-permute-start = (f32[512,128]{1,0:T(8,128)S(1)}, f32[512,128]{1,0:T(8,128)S(1)}, u32[]{:S(2)}, u32[]{:S(2)}) collective-permute-start(f32[512,128]{1,0:T(8,128)S(1)} %get-tuple-element.16), channel_id=1, source_target_pairs={{0,4},{4,0},{8,12},{12,8},{1,5},{5,1},{9,13},{13,9},{2,6},{6,2},{1... | collective-permute-start | bytes 786440 | tf_op jit(solution)/shard_map/ppermute | solution.py:45
  10.2 10.2 %collective-permute-start.3 = (f32[64,1024]{1,0:T(8,128)S(1)}, f32[64,1024]{1,0:T(8,128)S(1)}, u32[]{:S(2)}, u32[]{:S(2)}) collective-permute-start(f32[64,1024]{1,0:T(8,128)S(1)} %get-tuple-element.18), channel_id=1, source_target_pairs={{0,4},{4,0},{8,12},{12,8},{1,5},{5,1},{9,13},{13,9},{2,6},{6,2},{1... | collective-permute-start | bytes 786440 | tf_op jit(solution)/shard_map/ppermute | solution.py:45
  15.2 15.7 %collective-permute-start.1 = (f32[512,128]{1,0:T(8,128)S(1)}, f32[512,128]{1,0:T(8,128)S(1)}, u32[]{:S(2)}, u32[]{:S(2)}) collective-permute-start(f32[512,128]{1,0:T(8,128)S(1)} %add.21), channel_id=1, source_target_pairs={{0,12},{4,8},{8,4},{12,0},{1,13},{5,9},{9,5},{13,1},{2,14},{6,10},... | collective-permute-start | bytes 786440 | tf_op jit(solution)/shard_map/ppermute | solution.py:45
  20.5 13.5 %collective-permute-start.4 = (f32[32,1024]{1,0:T(8,128)S(1)}, f32[32,1024]{1,0:T(8,128)S(1)}, u32[]{:S(2)}, u32[]{:S(2)}) collective-permute-start(f32[32,1024]{1,0:T(8,128)S(1)} %slice.9), channel_id=1, source_target_pairs={{0,12},{4,8},{8,4},{12,0},{1,13},{5,9},{9,5},{13,1},{2,14},{6,10},... | collective-permute-start | bytes 393224 | tf_op jit(solution)/shard_map/ppermute | solution.py:45
  30.9 6.4 %collective-permute-start.2 = (f32[512,128]{1,0:T(8,128)S(1)}, f32[512,128]{1,0:T(8,128)S(1)}, u32[]{:S(2)}, u32[]{:S(2)}) collective-permute-start(f32[512,128]{1,0:T(8,128)S(1)} %add.22), channel_id=1, source_target_pairs={{0,4},{4,0},{8,12},{12,8},{1,5},{5,1},{9,13},{13,9},{2,6},{6,2},{1... | collective-permute-start | bytes 786440 | tf_op jit(solution)/shard_map/ppermute | solution.py:45
  38.0 9.2 %collective-permute-start.5 = (f32[1,32,32,128]{3,2,1,0:T(8,128)S(1)}, f32[1,32,32,128]{3,2,1,0:T(8,128)S(1)}, u32[]{:S(2)}, u32[]{:S(2)}) collective-permute-start(f32[1,32,32,128]{3,2,1,0:T(8,128)S(1)} %bitcast.12), channel_id=1, source_target_pairs={{0,2},{2,0},{1,3},{3,1},{4,6},{6,4},{5,7},{7,5},{8,10},{10,8},{9,1... | collective-permute-start | bytes 1572872 | tf_op jit(solution)/shard_map/ppermute | solution.py:45
  48.4 8.1 %collective-permute-start.6 = (f32[2,32,32,128]{3,2,1,0:T(8,128)}, f32[2,32,32,128]{3,2,1,0:T(8,128)S(1)}, u32[]{:S(2)}, u32[]{:S(2)}) collective-permute-start(f32[2,32,32,128]{3,2,1,0:T(8,128)} %pad_maximum_fusion.1), channel_id=1, source_target_pairs={{0,1},{1,0},{2,3},{3,2},{4,5},{5,4},{6,7},{7,6},{8,9},{9,8},{10,11... | collective-permute-start | bytes 3145736 | tf_op jit(solution)/shard_map/ppermute | solution.py:45
  56.5 2.4 %copy-start = (bf16[640,4096]{1,0:T(8,128)(2,1)}, bf16[640,4096]{1,0:T(8,128)(2,1)S(1)}, u32[]{:S(2)}) copy-start(bf16[640,4096]{1,0:T(8,128)(2,1)S(1)} %get-tuple-element.19.high_ref) | copy-start | bytes 15728644
  67.9 4.9 %collective-permute-start.7 = (f32[32,640]{1,0:T(8,128)S(1)}, f32[32,640]{1,0:T(8,128)S(1)}, u32[]{:S(2)}, u32[]{:S(2)}) collective-permute-start(f32[32,640]{1,0:T(8,128)S(1)} %get-tuple-element.22), channel_id=1, source_target_pairs={{0,4},{4,0},{8,12},{12,8},{1,5},{5,1},{9,13},{13,9},{2,6},{6,2},{1... | collective-permute-start | bytes 245768 | tf_op jit(solution)/shard_map/ppermute | solution.py:45
  69.2 9.7 %collective-permute-start.8 = (f32[32,640]{1,0:T(8,128)S(1)}, f32[32,640]{1,0:T(8,128)S(1)}, u32[]{:S(2)}, u32[]{:S(2)}) collective-permute-start(f32[32,640]{1,0:T(8,128)S(1)} %get-tuple-element.23), channel_id=1, source_target_pairs={{0,8},{4,12},{8,0},{12,4},{1,9},{5,13},{9,1},{13,5},{2,10},{6,14},... | collective-permute-start | bytes 245768 | tf_op jit(solution)/shard_map/ppermute | solution.py:45
  71.3 7.6 %collective-permute-start.9 = (f32[32,640]{1,0:T(8,128)S(1)}, f32[32,640]{1,0:T(8,128)S(1)}, u32[]{:S(2)}, u32[]{:S(2)}) collective-permute-start(f32[32,640]{1,0:T(8,128)S(1)} %get-tuple-element.24), channel_id=1, source_target_pairs={{0,12},{4,8},{8,4},{12,0},{1,13},{5,9},{9,5},{13,1},{2,14},{6,10},... | collective-permute-start | bytes 245768 | tf_op jit(solution)/shard_map/ppermute | solution.py:45

commit v2 on v0

v2 whole, which is shorter than its diff:
```python
import functools

import jax
import jax.numpy as jnp
from jax import lax
from jax.experimental import pallas as pl
from jax.experimental.pallas import tpu as pltpu
from jax.sharding import PartitionSpec as P

BF16, F32 = jnp.bfloat16, jnp.float32
NT = (((1,), (1,)), ((), ()))
NN = (((1,), (0,)), ((), ()))
MIB = 1024 * 1024


def params(limit):
    return pltpu.CompilerParams(vmem_limit_bytes=limit * MIB)


def in_vmem():
    return pl.BlockSpec(memory_space=pltpu.VMEM)


def anywhere():
    return pl.BlockSpec(memory_space=pl.ANY)


def in_hbm():
    return pl.BlockSpec(memory_space=pltpu.HBM)


def gray(k):
    return k ^ (k >> 1)


def ungray(code):
    k = 0
    while code:
        k ^= code
        code >>= 1
    return k


def reversed_bits(value, bits):
    return sum(((value >> b) & 1) << (bits - 1 - b) for b in range(bits))


def exchange(x, axis, count, mask):
    return lax.ppermute(x, axis, [(k, k ^ mask) for k in range(count)])


def split(x):
    high = x.astype(BF16)
    return high, (x - high.astype(F32)).astype(BF16)


def in_kernel(tiles, x_ref, w_ref, out_ref, x_buf, w_buf, sems):
    rows = x_buf.shape[0]
    size = rows // tiles
    half = (gray(lax.axis_index("feat")) & 1) ^ 1
    w_copy = pltpu.make_async_copy(w_ref, w_buf, sems.at[tiles])
    w_copy.start()
    copies = []
    for t in range(tiles):
        place = pl.multiple_of(half * rows + t * size, size)
        copies.append(
            pltpu.make_async_copy(x_ref.at[pl.ds(place, size)], x_buf.at[pl.ds(t * size, size)], sems.at[t])
        )
        copies[t].start()
    w_copy.wait()
    for t in range(tiles):
        copies[t].wait()
        tile = slice(t * size, (t + 1) * size)
        out_ref[tile, :] = jnp.dot(x_buf[tile, :], w_buf[...], preferred_element_type=F32)


def project_sent(x, w, tiles):
    rows, width = x.shape
    rank = w.shape[1]
    return pl.pallas_call(
        functools.partial(in_kernel, tiles),
        in_specs=[in_hbm()] * 2,
        out_specs=in_vmem(),
        out_shape=jax.ShapeDtypeStruct((rows // 2, rank), F32),
        scratch_shapes=[
            pltpu.VMEM((rows // 2, width), BF16),
            pltpu.VMEM(w.shape, BF16),
            pltpu.SemaphoreType.DMA((tiles + 1,)),
        ],
        compiler_params=params(60),
        cost_estimate=pl.CostEstimate(flops=rows * width * rank, bytes_accessed=0, transcendentals=0),
        name="project_sent",
    )(x, w)


def rest_kernel(n, tiles, out_x_ref, out_w_ref, in_x_ref, in_w_ref, after_ref, keep_ref, send_ref, in_ref, *scratch):
    del after_ref
    out_buf, out_w, in_buf, in_w, turned, sems = scratch
    bits = n.bit_length() - 1
    here = lax.axis_index("feat")
    half = gray(here) & 1
    rows = in_buf.shape[0]
    size = rows // tiles
    copies = [(out_w_ref, out_w)]
    for t in range(2 * tiles):
        place = pl.ds(t * size, size)
        copies.append((out_x_ref.at[place], out_buf.at[place]))
    copies.append((in_w_ref, in_w))
    for t in range(tiles):
        place = pl.multiple_of(half * rows + t * size, size)
        copies.append((in_x_ref.at[pl.ds(place, size)], in_buf.at[pl.ds(t * size, size)]))
    copies = [pltpu.make_async_copy(*pair, sems.at[k]) for k, pair in enumerate(copies)]
    for copy in copies:
        copy.start()
    copies[0].wait()
    for t in range(2 * tiles):
        copies[1 + t].wait()
        tile = slice(t * size, (t + 1) * size)
        turned[:, tile] = jnp.dot(out_buf[tile, :], out_w[...], preferred_element_type=F32).T
    features = turned.shape[0] // n
    for slot in range(n):
        chunk = here ^ ungray(reversed_bits(slot, bits))
        ref = keep_ref if slot < n // 2 else send_ref
        place = slot % (n // 2) * features
        ref[place : place + features, :] = turned[pl.ds(pl.multiple_of(chunk * features, features), features), :]
    copies[1 + 2 * tiles].wait()
    for t in range(tiles):
        copies[2 + 2 * tiles + t].wait()
        tile = slice(t * size, (t + 1) * size)
        in_ref[tile, :] = jnp.dot(in_buf[tile, :], in_w[...], preferred_element_type=F32)


def project_rest(out_x, out_w, in_x, in_w, after, tiles, n):
    rows, width = out_x.shape
    rank = out_w.shape[1]
    out = jax.ShapeDtypeStruct((rank // 2, rows), F32)
    return pl.pallas_call(
        functools.partial(rest_kernel, n, tiles),
        in_specs=[in_hbm()] * 4 + [anywhere()],
        out_specs=[in_vmem()] * 3,
        out_shape=[out, out, jax.ShapeDtypeStruct((rows // 2, rank), F32)],
        scratch_shapes=[
            pltpu.VMEM((rows, width), BF16),
            pltpu.VMEM(out_w.shape, BF16),
            pltpu.VMEM((rows // 2, width), BF16),
            pltpu.VMEM(in_w.shape, BF16),
            pltpu.VMEM((rank, rows), F32),
            pltpu.SemaphoreType.DMA((3 * tiles + 2,)),
        ],
        compiler_params=params(57),
        cost_estimate=pl.CostEstimate(
            flops=3 * rows * width * rank, bytes_accessed=0, transcendentals=0
        ),
        name="project_rest",
    )(out_x, out_w, in_x, in_w, after)


def add_kernel(parts, a_ref, b_ref, *rest):
    out_refs = rest[len(rest) - parts :]
    size = a_ref.shape[0] // parts
    for k, out_ref in enumerate(out_refs):
        rows = slice(k * size, (k + 1) * size)
        out_ref[...] = a_ref[rows, :] + b_ref[rows, :]


def add(a, b, parts=1, after=(), weight=1):
    out = jax.ShapeDtypeStruct((a.shape[0] // parts, a.shape[1]), F32)
    return pl.pallas_call(
        functools.partial(add_kernel, parts),
        in_specs=[in_vmem()] * 2 + [anywhere()] * len(after),
        out_specs=[in_vmem()] * parts,
        out_shape=[out] * parts,
        compiler_params=params(8),
        cost_estimate=pl.CostEstimate(flops=weight * a.size, bytes_accessed=12 * a.size, transcendentals=0),
        name="add",
    )(a, b, *after)


def outer_kernel(tokens, group, second, in_ref, out_ref, *rest):
    grad_ref = rest[-1]
    width = group * tokens
    rows, rank = in_ref.shape
    features = out_ref.shape[0]
    half = (gray(lax.axis_index("feat")) & 1) ^ second
    query = lax.broadcasted_iota(jnp.int32, (group, width), 0)
    token = lax.broadcasted_iota(jnp.int32, (group, width), 1)
    own = jnp.where(token // tokens == query, 1.0, 0.0).astype(F32)
    for g in range(rows // width):
        columns = out_ref[:, pl.ds(pl.multiple_of(half * rows + g * width, width), width)]
        spread = (columns[:, None, :] * own[None, :, :]).reshape(features * group, width)
        left, left_low = split(spread)
        right, right_low = split(in_ref[g * width : (g + 1) * width, :])
        total = jnp.dot(left, right, preferred_element_type=F32)
        total += jnp.dot(left_low, right, preferred_element_type=F32)
        total += jnp.dot(left, right_low, preferred_element_type=F32)
        grad_ref[:, g * group : (g + 1) * group, :] = total.reshape(features, group, rank)


def outer(in_rows, out_columns, tokens, group, second, after=()):
    rows, rank = in_rows.shape
    features = out_columns.shape[0]
    out = jax.ShapeDtypeStruct((features, rows // tokens, rank), F32)
    return pl.pallas_call(
        functools.partial(outer_kernel, tokens, group, second),
        in_specs=[in_vmem()] * 2 + [anywhere()] * len(after),
        out_specs=in_vmem(),
        out_shape=out,
        compiler_params=params(16),
        cost_estimate=pl.CostEstimate(
            flops=6 * rows * group * features * rank, bytes_accessed=8 * rows * rank, transcendentals=0
        ),
        name="outer",
    )(in_rows, out_columns, *after)


def split_kernel(first, tiles, x_ref, after_ref, high_ref, low_ref, x_buf, sems):
    del after_ref
    size = x_buf.shape[0] // tiles
    copies = []
    for t in range(tiles):
        copies.append(
            pltpu.make_async_copy(x_ref.at[pl.ds(first + t * size, size)], x_buf.at[pl.ds(t * size, size)], sems.at[t])
        )
        copies[t].start()
    for t in range(tiles):
        copies[t].wait()
        rows = slice(t * size, (t + 1) * size)
        high_ref[rows, :], low_ref[rows, :] = split(x_buf[rows, :])


def split_store(store, after, start, rows):
    width = store.shape[1]
    tiles = tile_count(rows, 16, 5)
    out = jax.ShapeDtypeStruct((rows, width), BF16)
    return pl.pallas_call(
        functools.partial(split_kernel, start, tiles),
        in_specs=[in_hbm(), anywhere()],
        out_specs=[in_vmem()] * 2,
        out_shape=[out] * 2,
        scratch_shapes=[pltpu.VMEM((rows, width), F32), pltpu.SemaphoreType.DMA((tiles,))],
        compiler_params=params(24),
        cost_estimate=pl.CostEstimate(flops=1000 * rows * width, bytes_accessed=0, transcendentals=0),
        name="split_store",
    )(store, after)


def score_kernel(n, sub, count, *refs):
    store_refs, out_refs, (both, result) = refs[count : -n - 2], refs[-n - 2 : -2], refs[-2:]
    grad_refs = refs[:count]
    features, queries, rank = grad_refs[0].shape
    total = count * queries
    here = lax.axis_index("feat")
    half = gray(here) & 1
    for d in range(count // 2):
        for second in range(2):
            ref = grad_refs[2 * d + second]
            place = 2 * d * queries + (half ^ second) * queries
            place = pl.multiple_of(place, queries)
            for i in range(features):
                high, low = split(ref[i])
                both[pl.ds(place, queries), i * rank : (i + 1) * rank] = high
                both[pl.ds(total + place, queries), i * rank : (i + 1) * rank] = low
    first = 0
    for high_ref, low_ref in zip(store_refs[::2], store_refs[1::2]):
        sums = lax.dot_general(both[...], high_ref[...], NT, preferred_element_type=F32)
        lows = lax.dot_general(both[:total, :], low_ref[...], NT, preferred_element_type=F32)
        result[:, first : first + high_ref.shape[0]] = sums[:total] + sums[total:] + lows
        first += high_ref.shape[0]
    own = here ^ (lax.axis_index("rows") * sub + lax.axis_index("sub"))
    size = 2 * queries
    for slot in range(n):
        out_refs[slot][...] = result[pl.ds(pl.multiple_of((own ^ slot) * size, size), size), :]


def score(grads, stored, n, sub):
    features, queries, rank = grads[0].shape
    examples, width = sum(part.shape[0] for part in stored[::2]), stored[0].shape[1]
    total = len(grads) * queries
    out = jax.ShapeDtypeStruct((total // n, examples), F32)
    return pl.pallas_call(
        functools.partial(score_kernel, n, sub, len(grads)),
        in_specs=[in_vmem()] * (len(grads) + len(stored)),
        out_specs=[in_vmem()] * n,
        out_shape=[out] * n,
        scratch_shapes=[pltpu.VMEM((2 * total, width), BF16), pltpu.VMEM((total, examples), F32)],
        compiler_params=params(24),
        cost_estimate=pl.CostEstimate(
            flops=6 * total * examples * width, bytes_accessed=4 * examples * width, transcendentals=0
        ),
        name="score",
    )(*grads, *stored)


def tile_count(extent, unit, most):
    return next(t for t in range(most, 0, -1) if extent % (t * unit) == 0)


def gathered(own, sizes):
    arrays = [own]
    for axis in ("rows", "sub"):
        mask = 1
        while mask < sizes[axis]:
            arrays = arrays + [exchange(a, axis, sizes[axis], mask) for a in arrays]
            mask *= 2
    return arrays


def neighbours(sizes):
    order = [0]
    for axis, unit in (("rows", sizes["sub"]), ("sub", 1)):
        mask = 1
        while mask < sizes[axis]:
            order = order + [d ^ (mask * unit) for d in order]
            mask *= 2
    return order


def local(sizes, acts, out_grads, proj_in, proj_out, store):
    n, rows, sub = sizes["feat"], sizes["rows"], sizes["sub"]
    bits = n.bit_length() - 1
    queries, tokens, width = acts.shape
    flat = queries * tokens
    acts = acts.reshape(flat, width)
    out_grads = out_grads.reshape(flat, width)

    in_send = project_sent(acts, proj_in, 2)
    in_recv = exchange(in_send, "feat", n, 1)
    out_keep, out_send, in_keep = project_rest(out_grads, proj_out, acts, proj_in, in_send, 2, n)
    (in_sum,) = add(in_keep, in_recv)
    examples = store.shape[0]
    early = examples // 512 * 256
    stored = split_store(store, in_sum, 0, early) if early else []
    for s in range(1, bits):
        mask = 2 ** (s + 1) - 1
        in_recv = exchange(in_sum, "feat", n, mask)
        out_keep, out_send = add(out_keep, exchange(out_send, "feat", n, mask // 2), 2, stored[:1])
        out_recv = exchange(out_send, "feat", n, mask)
        (in_sum,) = add(in_sum, in_recv)
    stored = stored + split_store(store, in_sum, early, examples - early)
    (out_sum,) = add(out_keep, out_recv, 1, stored[-1:], weight=10**6)
    in_other = exchange(in_sum, "feat", n, 1)

    first = gathered(outer(in_sum, out_sum, tokens, 8, 0), sizes)
    second = gathered(outer(in_other, out_sum, tokens, 8, 1), sizes)
    order = neighbours(sizes)
    grads = [None] * (2 * len(order))
    for place, d in enumerate(order):
        grads[2 * d], grads[2 * d + 1] = first[place], second[place]
    parts = score(grads, stored, n, sub)
    moved = [exchange(parts[mask], "feat", n, mask) for mask in reversed(range(1, n))]
    total = parts[0]
    for part in reversed(moved):
        total = total + part
    return total


def solution(mesh):
    return jax.shard_map(
        functools.partial(local, dict(mesh.shape)),
        mesh=mesh,
        in_specs=(
            P(("groups", "rows", "sub"), None, "feat"),
            P(("groups", "rows", "sub"), None, "feat"),
            P("feat", None),
            P("feat", None),
            P(("groups", "rows", "sub"), "feat"),
        ),
        out_specs=P(("groups", "feat"), ("rows", "sub")),
        check_vma=False,
    )
```

time: 142 us -> 61.4 us (0.43)
  waiting for transfers between devices: 84.4 us -> 16.2 us
  matrix products: 26 us -> 0 us
  starting transfers between devices: 0.31 us -> 24.5 us
  blocking collectives: 15.9 us -> 0 us
  Pallas kernels: 0 us -> 14.7 us
  between operations: 13.2 us -> 0.1 us
  local copies, waits for them, and re-layouts: 1.53 us -> 4.94 us
    reduce_scatter x3 -> x0, waiting for transfers between devices: 62.6 us -> none  [the longest x1 22.2 us: local(): lax.psum_scatter(out_part.reshape(queries_here, tokens, rank), 'feat', sc...]
    dot_general x4 -> x0, matrix products: 26 us -> none  [the longest x1 15.5 us: score_block(): lax.dot_general(grads_block, store, (((1,), (1,)), ((), ())), precision=l...]
    ppermute x0 -> x14, starting transfers between devices: none -> 24.5 us  [exchange(): return lax.ppermute(x, axis, [(k, k ^ mask) for k in range(count)])]
    all_gather x1 -> x0, waiting for transfers between devices: 21.7 us -> none  [local(): lax.all_gather(query_grad, ('rows', 'sub'), axis=0, tiled=True)]
    ppermute x0 -> x14, waiting for transfers between devices: none -> 16.2 us  [exchange(): return lax.ppermute(x, axis, [(k, k ^ mask) for k in range(count)])]
    all_to_all x1 -> x0, blocking collectives: 15.9 us -> none  [local(): lax.all_to_all(full_grad, 'feat', split_axis=1, concat_axis=0, tiled=True)]
    pallas_call x0 -> x11, Pallas kernels: none -> 14.7 us  [the longest x1 5 us: project_rest(): pl.pallas_call(functools.partial(rest_kernel, n, tiles), in_specs=[in_hbm...]
    unnamed x4 -> x6, local copies, waits for them, and re-layouts: 1.04 us -> 4.94 us
  transfers between devices with their start and end apart: 4 -> 14, of which waited for: 4 -> 8; matrix products, arithmetic and copies ran while one was open for 3% -> 0% of each run, Pallas kernels for 0% -> 13%
where the time goes in v2:
time: 61.4 us; the launch traced here: 61.1 us
  starting transfers between devices  24.5 us (40%)
  waiting for transfers between devices  16.2 us (26%)
  Pallas kernels  14.7 us (24%)
  local copies, waits for them, and re-layouts  4.94 us (8%)
  other arithmetic  0.65 us (1%)
    ppermute x14, starting transfers between devices, exchange(): return lax.ppermute(x, axis, [(k, k ^ mask) for k in range(count)])  24.5 us
    ppermute x14, waiting for transfers between devices, exchange(): return lax.ppermute(x, axis, [(k, k ^ mask) for k in range(count)])  16.2 us
    pallas_call x1, Pallas kernels, project_rest(): pl.pallas_call(functools.partial(rest_kernel, n, tiles), in_specs=[in_hbm...  5 us
    unnamed x6, local copies, waits for them, and re-layouts  4.94 us
    pallas_call x1, Pallas kernels, score(): pl.pallas_call(functools.partial(score_kernel, n, sub, len(grads)), in_sp...  3.65 us
    pallas_call x1, Pallas kernels, project_sent(): pl.pallas_call(functools.partial(in_kernel, tiles), in_specs=[in_hbm()] *...  2.96 us
    pallas_call x2, Pallas kernels, split_store(): pl.pallas_call(functools.partial(split_kernel, start, tiles), in_specs=[i...  2.27 us
  transfers between devices with their start and end apart: 14, of which 8 were waited for; matrix products, arithmetic and copies ran while one was open for 0% of the time, Pallas kernels for 13%

profile of v2, /device:TPU:0, one launch (start us, length us, event | category | flops | bytes accessed | tf_op | source)
XLA Modules:
  0.0 61.1 jit_solution(7261863601329024716)
XLA Ops:
  0.0 3.0 %project_sent.1.after_ref = f32[512,128]{1,0:T(8,128)} custom-call(bf16[1024,2048]{1,0:T(8,128)(2,1)} %bitcast.2, bf16[2048,128]{1,0:T(8,128)(2,1)} %in_w_ref.1), custom_call_target="tpu_custom_call" | custom-call | flops 268435456 | tf_op jit(solution)/shard_map/project_sent/pallas_call | solution.py:80
  3.0 3.1 %collective-permute-start = (f32[512,128]{1,0:T(8,128)}, f32[512,128]{1,0:T(8,128)S(1)}, u32[]{:S(2)}, u32[]{:S(2)}) collective-permute-start(f32[512,128]{1,0:T(8,128)} %project_sent.1.after_ref), channel_id=1, source_target_pairs={{0,4},{4,0},{8,12},{12,8},{1,5},{5,1},{9,13},{13,9},{2,6},{6,2},{1... | collective-permute-start | bytes 786440 | tf_op jit(solution)/shard_map/ppermute | solution.py:49
  6.1 5.0 %project_rest.1 = (f32[64,1024]{1,0:T(8,128)}, f32[64,1024]{1,0:T(8,128)}, f32[512,128]{1,0:T(8,128)}) custom-call(bf16[1024,2048]{1,0:T(8,128)(2,1)} %bitcast.4, bf16[2048,128]{1,0:T(8,128)(2,1)} %out_w_ref.1, bf16[1024,2048]{1,0:T(8,128)(2,1)} %bitcast.3, bf16[2048,128]{1,0:T(8,128)(2,1)} %in_w_ref.1, f32[512,128]{1,0:T(8,128)} %project_sent.1.after_ref), custom_call_target="tpu_custom_call" | custom-call | flops 805306368 | tf_op jit(solution)/shard_map/project_rest/pallas_call | solution.py:137
  11.1 0.1 collective-permute-start.2
  11.1 1.4 %collective-permute-done.b_ref = f32[512,128]{1,0:T(8,128)S(1)} collective-permute-done((f32[512,128]{1,0:T(8,128)}, f32[512,128]{1,0:T(8,128)S(1)}, u32[]{:S(2)}, u32[]{:S(2)}) %collective-permute-start) | collective-permute-done | bytes 262176 | tf_op jit(solution)/shard_map/ppermute | solution.py:49
  12.6 0.0 copy-start.2
  12.6 0.9 %copy-done.2 = f32[512,128]{1,0:T(8,128)S(1)} copy-done((f32[512,128]{1,0:T(8,128)S(1)}, f32[512,128]{1,0:T(8,128)}, u32[]{:S(2)}) %copy-start.2) | copy-done | bytes 262168
  13.6 4.1 %collective-permute-start.1 = (f32[512,128]{1,0:T(8,128)S(1)}, f32[512,128]{1,0:T(8,128)S(1)}, u32[]{:S(2)}, u32[]{:S(2)}) collective-permute-start(f32[512,128]{1,0:T(8,128)S(1)} %add.19.a_ref.after_ref), channel_id=1, source_target_pairs={{0,12},{4,8},{8,4},{12,0},{1,13},{5,9},{9,5},{13,1},{2,14},{6,10},... | collective-permute-start | bytes 786440 | tf_op jit(solution)/shard_map/ppermute | solution.py:49
  17.7 0.0 copy-start
  17.7 4.0 %copy-done = f32[640,4096]{1,0:T(8,128)S(1)} copy-done((f32[640,4096]{1,0:T(8,128)S(1)}, f32[640,4096]{1,0:T(8,128)}, u32[]{:S(2)}) %copy-start) | copy-done | bytes 10485784
  21.7 0.0 copy-start.1
  21.7 0.9 %split_store.2 = (bf16[256,4096]{1,0:T(8,128)(2,1)S(1)}, bf16[256,4096]{1,0:T(8,128)(2,1)S(1)}) custom-call(f32[640,4096]{1,0:T(8,128)S(1)} %copy-done, f32[512,128]{1,0:T(8,128)S(1)} %add.19.a_ref.after_ref), custom_call_target="tpu_custom_call" | custom-call | flops 1048576000 | tf_op jit(solution)/shard_map/split_store/pallas_call | solution.py:235
  22.6 0.0 collective-permute-done.2.b_ref
  22.6 0.0 copy-done.1
  22.7 6.4 %collective-permute-start.3 = (f32[32,1024]{1,0:T(8,128)S(1)}, f32[32,1024]{1,0:T(8,128)S(1)}, u32[]{:S(2)}, u32[]{:S(2)}) collective-permute-start(f32[32,1024]{1,0:T(8,128)S(1)} %get-tuple-element.23), channel_id=1, source_target_pairs={{0,12},{4,8},{8,4},{12,0},{1,13},{5,9},{9,5},{13,1},{2,14},{6,10},... | collective-permute-start | bytes 393224 | tf_op jit(solution)/shard_map/ppermute | solution.py:49
  29.1 0.0 collective-permute-done.1.b_ref
  29.1 1.2 %collective-permute-start.4 = (f32[512,128]{1,0:T(8,128)S(1)}, f32[512,128]{1,0:T(8,128)S(1)}, u32[]{:S(2)}, u32[]{:S(2)}) collective-permute-start(f32[512,128]{1,0:T(8,128)S(1)} %add.20.after_ref.in_ref), channel_id=1, source_target_pairs={{0,4},{4,0},{8,12},{12,8},{1,5},{5,1},{9,13},{13,9},{2,6},{6,2},{1... | collective-permute-start | bytes 786440 | tf_op jit(solution)/shard_map/ppermute | solution.py:49
  30.3 1.4 %split_store.3 = (bf16[384,4096]{1,0:T(8,128)(2,1)S(1)}, bf16[384,4096]{1,0:T(8,128)(2,1)S(1)}) custom-call(f32[640,4096]{1,0:T(8,128)S(1)} %copy-done, f32[512,128]{1,0:T(8,128)S(1)} %add.20.after_ref.in_ref), custom_call_target="tpu_custom_call" | custom-call | flops 1572864000 | tf_op jit(solution)/shard_map/split_store/pallas_call | solution.py:235
  31.7 1.6 %collective-permute-done.3.b_ref = f32[32,1024]{1,0:T(8,128)S(1)} collective-permute-done((f32[32,1024]{1,0:T(8,128)S(1)}, f32[32,1024]{1,0:T(8,128)S(1)}, u32[]{:S(2)}, u32[]{:S(2)}) %collective-permute-start.3) | collective-permute-done | bytes 131104 | tf_op jit(solution)/shard_map/ppermute | solution.py:49
  33.3 0.4 outer.2.refs_0_
  33.7 1.5 %collective-permute-start.7 = (f32[32,16,128]{2,1,0:T(8,128)S(1)}, f32[32,16,128]{2,1,0:T(8,128)S(1)}, u32[]{:S(2)}, u32[]{:S(2)}) collective-permute-start(f32[32,16,128]{2,1,0:T(8,128)S(1)} %outer.2.refs_0_), channel_id=1, source_target_pairs={{0,2},{2,0},{1,3},{3,1},{4,6},{6,4},{5,7},{7,5},{8,10},{10,8},{9,1... | collective-permute-start | bytes 786440 | tf_op jit(solution)/shard_map/ppermute | solution.py:49
  35.2 0.6 collective-permute-done.4.in_ref
  35.8 0.4 outer.3.refs_1_
  36.2 1.5 %collective-permute-start.8 = (f32[32,16,128]{2,1,0:T(8,128)S(1)}, f32[32,16,128]{2,1,0:T(8,128)S(1)}, u32[]{:S(2)}, u32[]{:S(2)}) collective-permute-start(f32[32,16,128]{2,1,0:T(8,128)S(1)} %outer.3.refs_1_), channel_id=1, source_target_pairs={{0,2},{2,0},{1,3},{3,1},{4,6},{6,4},{5,7},{7,5},{8,10},{10,8},{9,1... | collective-permute-start | bytes 786440 | tf_op jit(solution)/shard_map/ppermute | solution.py:49
  37.8 0.0 collective-permute-start.5
  37.8 0.5 collective-permute-start.6
  38.3 2.1 %collective-permute-done.7.refs_4_ = f32[32,16,128]{2,1,0:T(8,128)S(1)} collective-permute-done((f32[32,16,128]{2,1,0:T(8,128)S(1)}, f32[32,16,128]{2,1,0:T(8,128)S(1)}, u32[]{:S(2)}, u32[]{:S(2)}) %collective-permute-start.7) | collective-permute-done | bytes 262176 | tf_op jit(solution)/shard_map/ppermute | solution.py:49
  40.4 0.0 collective-permute-start.9
  40.4 2.8 %collective-permute-done.8.refs_5_ = f32[32,16,128]{2,1,0:T(8,128)S(1)} collective-permute-done((f32[32,16,128]{2,1,0:T(8,128)S(1)}, f32[32,16,128]{2,1,0:T(8,128)S(1)}, u32[]{:S(2)}, u32[]{:S(2)}) %collective-permute-start.8) | collective-permute-done | bytes 262176 | tf_op jit(solution)/shard_map/ppermute | solution.py:49
  43.2 0.0 collective-permute-start.10
  43.2 0.0 collective-permute-done.5.refs_2_
  43.2 0.0 collective-permute-done.9.refs_6_
  43.2 0.0 collective-permute-done.6.refs_3_
  43.2 1.5 %collective-permute-done.10.refs_7_ = f32[32,16,128]{2,1,0:T(8,128)S(1)} collective-permute-done((f32[32,16,128]{2,1,0:T(8,128)S(1)}, f32[32,16,128]{2,1,0:T(8,128)S(1)}, u32[]{:S(2)}, u32[]{:S(2)}) %collective-permute-start.10) | collective-permute-done | bytes 262176 | tf_op jit(solution)/shard_map/ppermute | solution.py:49
  44.7 3.7 %score.1 = (f32[32,640]{1,0:T(8,128)S(1)}, f32[32,640]{1,0:T(8,128)S(1)}, f32[32,640]{1,0:T(8,128)S(1)}, f32[32,640]{1,0:T(8,128)S(1)}) custom-call(f32[32,16,128]{2,1,0:T(8,128)S(1)} %outer.2.refs_0_, f32[32,16,128]{2,1,0:T(8,128)S(1)} %outer.3.refs_1_, f32[32,16,128]{2,1,0:T(8,128)S(1)} %collective-permute-done.5.refs_2_, ...), custom_call_target="tpu_custom_call" | custom-call | flops 2013265920 | bytes 10485760 | tf_op jit(solution)/shard_map/score/pallas_call | solution.py:280
  48.4 3.5 %collective-permute-start.11 = (f32[32,640]{1,0:T(8,128)S(1)}, f32[32,640]{1,0:T(8,128)S(1)}, u32[]{:S(2)}, u32[]{:S(2)}) collective-permute-start(f32[32,640]{1,0:T(8,128)S(1)} %get-tuple-element.28), channel_id=1, source_target_pairs={{0,4},{4,0},{8,12},{12,8},{1,5},{5,1},{9,13},{13,9},{2,6},{6,2},{1... | collective-permute-start | bytes 245768 | tf_op jit(solution)/shard_map/ppermute | solution.py:49
  51.9 0.0 collective-permute-start.12
  51.9 2.4 %collective-permute-start.13 = (f32[32,640]{1,0:T(8,128)S(1)}, f32[32,640]{1,0:T(8,128)S(1)}, u32[]{:S(2)}, u32[]{:S(2)}) collective-permute-start(f32[32,640]{1,0:T(8,128)S(1)} %get-tuple-element.30), channel_id=1, source_target_pairs={{0,12},{4,8},{8,4},{12,0},{1,13},{5,9},{9,5},{13,1},{2,14},{6,10},... | collective-permute-start | bytes 245768 | tf_op jit(solution)/shard_map/ppermute | solution.py:49
  54.3 0.4 collective-permute-done.11
  54.7 5.7 %collective-permute-done.12 = f32[32,640]{1,0:T(8,128)S(1)} collective-permute-done((f32[32,640]{1,0:T(8,128)S(1)}, f32[32,640]{1,0:T(8,128)S(1)}, u32[]{:S(2)}, u32[]{:S(2)}) %collective-permute-start.12) | collective-permute-done | bytes 81952 | tf_op jit(solution)/shard_map/ppermute | solution.py:49
  60.5 0.0 collective-permute-done.13
  60.5 0.7 %add_add_fusion = f32[32,640]{1,0:T(8,128)} fusion(f32[32,640]{1,0:T(8,128)S(1)} %collective-permute-done.13, f32[32,640]{1,0:T(8,128)S(1)} %collective-permute-done.12, f32[32,640]{1,0:T(8,128)S(1)} %get-tuple-element.27, f32[32,640]{1,0:T(8,128)S(1)} %collective-permute-done.11), kind=kLoop, calls=%fused_computation | loop fusion | flops 61440 | bytes 409600 | tf_op jit(solution)/shard_map/add | solution.py:353
  (4 shorter events, 0.1 us)
Async XLA Ops:
  3.0 9.6 %collective-permute-start = (f32[512,128]{1,0:T(8,128)}, f32[512,128]{1,0:T(8,128)S(1)}, u32[]{:S(2)}, u32[]{:S(2)}) collective-permute-start(f32[512,128]{1,0:T(8,128)} %project_sent.1.after_ref), channel_id=1, source_target_pairs={{0,4},{4,0},{8,12},{12,8},{1,5},{5,1},{9,13},{13,9},{2,6},{6,2},{1... | collective-permute-start | bytes 786440 | tf_op jit(solution)/shard_map/ppermute | solution.py:49
  11.1 11.5 %collective-permute-start.2 = (f32[64,1024]{1,0:T(8,128)}, f32[64,1024]{1,0:T(8,128)S(1)}, u32[]{:S(2)}, u32[]{:S(2)}) collective-permute-start(f32[64,1024]{1,0:T(8,128)} %get-tuple-element.20), channel_id=1, source_target_pairs={{0,4},{4,0},{8,12},{12,8},{1,5},{5,1},{9,13},{13,9},{2,6},{6,2},{1... | collective-permute-start | bytes 786440 | tf_op jit(solution)/shard_map/ppermute | solution.py:49
  12.6 1.0 %copy-start.2 = (f32[512,128]{1,0:T(8,128)S(1)}, f32[512,128]{1,0:T(8,128)}, u32[]{:S(2)}) copy-start(f32[512,128]{1,0:T(8,128)} %get-tuple-element.18.a_ref) | copy-start | bytes 786436
  13.6 15.5 %collective-permute-start.1 = (f32[512,128]{1,0:T(8,128)S(1)}, f32[512,128]{1,0:T(8,128)S(1)}, u32[]{:S(2)}, u32[]{:S(2)}) collective-permute-start(f32[512,128]{1,0:T(8,128)S(1)} %add.19.a_ref.after_ref), channel_id=1, source_target_pairs={{0,12},{4,8},{8,4},{12,0},{1,13},{5,9},{9,5},{13,1},{2,14},{6,10},... | collective-permute-start | bytes 786440 | tf_op jit(solution)/shard_map/ppermute | solution.py:49
  17.7 4.0 %copy-start = (f32[640,4096]{1,0:T(8,128)S(1)}, f32[640,4096]{1,0:T(8,128)}, u32[]{:S(2)}) copy-start(f32[640,4096]{1,0:T(8,128)} %x_ref.3) | copy-start | bytes 31457284
  21.7 0.9 %copy-start.1 = (f32[64,1024]{1,0:T(8,128)S(1)}, f32[64,1024]{1,0:T(8,128)}, u32[]{:S(2)}) copy-start(f32[64,1024]{1,0:T(8,128)} %get-tuple-element.19.a_ref) | copy-start | bytes 786436
  22.7 10.7 %collective-permute-start.3 = (f32[32,1024]{1,0:T(8,128)S(1)}, f32[32,1024]{1,0:T(8,128)S(1)}, u32[]{:S(2)}, u32[]{:S(2)}) collective-permute-start(f32[32,1024]{1,0:T(8,128)S(1)} %get-tuple-element.23), channel_id=1, source_target_pairs={{0,12},{4,8},{8,4},{12,0},{1,13},{5,9},{9,5},{13,1},{2,14},{6,10},... | collective-permute-start | bytes 393224 | tf_op jit(solution)/shard_map/ppermute | solution.py:49
  29.1 6.7 %collective-permute-start.4 = (f32[512,128]{1,0:T(8,128)S(1)}, f32[512,128]{1,0:T(8,128)S(1)}, u32[]{:S(2)}, u32[]{:S(2)}) collective-permute-start(f32[512,128]{1,0:T(8,128)S(1)} %add.20.after_ref.in_ref), channel_id=1, source_target_pairs={{0,4},{4,0},{8,12},{12,8},{1,5},{5,1},{9,13},{13,9},{2,6},{6,2},{1... | collective-permute-start | bytes 786440 | tf_op jit(solution)/shard_map/ppermute | solution.py:49
  33.7 6.7 %collective-permute-start.7 = (f32[32,16,128]{2,1,0:T(8,128)S(1)}, f32[32,16,128]{2,1,0:T(8,128)S(1)}, u32[]{:S(2)}, u32[]{:S(2)}) collective-permute-start(f32[32,16,128]{2,1,0:T(8,128)S(1)} %outer.2.refs_0_), channel_id=1, source_target_pairs={{0,2},{2,0},{1,3},{3,1},{4,6},{6,4},{5,7},{7,5},{8,10},{10,8},{9,1... | collective-permute-start | bytes 786440 | tf_op jit(solution)/shard_map/ppermute | solution.py:49
  36.2 7.0 %collective-permute-start.8 = (f32[32,16,128]{2,1,0:T(8,128)S(1)}, f32[32,16,128]{2,1,0:T(8,128)S(1)}, u32[]{:S(2)}, u32[]{:S(2)}) collective-permute-start(f32[32,16,128]{2,1,0:T(8,128)S(1)} %outer.3.refs_1_), channel_id=1, source_target_pairs={{0,2},{2,0},{1,3},{3,1},{4,6},{6,4},{5,7},{7,5},{8,10},{10,8},{9,1... | collective-permute-start | bytes 786440 | tf_op jit(solution)/shard_map/ppermute | solution.py:49
  37.8 5.4 %collective-permute-start.5 = (f32[32,16,128]{2,1,0:T(8,128)S(1)}, f32[32,16,128]{2,1,0:T(8,128)S(1)}, u32[]{:S(2)}, u32[]{:S(2)}) collective-permute-start(f32[32,16,128]{2,1,0:T(8,128)S(1)} %outer.2.refs_0_), channel_id=1, source_target_pairs={{0,1},{1,0},{2,3},{3,2},{4,5},{5,4},{6,7},{7,6},{8,9},{9,8},{10,11... | collective-permute-start | bytes 786440 | tf_op jit(solution)/shard_map/ppermute | solution.py:49
  37.8 5.4 %collective-permute-start.6 = (f32[32,16,128]{2,1,0:T(8,128)S(1)}, f32[32,16,128]{2,1,0:T(8,128)S(1)}, u32[]{:S(2)}, u32[]{:S(2)}) collective-permute-start(f32[32,16,128]{2,1,0:T(8,128)S(1)} %outer.3.refs_1_), channel_id=1, source_target_pairs={{0,1},{1,0},{2,3},{3,2},{4,5},{5,4},{6,7},{7,6},{8,9},{9,8},{10,11... | collective-permute-start | bytes 786440 | tf_op jit(solution)/shard_map/ppermute | solution.py:49
  40.4 2.8 %collective-permute-start.9 = (f32[32,16,128]{2,1,0:T(8,128)S(1)}, f32[32,16,128]{2,1,0:T(8,128)S(1)}, u32[]{:S(2)}, u32[]{:S(2)}) collective-permute-start(f32[32,16,128]{2,1,0:T(8,128)S(1)} %collective-permute-done.7.refs_4_), channel_id=1, source_target_pairs={{0,1},{1,0},{2,3},{3,2},{4,5},{5,4},{6,7},{7,6},{8,9},{9,8},{10,11... | collective-permute-start | bytes 786440 | tf_op jit(solution)/shard_map/ppermute | solution.py:49
  43.2 1.5 %collective-permute-start.10 = (f32[32,16,128]{2,1,0:T(8,128)S(1)}, f32[32,16,128]{2,1,0:T(8,128)S(1)}, u32[]{:S(2)}, u32[]{:S(2)}) collective-permute-start(f32[32,16,128]{2,1,0:T(8,128)S(1)} %collective-permute-done.8.refs_5_), channel_id=1, source_target_pairs={{0,1},{1,0},{2,3},{3,2},{4,5},{5,4},{6,7},{7,6},{8,9},{9,8},{10,11... | collective-permute-start | bytes 786440 | tf_op jit(solution)/shard_map/ppermute | solution.py:49
  48.4 6.3 %collective-permute-start.11 = (f32[32,640]{1,0:T(8,128)S(1)}, f32[32,640]{1,0:T(8,128)S(1)}, u32[]{:S(2)}, u32[]{:S(2)}) collective-permute-start(f32[32,640]{1,0:T(8,128)S(1)} %get-tuple-element.28), channel_id=1, source_target_pairs={{0,4},{4,0},{8,12},{12,8},{1,5},{5,1},{9,13},{13,9},{2,6},{6,2},{1... | collective-permute-start | bytes 245768 | tf_op jit(solution)/shard_map/ppermute | solution.py:49
  51.9 8.6 %collective-permute-start.12 = (f32[32,640]{1,0:T(8,128)S(1)}, f32[32,640]{1,0:T(8,128)S(1)}, u32[]{:S(2)}, u32[]{:S(2)}) collective-permute-start(f32[32,640]{1,0:T(8,128)S(1)} %get-tuple-element.29), channel_id=1, source_target_pairs={{0,8},{4,12},{8,0},{12,4},{1,9},{5,13},{9,1},{13,5},{2,10},{6,14},... | collective-permute-start | bytes 245768 | tf_op jit(solution)/shard_map/ppermute | solution.py:49
  51.9 8.6 %collective-permute-start.13 = (f32[32,640]{1,0:T(8,128)S(1)}, f32[32,640]{1,0:T(8,128)S(1)}, u32[]{:S(2)}, u32[]{:S(2)}) collective-permute-start(f32[32,640]{1,0:T(8,128)S(1)} %get-tuple-element.30), channel_id=1, source_target_pairs={{0,12},{4,8},{8,4},{12,0},{1,13},{5,9},{9,5},{13,1},{2,14},{6,10},... | collective-permute-start | bytes 245768 | tf_op jit(solution)/shard_map/ppermute | solution.py:49

commit v3 on v2

v3 whole, which is shorter than its diff:
```python
import functools

import jax
import jax.numpy as jnp
from jax import lax
from jax.experimental import pallas as pl
from jax.experimental.pallas import tpu as pltpu
from jax.sharding import PartitionSpec as P

BF16, F32 = jnp.bfloat16, jnp.float32
NT = (((1,), (1,)), ((), ()))
NN = (((1,), (0,)), ((), ()))
MIB = 1024 * 1024


def params(limit):
    return pltpu.CompilerParams(vmem_limit_bytes=limit * MIB)


def in_vmem():
    return pl.BlockSpec(memory_space=pltpu.VMEM)


def anywhere():
    return pl.BlockSpec(memory_space=pl.ANY)


def in_hbm():
    return pl.BlockSpec(memory_space=pltpu.HBM)


def gray(k):
    return k ^ (k >> 1)


def ungray(code):
    k = 0
    while code:
        k ^= code
        code >>= 1
    return k


def reversed_bits(value, bits):
    return sum(((value >> b) & 1) << (bits - 1 - b) for b in range(bits))


def exchange(x, axis, count, mask):
    return lax.ppermute(x, axis, [(k, k ^ mask) for k in range(count)])


def split(x):
    high = x.astype(BF16)
    return high, (x - high.astype(F32)).astype(BF16)


def sent_kernel(x_ref, w_ref, out_ref):
    rows = out_ref.shape[0]
    half = (gray(lax.axis_index("feat")) & 1) ^ 1
    place = pl.ds(pl.multiple_of(half * 2 * rows, rows), rows)
    out_ref[...] = jnp.dot(x_ref[place, :], w_ref[...], preferred_element_type=F32)


def project_sent(x, w):
    rows, width = x.shape
    rank = w.shape[1]
    return pl.pallas_call(
        sent_kernel,
        in_specs=[in_vmem()] * 2,
        out_specs=in_vmem(),
        out_shape=jax.ShapeDtypeStruct((rows // 4, rank), F32),
        compiler_params=params(16),
        cost_estimate=pl.CostEstimate(flops=rows * width * rank, bytes_accessed=rows * width, transcendentals=0),
        name="project_sent",
    )(x, w)


def rest_kernel(n, tiles, in_x_ref, in_w_ref, out_x_ref, out_w_ref, after_ref, *rest):
    del after_ref
    in_send_ref, in_first_ref, in_second_ref, out_keep_ref, out_send_ref, turned = rest
    bits = n.bit_length() - 1
    here = lax.axis_index("feat")
    half = gray(here) & 1
    rows = in_send_ref.shape[0]
    for ref, piece in (
        (in_send_ref, 2 * (half ^ 1) + 1),
        (in_first_ref, 2 * half),
        (in_second_ref, 2 * half + 1),
    ):
        place = pl.ds(pl.multiple_of(piece * rows, rows), rows)
        ref[...] = jnp.dot(in_x_ref[place, :], in_w_ref[...], preferred_element_type=F32)
    size = out_x_ref.shape[0] // tiles
    for t in range(tiles):
        tile = slice(t * size, (t + 1) * size)
        turned[:, tile] = jnp.dot(out_x_ref[tile, :], out_w_ref[...], preferred_element_type=F32).T
    features = turned.shape[0] // n
    for slot in range(n):
        chunk = here ^ ungray(reversed_bits(slot, bits))
        ref = out_keep_ref if slot < n // 2 else out_send_ref
        place = slot % (n // 2) * features
        ref[place : place + features, :] = turned[pl.ds(pl.multiple_of(chunk * features, features), features), :]


def project_rest(in_x, in_w, out_x, out_w, after, tiles, n):
    rows, width = out_x.shape
    rank = out_w.shape[1]
    piece = jax.ShapeDtypeStruct((rows // 4, rank), F32)
    out = jax.ShapeDtypeStruct((rank // 2, rows), F32)
    return pl.pallas_call(
        functools.partial(rest_kernel, n, tiles),
        in_specs=[in_vmem()] * 4 + [anywhere()],
        out_specs=[in_vmem()] * 5,
        out_shape=[piece] * 3 + [out] * 2,
        scratch_shapes=[pltpu.VMEM((rank, rows), F32)],
        compiler_params=params(16),
        cost_estimate=pl.CostEstimate(
            flops=3 * rows * width * rank, bytes_accessed=3 * rows * width, transcendentals=0
        ),
        name="project_rest",
    )(in_x, in_w, out_x, out_w, after)


def add_kernel(parts, a_ref, b_ref, *rest):
    out_refs = rest[len(rest) - parts :]
    size = a_ref.shape[0] // parts
    for k, out_ref in enumerate(out_refs):
        rows = slice(k * size, (k + 1) * size)
        out_ref[...] = a_ref[rows, :] + b_ref[rows, :]


def add(a, b, parts=1, after=(), weight=0.1):
    out = jax.ShapeDtypeStruct((a.shape[0] // parts, a.shape[1]), F32)
    return pl.pallas_call(
        functools.partial(add_kernel, parts),
        in_specs=[in_vmem()] * 2 + [anywhere()] * len(after),
        out_specs=[in_vmem()] * parts,
        out_shape=[out] * parts,
        compiler_params=params(8),
        cost_estimate=pl.CostEstimate(flops=int(weight * 1e9), bytes_accessed=12 * a.size, transcendentals=0),
        name="add",
    )(a, b, *after)


def add_beside_kernel(a_ref, b_ref, other_ref, sum_ref, same_ref):
    sum_ref[...] = a_ref[...] + b_ref[...]
    same_ref[...] = other_ref[...]


def add_beside(a, b, other, weight):
    return pl.pallas_call(
        add_beside_kernel,
        in_specs=[in_vmem()] * 3,
        out_specs=[in_vmem()] * 2,
        out_shape=[jax.ShapeDtypeStruct(a.shape, F32), jax.ShapeDtypeStruct(other.shape, F32)],
        compiler_params=params(8),
        cost_estimate=pl.CostEstimate(flops=int(weight * 1e9), bytes_accessed=12 * a.size, transcendentals=0),
        name="add_beside",
    )(a, b, other)


def outer_kernel(tokens, group, *refs):
    in_refs, (out_ref, grad_ref) = refs[:-2], refs[-2:]
    width = group * tokens
    rows, rank = in_refs[0].shape
    features = out_ref.shape[0]
    mine = gray(lax.axis_index("feat")) & 1
    query = lax.broadcasted_iota(jnp.int32, (group, width), 0)
    token = lax.broadcasted_iota(jnp.int32, (group, width), 1)
    own = jnp.where(token // tokens == query, 1.0, 0.0).astype(F32)
    for k, in_ref in enumerate(in_refs):
        half = mine ^ (k // 2)
        for g in range(rows // width):
            step = half * (2 * rows // width) + (k % 2) * (rows // width) + g
            columns = out_ref[:, pl.ds(pl.multiple_of(step * width, width), width)]
            spread = (columns[:, None, :] * own[None, :, :]).reshape(features * group, width)
            left, left_low = split(spread)
            right, right_low = split(in_ref[g * width : (g + 1) * width, :])
            total = jnp.dot(left, right, preferred_element_type=F32)
            total += jnp.dot(left_low, right, preferred_element_type=F32)
            total += jnp.dot(left, right_low, preferred_element_type=F32)
            place = pl.ds(pl.multiple_of(step * group, group), group)
            grad_ref[:, place, :] = total.reshape(features, group, rank)


def outer(in_pieces, out_columns, tokens, group):
    rank = in_pieces[0].shape[1]
    features, rows = out_columns.shape
    out = jax.ShapeDtypeStruct((features, rows // tokens, rank), F32)
    return pl.pallas_call(
        functools.partial(outer_kernel, tokens, group),
        in_specs=[in_vmem()] * (len(in_pieces) + 1),
        out_specs=in_vmem(),
        out_shape=out,
        compiler_params=params(16),
        cost_estimate=pl.CostEstimate(
            flops=6 * rows * group * features * rank, bytes_accessed=8 * rows * rank, transcendentals=0
        ),
        name="outer",
    )(*in_pieces, out_columns)


def split_kernel(first, tiles, x_ref, after_ref, high_ref, low_ref, x_buf, sems):
    del after_ref
    size = x_buf.shape[0] // tiles
    copies = []
    for t in range(tiles):
        copies.append(
            pltpu.make_async_copy(x_ref.at[pl.ds(first + t * size, size)], x_buf.at[pl.ds(t * size, size)], sems.at[t])
        )
        copies[t].start()
    for t in range(tiles):
        copies[t].wait()
        rows = slice(t * size, (t + 1) * size)
        high_ref[rows, :], low_ref[rows, :] = split(x_buf[rows, :])


def split_store(store, after, start, rows):
    width = store.shape[1]
    tiles = tile_count(rows, 16, 5)
    out = jax.ShapeDtypeStruct((rows, width), BF16)
    return pl.pallas_call(
        functools.partial(split_kernel, start, tiles),
        in_specs=[in_hbm(), anywhere()],
        out_specs=[in_vmem()] * 2,
        out_shape=[out] * 2,
        scratch_shapes=[pltpu.VMEM((rows, width), F32), pltpu.SemaphoreType.DMA((tiles,))],
        compiler_params=params(24),
        cost_estimate=pl.CostEstimate(flops=1000 * rows * width, bytes_accessed=0, transcendentals=0),
        name="split_store",
    )(store, after)


def score_kernel(n, sub, count, *refs):
    store_refs, out_refs, (both, result) = refs[count : -n - 2], refs[-n - 2 : -2], refs[-2:]
    grad_refs = refs[:count]
    features, queries, rank = grad_refs[0].shape
    total = count * queries
    for d, ref in enumerate(grad_refs):
        place = d * queries
        for i in range(features):
            high, low = split(ref[i])
            both[place : place + queries, i * rank : (i + 1) * rank] = high
            both[total + place : total + place + queries, i * rank : (i + 1) * rank] = low
    first = 0
    for high_ref, low_ref in zip(store_refs[::2], store_refs[1::2]):
        sums = lax.dot_general(both[...], high_ref[...], NT, preferred_element_type=F32)
        lows = lax.dot_general(both[:total, :], low_ref[...], NT, preferred_element_type=F32)
        result[:, first : first + high_ref.shape[0]] = sums[:total] + sums[total:] + lows
        first += high_ref.shape[0]
    own = lax.axis_index("feat") ^ (lax.axis_index("rows") * sub + lax.axis_index("sub"))
    size = queries
    for slot in range(n):
        out_refs[slot][...] = result[pl.ds(pl.multiple_of((own ^ slot) * size, size), size), :]


def score(grads, stored, n, sub):
    features, queries, rank = grads[0].shape
    examples, width = sum(part.shape[0] for part in stored[::2]), stored[0].shape[1]
    total = len(grads) * queries
    out = jax.ShapeDtypeStruct((total // n, examples), F32)
    return pl.pallas_call(
        functools.partial(score_kernel, n, sub, len(grads)),
        in_specs=[in_vmem()] * (len(grads) + len(stored)),
        out_specs=[in_vmem()] * n,
        out_shape=[out] * n,
        scratch_shapes=[pltpu.VMEM((2 * total, width), BF16), pltpu.VMEM((total, examples), F32)],
        compiler_params=params(24),
        cost_estimate=pl.CostEstimate(
            flops=6 * total * examples * width, bytes_accessed=4 * examples * width, transcendentals=0
        ),
        name="score",
    )(*grads, *stored)


def tile_count(extent, unit, most):
    return next(t for t in range(most, 0, -1) if extent % (t * unit) == 0)


def local(sizes, acts, out_grads, proj_in, proj_out, store):
    n, rows, sub = sizes["feat"], sizes["rows"], sizes["sub"]
    bits = n.bit_length() - 1
    queries, tokens, width = acts.shape
    flat = queries * tokens
    acts = acts.reshape(flat, width)
    out_grads = out_grads.reshape(flat, width)

    in_send = project_sent(acts, proj_in)
    in_recv = exchange(in_send, "feat", n, 1)
    in_send, *in_keep, out_keep, out_send = project_rest(acts, proj_in, out_grads, proj_out, in_send, 4, n)
    piece, out_send = add_beside(in_keep[0], in_recv, out_send, 2)
    pieces = [piece, *add(in_keep[1], exchange(in_send, "feat", n, 1), 1, (piece,), 1)]
    examples = store.shape[0]
    early = examples // 512 * 256
    stored = split_store(store, pieces[1], 0, early) if early else []
    for s in range(1, bits):
        mask = 2 ** (s + 1) - 1
        in_recvs = [exchange(piece, "feat", n, mask) for piece in pieces]
        out_keep, out_send = add(out_keep, exchange(out_send, "feat", n, mask // 2), 2, stored[:1])
        out_recv = exchange(out_send, "feat", n, mask)
        (first,) = add(pieces[0], in_recvs[0], 1, (), 1)
        pieces = [first, *add(pieces[1], in_recvs[1], 1, (first,), 1)]
    stored = stored + split_store(store, pieces[1], early, examples - early)
    (out_sum,) = add(out_keep, out_recv, 1, stored[-1:], weight=20)
    others = [exchange(piece, "feat", n, 1) for piece in pieces]

    blocks = [(0, [*pieces, *others], out_sum)]
    mask = 1
    while mask < rows:
        for d, block, out in list(blocks):
            parts = [exchange(part, "rows", rows, mask) for part in (*block, out)]
            blocks.append((d ^ (mask * sub), parts[:-1], parts[-1]))
        mask *= 2
    grads = {d: outer(block, out, tokens, 8) for d, block, out in blocks}
    mask = 1
    while mask < sub:
        for d, grad in list(grads.items()):
            grads[d ^ mask] = exchange(grad, "sub", sub, mask)
        mask *= 2
    grads = [grads[d] for d in range(len(grads))]
    parts = score(grads, stored, n, sub)
    moved = [exchange(parts[mask], "feat", n, mask) for mask in reversed(range(1, n))]
    total = parts[0]
    for part in reversed(moved):
        total = total + part
    return total


def solution(mesh):
    return jax.shard_map(
        functools.partial(local, dict(mesh.shape)),
        mesh=mesh,
        in_specs=(
            P(("groups", "rows", "sub"), None, "feat"),
            P(("groups", "rows", "sub"), None, "feat"),
            P("feat", None),
            P("feat", None),
            P(("groups", "rows", "sub"), "feat"),
        ),
        out_specs=P(("groups", "feat"), ("rows", "sub")),
        check_vma=False,
    )
```

time: 61.4 us -> 58.9 us (0.959)
  starting transfers between devices: 24.5 us -> 30.3 us
  Pallas kernels: 14.7 us -> 9.52 us
  local copies, waits for them, and re-layouts: 4.94 us -> 3.25 us
  waiting for transfers between devices: 16.2 us -> 14.8 us
    ppermute x14 -> x18, starting transfers between devices: 24.5 us -> 30.3 us  [exchange(): return lax.ppermute(x, axis, [(k, k ^ mask) for k in range(count)])]
    pallas_call x4 -> x5, Pallas kernels: 8.69 us -> 3.76 us  [the longest x1 2.16 us: project_rest(): pl.pallas_call(functools.partial(rest_kernel, n, tiles), in_specs=[in_vme...]
    unnamed x6 -> x14, local copies, waits for them, and re-layouts: 4.94 us -> 3.25 us
    ppermute x14 -> x18, waiting for transfers between devices: 16.2 us -> 14.8 us  [exchange(): return lax.ppermute(x, axis, [(k, k ^ mask) for k in range(count)])]
  transfers between devices with their start and end apart: 14 -> 18, of which waited for: 8 -> 11; matrix products, arithmetic and copies ran while one was open for 0% -> 0% of each run, Pallas kernels for 13% -> 10%
where the time goes in v3:
time: 58.9 us; the launch traced here: 58.7 us
  starting transfers between devices  30.3 us (51%)
  waiting for transfers between devices  14.8 us (25%)
  Pallas kernels  9.52 us (16%)
  local copies, waits for them, and re-layouts  3.25 us (6%)
  other arithmetic  0.65 us (1%)
    ppermute x18, starting transfers between devices, exchange(): return lax.ppermute(x, axis, [(k, k ^ mask) for k in range(count)])  30.3 us
    ppermute x18, waiting for transfers between devices, exchange(): return lax.ppermute(x, axis, [(k, k ^ mask) for k in range(count)])  14.8 us
    pallas_call x1, Pallas kernels, score(): pl.pallas_call(functools.partial(score_kernel, n, sub, len(grads)), in_sp...  3.39 us
    unnamed x14, local copies, waits for them, and re-layouts  3.25 us
    pallas_call x2, Pallas kernels, split_store(): pl.pallas_call(functools.partial(split_kernel, start, tiles), in_specs=[i...  2.28 us
    pallas_call x1, Pallas kernels, project_rest(): pl.pallas_call(functools.partial(rest_kernel, n, tiles), in_specs=[in_vme...  2.16 us
  transfers between devices with their start and end apart: 18, of which 11 were waited for; matrix products, arithmetic and copies ran while one was open for 0% of the time, Pallas kernels for 10%

profile of v3, /device:TPU:0, one launch (start us, length us, event | category | flops | bytes accessed | tf_op | source)
XLA Modules:
  0.0 58.7 jit_solution(5235882881233273534)
XLA Ops:
  0.0 2.2 %copy-done = bf16[32,32,2048]{2,1,0:T(8,128)(2,1)S(1)} copy-done((bf16[32,32,2048]{2,1,0:T(8,128)(2,1)S(1)}, bf16[32,32,2048]{2,1,0:T(8,128)(2,1)}, u32[]{:S(2)}) %copy-start) | copy-done | bytes 4194328
  2.2 1.0 %copy-done.2 = bf16[2048,128]{1,0:T(8,128)(2,1)S(1)} copy-done((bf16[2048,128]{1,0:T(8,128)(2,1)S(1)}, bf16[2048,128]{1,0:T(8,128)(2,1)}, u32[]{:S(2)}) %copy-start.2) | copy-done | bytes 524312
  3.2 0.4 project_sent.1.after_ref
  3.7 3.1 %collective-permute-start = (f32[256,128]{1,0:T(8,128)S(1)}, f32[256,128]{1,0:T(8,128)S(1)}, u32[]{:S(2)}, u32[]{:S(2)}) collective-permute-start(f32[256,128]{1,0:T(8,128)S(1)} %project_sent.1.after_ref), channel_id=1, source_target_pairs={{0,4},{4,0},{8,12},{12,8},{1,5},{5,1},{9,13},{13,9},{2,6},{6,2},{1... | collective-permute-start | bytes 393224 | tf_op jit(solution)/shard_map/ppermute | solution.py:49
  6.8 0.0 copy-done.1
  6.8 2.2 %project_rest.1 = (f32[256,128]{1,0:T(8,128)S(1)}, f32[256,128]{1,0:T(8,128)S(1)}, f32[256,128]{1,0:T(8,128)S(1)}, f32[64,1024]{1,0:T(8,128)S(1)}, f32[64,1024]{1,0:T(8,128)S(1)}) custom-call(bf16[1024,2048]{1,0:T(8,128)(2,1)S(1)} %bitcast.5, bf16[2048,128]{1,0:T(8,128)(2,1)S(1)} %copy-done.2, bf16[1024,2048]{1,0:T(8,128)(2,1)S(1)} %bitcast.6, ...), custom_call_target="tpu_custom_call" | custom-call | flops 805306368 | bytes 6291456 | tf_op jit(solution)/shard_map/project_rest/pallas_call | solution.py:109
  8.9 1.9 %collective-permute-start.2 = (f32[256,128]{1,0:T(8,128)S(1)}, f32[256,128]{1,0:T(8,128)S(1)}, u32[]{:S(2)}, u32[]{:S(2)}) collective-permute-start(f32[256,128]{1,0:T(8,128)S(1)} %get-tuple-element.26), channel_id=1, source_target_pairs={{0,4},{4,0},{8,12},{12,8},{1,5},{5,1},{9,13},{13,9},{2,6},{6,2},{1... | collective-permute-start | bytes 393224 | tf_op jit(solution)/shard_map/ppermute | solution.py:49
  10.8 0.0 collective-permute-done.b_ref
  10.8 3.3 %collective-permute-start.1 = (f32[256,128]{1,0:T(8,128)S(1)}, f32[256,128]{1,0:T(8,128)S(1)}, u32[]{:S(2)}, u32[]{:S(2)}) collective-permute-start(f32[256,128]{1,0:T(8,128)S(1)} %get-tuple-element.24.a_ref.rest_0_), channel_id=1, source_target_pairs={{0,12},{4,8},{8,4},{12,0},{1,13},{5,9},{9,5},{13,1},{2,14},{6,10},... | collective-permute-start | bytes 393224 | tf_op jit(solution)/shard_map/ppermute | solution.py:49
  14.1 0.2 collective-permute-done.2.b_ref
  14.3 5.2 %collective-permute-start.3 = (f32[256,128]{1,0:T(8,128)S(1)}, f32[256,128]{1,0:T(8,128)S(1)}, u32[]{:S(2)}, u32[]{:S(2)}) collective-permute-start(f32[256,128]{1,0:T(8,128)S(1)} %add.21.a_ref.after_ref), channel_id=1, source_target_pairs={{0,12},{4,8},{8,4},{12,0},{1,13},{5,9},{9,5},{13,1},{2,14},{6,10},... | collective-permute-start | bytes 393224 | tf_op jit(solution)/shard_map/ppermute | solution.py:49
  19.6 0.0 collective-permute-start.6
  19.6 0.0 slice-done.2
  19.6 0.9 %split_store.2 = (bf16[256,4096]{1,0:T(8,128)(2,1)S(1)}, bf16[256,4096]{1,0:T(8,128)(2,1)S(1)}) custom-call(f32[640,4096]{1,0:T(8,128)S(1)} %bitcast.3, f32[256,128]{1,0:T(8,128)S(1)} %add.21.a_ref.after_ref), custom_call_target="tpu_custom_call" | custom-call | flops 1048576000 | tf_op jit(solution)/shard_map/split_store/pallas_call | solution.py:221
  20.5 0.1 collective-permute-done.1.b_ref
  20.7 1.6 %collective-permute-start.9 = (f32[256,128]{1,0:T(8,128)S(1)}, f32[256,128]{1,0:T(8,128)S(1)}, u32[]{:S(2)}, u32[]{:S(2)}) collective-permute-start(f32[256,128]{1,0:T(8,128)S(1)} %add.20.rest_0_.refs_0_), channel_id=1, source_target_pairs={{0,2},{2,0},{1,3},{3,1},{4,6},{6,4},{5,7},{7,5},{8,10},{10,8},{9,1... | collective-permute-start | bytes 393224 | tf_op jit(solution)/shard_map/ppermute | solution.py:49
  22.2 1.9 %collective-permute-start.4 = (f32[256,128]{1,0:T(8,128)S(1)}, f32[256,128]{1,0:T(8,128)S(1)}, u32[]{:S(2)}, u32[]{:S(2)}) collective-permute-start(f32[256,128]{1,0:T(8,128)S(1)} %add.20.rest_0_.refs_0_), channel_id=1, source_target_pairs={{0,4},{4,0},{8,12},{12,8},{1,5},{5,1},{9,13},{13,9},{2,6},{6,2},{1... | collective-permute-start | bytes 393224 | tf_op jit(solution)/shard_map/ppermute | solution.py:49
  24.1 0.0 collective-permute-done.3.b_ref
  24.1 1.4 %collective-permute-start.10 = (f32[256,128]{1,0:T(8,128)S(1)}, f32[256,128]{1,0:T(8,128)S(1)}, u32[]{:S(2)}, u32[]{:S(2)}) collective-permute-start(f32[256,128]{1,0:T(8,128)S(1)} %add.22.after_ref.refs_1_), channel_id=1, source_target_pairs={{0,2},{2,0},{1,3},{3,1},{4,6},{6,4},{5,7},{7,5},{8,10},{10,8},{9,1... | collective-permute-start | bytes 393224 | tf_op jit(solution)/shard_map/ppermute | solution.py:49
  25.5 1.7 %collective-permute-start.5 = (f32[256,128]{1,0:T(8,128)S(1)}, f32[256,128]{1,0:T(8,128)S(1)}, u32[]{:S(2)}, u32[]{:S(2)}) collective-permute-start(f32[256,128]{1,0:T(8,128)S(1)} %add.22.after_ref.refs_1_), channel_id=1, source_target_pairs={{0,4},{4,0},{8,12},{12,8},{1,5},{5,1},{9,13},{13,9},{2,6},{6,2},{1... | collective-permute-start | bytes 393224 | tf_op jit(solution)/shard_map/ppermute | solution.py:49
  27.3 1.9 %collective-permute-done.6.b_ref = f32[64,1024]{1,0:T(8,128)S(1)} collective-permute-done((f32[64,1024]{1,0:T(8,128)S(1)}, f32[64,1024]{1,0:T(8,128)S(1)}, u32[]{:S(2)}, u32[]{:S(2)}) %collective-permute-start.6) | collective-permute-done | bytes 262176 | tf_op jit(solution)/shard_map/ppermute | solution.py:49
  29.3 1.1 %collective-permute-start.7 = (f32[32,1024]{1,0:T(8,128)S(1)}, f32[32,1024]{1,0:T(8,128)S(1)}, u32[]{:S(2)}, u32[]{:S(2)}) collective-permute-start(f32[32,1024]{1,0:T(8,128)S(1)} %get-tuple-element.31), channel_id=1, source_target_pairs={{0,12},{4,8},{8,4},{12,0},{1,13},{5,9},{9,5},{13,1},{2,14},{6,10},... | collective-permute-start | bytes 393224 | tf_op jit(solution)/shard_map/ppermute | solution.py:49
  30.4 1.4 %split_store.3 = (bf16[384,4096]{1,0:T(8,128)(2,1)S(1)}, bf16[384,4096]{1,0:T(8,128)(2,1)S(1)}) custom-call(f32[640,4096]{1,0:T(8,128)S(1)} %bitcast.3, f32[256,128]{1,0:T(8,128)S(1)} %add.22.after_ref.refs_1_), custom_call_target="tpu_custom_call" | custom-call | flops 1572864000 | tf_op jit(solution)/shard_map/split_store/pallas_call | solution.py:221
  31.7 0.8 %collective-permute-done.4.refs_2_ = f32[256,128]{1,0:T(8,128)S(1)} collective-permute-done((f32[256,128]{1,0:T(8,128)S(1)}, f32[256,128]{1,0:T(8,128)S(1)}, u32[]{:S(2)}, u32[]{:S(2)}) %collective-permute-start.4) | collective-permute-done | bytes 131104 | tf_op jit(solution)/shard_map/ppermute | solution.py:49
  32.5 1.5 %collective-permute-start.11 = (f32[256,128]{1,0:T(8,128)S(1)}, f32[256,128]{1,0:T(8,128)S(1)}, u32[]{:S(2)}, u32[]{:S(2)}) collective-permute-start(f32[256,128]{1,0:T(8,128)S(1)} %collective-permute-done.4.refs_2_), channel_id=1, source_target_pairs={{0,2},{2,0},{1,3},{3,1},{4,6},{6,4},{5,7},{7,5},{8,10},{10,8},{9,1... | collective-permute-start | bytes 393224 | tf_op jit(solution)/shard_map/ppermute | solution.py:49
  34.0 0.9 %collective-permute-done.5.refs_3_ = f32[256,128]{1,0:T(8,128)S(1)} collective-permute-done((f32[256,128]{1,0:T(8,128)S(1)}, f32[256,128]{1,0:T(8,128)S(1)}, u32[]{:S(2)}, u32[]{:S(2)}) %collective-permute-start.5) | collective-permute-done | bytes 131104 | tf_op jit(solution)/shard_map/ppermute | solution.py:49
  34.8 1.5 %collective-permute-start.12 = (f32[256,128]{1,0:T(8,128)S(1)}, f32[256,128]{1,0:T(8,128)S(1)}, u32[]{:S(2)}, u32[]{:S(2)}) collective-permute-start(f32[256,128]{1,0:T(8,128)S(1)} %collective-permute-done.5.refs_3_), channel_id=1, source_target_pairs={{0,2},{2,0},{1,3},{3,1},{4,6},{6,4},{5,7},{7,5},{8,10},{10,8},{9,1... | collective-permute-start | bytes 393224 | tf_op jit(solution)/shard_map/ppermute | solution.py:49
  36.3 0.0 collective-permute-done.7.b_ref
  36.4 1.5 %collective-permute-start.13 = (f32[32,1024]{1,0:T(8,128)S(1)}, f32[32,1024]{1,0:T(8,128)S(1)}, u32[]{:S(2)}, u32[]{:S(2)}) collective-permute-start(f32[32,1024]{1,0:T(8,128)S(1)} %add.24.refs_4_), channel_id=1, source_target_pairs={{0,2},{2,0},{1,3},{3,1},{4,6},{6,4},{5,7},{7,5},{8,10},{10,8},{9,1... | collective-permute-start | bytes 393224 | tf_op jit(solution)/shard_map/ppermute | solution.py:49
  37.9 0.6 outer.2.refs_0_
  38.4 0.0 collective-permute-done.9.refs_0_
  38.5 0.1 collective-permute-start.8
  38.5 0.0 collective-permute-done.10.refs_1_
  38.5 0.3 collective-permute-done.11.refs_2_
  38.8 2.0 %collective-permute-done.12.refs_3_ = f32[256,128]{1,0:T(8,128)S(1)} collective-permute-done((f32[256,128]{1,0:T(8,128)S(1)}, f32[256,128]{1,0:T(8,128)S(1)}, u32[]{:S(2)}, u32[]{:S(2)}) %collective-permute-start.12) | collective-permute-done | bytes 131104 | tf_op jit(solution)/shard_map/ppermute | solution.py:49
  40.8 1.4 %collective-permute-done.13.refs_4_ = f32[32,1024]{1,0:T(8,128)S(1)} collective-permute-done((f32[32,1024]{1,0:T(8,128)S(1)}, f32[32,1024]{1,0:T(8,128)S(1)}, u32[]{:S(2)}, u32[]{:S(2)}) %collective-permute-start.13) | collective-permute-done | bytes 131104 | tf_op jit(solution)/shard_map/ppermute | solution.py:49
  42.2 0.6 outer.3.refs_2_
  42.8 0.1 collective-permute-start.14
  42.9 0.0 collective-permute-done.8.refs_1_
  42.9 1.9 %collective-permute-done.14.refs_3_ = f32[32,32,128]{2,1,0:T(8,128)S(1)} collective-permute-done((f32[32,32,128]{2,1,0:T(8,128)S(1)}, f32[32,32,128]{2,1,0:T(8,128)S(1)}, u32[]{:S(2)}, u32[]{:S(2)}) %collective-permute-start.14) | collective-permute-done | bytes 524320 | tf_op jit(solution)/shard_map/ppermute | solution.py:49
  44.8 3.4 %score.1 = (f32[32,640]{1,0:T(8,128)S(1)}, f32[32,640]{1,0:T(8,128)S(1)}, f32[32,640]{1,0:T(8,128)S(1)}, f32[32,640]{1,0:T(8,128)S(1)}) custom-call(f32[32,32,128]{2,1,0:T(8,128)S(1)} %outer.2.refs_0_, f32[32,32,128]{2,1,0:T(8,128)S(1)} %collective-permute-done.8.refs_1_, f32[32,32,128]{2,1,0:T(8,128)S(1)} %outer.3.refs_2_, ...), custom_call_target="tpu_custom_call" | custom-call | flops 2013265920 | bytes 10485760 | tf_op jit(solution)/shard_map/score/pallas_call | solution.py:261
  48.2 0.1 collective-permute-start.15
  48.3 2.8 %collective-permute-start.16 = (f32[32,640]{1,0:T(8,128)S(1)}, f32[32,640]{1,0:T(8,128)S(1)}, u32[]{:S(2)}, u32[]{:S(2)}) collective-permute-start(f32[32,640]{1,0:T(8,128)S(1)} %get-tuple-element.37), channel_id=1, source_target_pairs={{0,8},{4,12},{8,0},{12,4},{1,9},{5,13},{9,1},{13,5},{2,10},{6,14},... | collective-permute-start | bytes 245768 | tf_op jit(solution)/shard_map/ppermute | solution.py:49
  51.0 1.6 %collective-permute-start.17 = (f32[32,640]{1,0:T(8,128)S(1)}, f32[32,640]{1,0:T(8,128)S(1)}, u32[]{:S(2)}, u32[]{:S(2)}) collective-permute-start(f32[32,640]{1,0:T(8,128)S(1)} %get-tuple-element.38), channel_id=1, source_target_pairs={{0,12},{4,8},{8,4},{12,0},{1,13},{5,9},{9,5},{13,1},{2,14},{6,10},... | collective-permute-start | bytes 245768 | tf_op jit(solution)/shard_map/ppermute | solution.py:49
  52.6 1.2 %collective-permute-done.15 = f32[32,640]{1,0:T(8,128)S(1)} collective-permute-done((f32[32,640]{1,0:T(8,128)S(1)}, f32[32,640]{1,0:T(8,128)S(1)}, u32[]{:S(2)}, u32[]{:S(2)}) %collective-permute-start.15) | collective-permute-done | bytes 81952 | tf_op jit(solution)/shard_map/ppermute | solution.py:49
  53.9 4.2 %collective-permute-done.16 = f32[32,640]{1,0:T(8,128)S(1)} collective-permute-done((f32[32,640]{1,0:T(8,128)S(1)}, f32[32,640]{1,0:T(8,128)S(1)}, u32[]{:S(2)}, u32[]{:S(2)}) %collective-permute-start.16) | collective-permute-done | bytes 81952 | tf_op jit(solution)/shard_map/ppermute | solution.py:49
  58.0 0.0 collective-permute-done.17
  58.0 0.7 %add_add_fusion = f32[32,640]{1,0:T(8,128)} fusion(f32[32,640]{1,0:T(8,128)S(1)} %collective-permute-done.17, f32[32,640]{1,0:T(8,128)S(1)} %collective-permute-done.16, f32[32,640]{1,0:T(8,128)S(1)} %get-tuple-element.35, f32[32,640]{1,0:T(8,128)S(1)} %collective-permute-done.15), kind=kLoop, calls=%fused_computation | loop fusion | flops 61440 | bytes 409600 | tf_op jit(solution)/shard_map/add | solution.py:324
  (17 shorter events, 0.1 us)
Async XLA Ops:
  0.0 2.2 %copy-start = (bf16[32,32,2048]{2,1,0:T(8,128)(2,1)S(1)}, bf16[32,32,2048]{2,1,0:T(8,128)(2,1)}, u32[]{:S(2)}) copy-start(bf16[32,32,2048]{2,1,0:T(8,128)(2,1)} %param.5) | copy-start | bytes 12582916
  2.2 1.0 %copy-start.2 = (bf16[2048,128]{1,0:T(8,128)(2,1)S(1)}, bf16[2048,128]{1,0:T(8,128)(2,1)}, u32[]{:S(2)}) copy-start(bf16[2048,128]{1,0:T(8,128)(2,1)} %in_w_ref.1) | copy-start | bytes 1572868
  3.2 3.5 %copy-start.1 = (bf16[32,32,2048]{2,1,0:T(8,128)(2,1)S(1)}, bf16[32,32,2048]{2,1,0:T(8,128)(2,1)}, u32[]{:S(2)}) copy-start(bf16[32,32,2048]{2,1,0:T(8,128)(2,1)} %param.6) | copy-start | bytes 12582916
  3.2 3.5 %copy-start.3 = (bf16[2048,128]{1,0:T(8,128)(2,1)S(1)}, bf16[2048,128]{1,0:T(8,128)(2,1)}, u32[]{:S(2)}) copy-start(bf16[2048,128]{1,0:T(8,128)(2,1)} %out_w_ref.1) | copy-start | bytes 1572868
  3.7 7.1 %collective-permute-start = (f32[256,128]{1,0:T(8,128)S(1)}, f32[256,128]{1,0:T(8,128)S(1)}, u32[]{:S(2)}, u32[]{:S(2)}) collective-permute-start(f32[256,128]{1,0:T(8,128)S(1)} %project_sent.1.after_ref), channel_id=1, source_target_pairs={{0,4},{4,0},{8,12},{12,8},{1,5},{5,1},{9,13},{13,9},{2,6},{6,2},{1... | collective-permute-start | bytes 393224 | tf_op jit(solution)/shard_map/ppermute | solution.py:49
  6.8 12.8 %slice-start = ((s8[10485760]{0:T(1024)(128)(4,1)}), s8[4194304]{0:T(1024)(128)(4,1)S(1)}, s32[]{:S(2)}) async-start(s8[10485760]{0:T(1024)(128)(4,1)} %bitcast.2), calls=%async_computation | async-start | bytes 8388608
  6.8 12.8 %slice-start.1 = ((s8[10485760]{0:T(1024)(128)(4,1)}), s8[4194304]{0:T(1024)(128)(4,1)S(1)}, s32[]{:S(2)}) async-start(s8[10485760]{0:T(1024)(128)(4,1)} %bitcast.2), calls=%async_computation.1 | async-start | bytes 8388608
  8.9 5.4 %collective-permute-start.2 = (f32[256,128]{1,0:T(8,128)S(1)}, f32[256,128]{1,0:T(8,128)S(1)}, u32[]{:S(2)}, u32[]{:S(2)}) collective-permute-start(f32[256,128]{1,0:T(8,128)S(1)} %get-tuple-element.26), channel_id=1, source_target_pairs={{0,4},{4,0},{8,12},{12,8},{1,5},{5,1},{9,13},{13,9},{2,6},{6,2},{1... | collective-permute-start | bytes 393224 | tf_op jit(solution)/shard_map/ppermute | solution.py:49
  10.8 8.8 %slice-start.2 = ((s8[10485760]{0:T(1024)(128)(4,1)}), s8[2097152]{0:T(1024)(128)(4,1)S(1)}, s32[]{:S(2)}) async-start(s8[10485760]{0:T(1024)(128)(4,1)} %bitcast.2), calls=%async_computation.2 | async-start | bytes 4194304
  10.8 9.8 %collective-permute-start.1 = (f32[256,128]{1,0:T(8,128)S(1)}, f32[256,128]{1,0:T(8,128)S(1)}, u32[]{:S(2)}, u32[]{:S(2)}) collective-permute-start(f32[256,128]{1,0:T(8,128)S(1)} %get-tuple-element.24.a_ref.rest_0_), channel_id=1, source_target_pairs={{0,12},{4,8},{8,4},{12,0},{1,13},{5,9},{9,5},{13,1},{2,14},{6,10},... | collective-permute-start | bytes 393224 | tf_op jit(solution)/shard_map/ppermute | solution.py:49
  14.3 9.8 %collective-permute-start.3 = (f32[256,128]{1,0:T(8,128)S(1)}, f32[256,128]{1,0:T(8,128)S(1)}, u32[]{:S(2)}, u32[]{:S(2)}) collective-permute-start(f32[256,128]{1,0:T(8,128)S(1)} %add.21.a_ref.after_ref), channel_id=1, source_target_pairs={{0,12},{4,8},{8,4},{12,0},{1,13},{5,9},{9,5},{13,1},{2,14},{6,10},... | collective-permute-start | bytes 393224 | tf_op jit(solution)/shard_map/ppermute | solution.py:49
  19.6 9.7 %collective-permute-start.6 = (f32[64,1024]{1,0:T(8,128)S(1)}, f32[64,1024]{1,0:T(8,128)S(1)}, u32[]{:S(2)}, u32[]{:S(2)}) collective-permute-start(f32[64,1024]{1,0:T(8,128)S(1)} %get-tuple-element.28), channel_id=1, source_target_pairs={{0,4},{4,0},{8,12},{12,8},{1,5},{5,1},{9,13},{13,9},{2,6},{6,2},{1... | collective-permute-start | bytes 786440 | tf_op jit(solution)/shard_map/ppermute | solution.py:49
  20.7 17.8 %collective-permute-start.9 = (f32[256,128]{1,0:T(8,128)S(1)}, f32[256,128]{1,0:T(8,128)S(1)}, u32[]{:S(2)}, u32[]{:S(2)}) collective-permute-start(f32[256,128]{1,0:T(8,128)S(1)} %add.20.rest_0_.refs_0_), channel_id=1, source_target_pairs={{0,2},{2,0},{1,3},{3,1},{4,6},{6,4},{5,7},{7,5},{8,10},{10,8},{9,1... | collective-permute-start | bytes 393224 | tf_op jit(solution)/shard_map/ppermute | solution.py:49
  22.2 10.3 %collective-permute-start.4 = (f32[256,128]{1,0:T(8,128)S(1)}, f32[256,128]{1,0:T(8,128)S(1)}, u32[]{:S(2)}, u32[]{:S(2)}) collective-permute-start(f32[256,128]{1,0:T(8,128)S(1)} %add.20.rest_0_.refs_0_), channel_id=1, source_target_pairs={{0,4},{4,0},{8,12},{12,8},{1,5},{5,1},{9,13},{13,9},{2,6},{6,2},{1... | collective-permute-start | bytes 393224 | tf_op jit(solution)/shard_map/ppermute | solution.py:49
  24.1 14.4 %collective-permute-start.10 = (f32[256,128]{1,0:T(8,128)S(1)}, f32[256,128]{1,0:T(8,128)S(1)}, u32[]{:S(2)}, u32[]{:S(2)}) collective-permute-start(f32[256,128]{1,0:T(8,128)S(1)} %add.22.after_ref.refs_1_), channel_id=1, source_target_pairs={{0,2},{2,0},{1,3},{3,1},{4,6},{6,4},{5,7},{7,5},{8,10},{10,8},{9,1... | collective-permute-start | bytes 393224 | tf_op jit(solution)/shard_map/ppermute | solution.py:49
  25.5 9.3 %collective-permute-start.5 = (f32[256,128]{1,0:T(8,128)S(1)}, f32[256,128]{1,0:T(8,128)S(1)}, u32[]{:S(2)}, u32[]{:S(2)}) collective-permute-start(f32[256,128]{1,0:T(8,128)S(1)} %add.22.after_ref.refs_1_), channel_id=1, source_target_pairs={{0,4},{4,0},{8,12},{12,8},{1,5},{5,1},{9,13},{13,9},{2,6},{6,2},{1... | collective-permute-start | bytes 393224 | tf_op jit(solution)/shard_map/ppermute | solution.py:49
  29.3 7.1 %collective-permute-start.7 = (f32[32,1024]{1,0:T(8,128)S(1)}, f32[32,1024]{1,0:T(8,128)S(1)}, u32[]{:S(2)}, u32[]{:S(2)}) collective-permute-start(f32[32,1024]{1,0:T(8,128)S(1)} %get-tuple-element.31), channel_id=1, source_target_pairs={{0,12},{4,8},{8,4},{12,0},{1,13},{5,9},{9,5},{13,1},{2,14},{6,10},... | collective-permute-start | bytes 393224 | tf_op jit(solution)/shard_map/ppermute | solution.py:49
  32.5 6.3 %collective-permute-start.11 = (f32[256,128]{1,0:T(8,128)S(1)}, f32[256,128]{1,0:T(8,128)S(1)}, u32[]{:S(2)}, u32[]{:S(2)}) collective-permute-start(f32[256,128]{1,0:T(8,128)S(1)} %collective-permute-done.4.refs_2_), channel_id=1, source_target_pairs={{0,2},{2,0},{1,3},{3,1},{4,6},{6,4},{5,7},{7,5},{8,10},{10,8},{9,1... | collective-permute-start | bytes 393224 | tf_op jit(solution)/shard_map/ppermute | solution.py:49
  34.8 6.0 %collective-permute-start.12 = (f32[256,128]{1,0:T(8,128)S(1)}, f32[256,128]{1,0:T(8,128)S(1)}, u32[]{:S(2)}, u32[]{:S(2)}) collective-permute-start(f32[256,128]{1,0:T(8,128)S(1)} %collective-permute-done.5.refs_3_), channel_id=1, source_target_pairs={{0,2},{2,0},{1,3},{3,1},{4,6},{6,4},{5,7},{7,5},{8,10},{10,8},{9,1... | collective-permute-start | bytes 393224 | tf_op jit(solution)/shard_map/ppermute | solution.py:49
  36.4 5.9 %collective-permute-start.13 = (f32[32,1024]{1,0:T(8,128)S(1)}, f32[32,1024]{1,0:T(8,128)S(1)}, u32[]{:S(2)}, u32[]{:S(2)}) collective-permute-start(f32[32,1024]{1,0:T(8,128)S(1)} %add.24.refs_4_), channel_id=1, source_target_pairs={{0,2},{2,0},{1,3},{3,1},{4,6},{6,4},{5,7},{7,5},{8,10},{10,8},{9,1... | collective-permute-start | bytes 393224 | tf_op jit(solution)/shard_map/ppermute | solution.py:49
  38.5 4.4 %collective-permute-start.8 = (f32[32,32,128]{2,1,0:T(8,128)S(1)}, f32[32,32,128]{2,1,0:T(8,128)S(1)}, u32[]{:S(2)}, u32[]{:S(2)}) collective-permute-start(f32[32,32,128]{2,1,0:T(8,128)S(1)} %outer.2.refs_0_), channel_id=1, source_target_pairs={{0,1},{1,0},{2,3},{3,2},{4,5},{5,4},{6,7},{7,6},{8,9},{9,8},{10,11... | collective-permute-start | bytes 1572872 | tf_op jit(solution)/shard_map/ppermute | solution.py:49
  42.8 2.0 %collective-permute-start.14 = (f32[32,32,128]{2,1,0:T(8,128)S(1)}, f32[32,32,128]{2,1,0:T(8,128)S(1)}, u32[]{:S(2)}, u32[]{:S(2)}) collective-permute-start(f32[32,32,128]{2,1,0:T(8,128)S(1)} %outer.3.refs_2_), channel_id=1, source_target_pairs={{0,1},{1,0},{2,3},{3,2},{4,5},{5,4},{6,7},{7,6},{8,9},{9,8},{10,11... | collective-permute-start | bytes 1572872 | tf_op jit(solution)/shard_map/ppermute | solution.py:49
  48.2 5.7 %collective-permute-start.15 = (f32[32,640]{1,0:T(8,128)S(1)}, f32[32,640]{1,0:T(8,128)S(1)}, u32[]{:S(2)}, u32[]{:S(2)}) collective-permute-start(f32[32,640]{1,0:T(8,128)S(1)} %get-tuple-element.36), channel_id=1, source_target_pairs={{0,4},{4,0},{8,12},{12,8},{1,5},{5,1},{9,13},{13,9},{2,6},{6,2},{1... | collective-permute-start | bytes 245768 | tf_op jit(solution)/shard_map/ppermute | solution.py:49
  48.3 9.8 %collective-permute-start.16 = (f32[32,640]{1,0:T(8,128)S(1)}, f32[32,640]{1,0:T(8,128)S(1)}, u32[]{:S(2)}, u32[]{:S(2)}) collective-permute-start(f32[32,640]{1,0:T(8,128)S(1)} %get-tuple-element.37), channel_id=1, source_target_pairs={{0,8},{4,12},{8,0},{12,4},{1,9},{5,13},{9,1},{13,5},{2,10},{6,14},... | collective-permute-start | bytes 245768 | tf_op jit(solution)/shard_map/ppermute | solution.py:49
  51.0 7.0 %collective-permute-start.17 = (f32[32,640]{1,0:T(8,128)S(1)}, f32[32,640]{1,0:T(8,128)S(1)}, u32[]{:S(2)}, u32[]{:S(2)}) collective-permute-start(f32[32,640]{1,0:T(8,128)S(1)} %get-tuple-element.38), channel_id=1, source_target_pairs={{0,12},{4,8},{8,4},{12,0},{1,13},{5,9},{9,5},{13,1},{2,14},{6,10},... | collective-permute-start | bytes 245768 | tf_op jit(solution)/shard_map/ppermute | solution.py:49

commit v4 on v3

--- a/solution.py
+++ b/solution.py
@@ -75,49 +75,61 @@
     )(x, w)
 
 
-def rest_kernel(n, tiles, in_x_ref, in_w_ref, out_x_ref, out_w_ref, after_ref, *rest):
+def rest_kernel(x_ref, w_ref, after_ref, send_ref, first_ref, second_ref):
     del after_ref
-    in_send_ref, in_first_ref, in_second_ref, out_keep_ref, out_send_ref, turned = rest
+    half = gray(lax.axis_index("feat")) & 1
+    rows = send_ref.shape[0]
+    for ref, piece in ((send_ref, 2 * (half ^ 1) + 1), (first_ref, 2 * half), (second_ref, 2 * half + 1)):
+        place = pl.ds(pl.multiple_of(piece * rows, rows), rows)
+        ref[...] = jnp.dot(x_ref[place, :], w_ref[...], preferred_element_type=F32)
+
+
+def project_rest(x, w, after):
+    rows, width = x.shape
+    rank = w.shape[1]
+    return pl.pallas_call(
+        rest_kernel,
+        in_specs=[in_vmem()] * 2 + [anywhere()],
+        out_specs=[in_vmem()] * 3,
+        out_shape=[jax.ShapeDtypeStruct((rows // 4, rank), F32)] * 3,
+        compiler_params=params(16),
+        cost_estimate=pl.CostEstimate(flops=rows * width * rank, bytes_accessed=rows * width, transcendentals=0),
+        name="project_rest",
+    )(x, w, after)
+
+
+def out_kernel(n, tiles, x_ref, w_ref, after_ref, keep_ref, send_ref, turned):
+    del after_ref
     bits = n.bit_length() - 1
     here = lax.axis_index("feat")
-    half = gray(here) & 1
-    rows = in_send_ref.shape[0]
-    for ref, piece in (
-        (in_send_ref, 2 * (half ^ 1) + 1),
-        (in_first_ref, 2 * half),
-        (in_second_ref, 2 * half + 1),
-    ):
-        place = pl.ds(pl.multiple_of(piece * rows, rows), rows)
-        ref[...] = jnp.dot(in_x_ref[place, :], in_w_ref[...], preferred_element_type=F32)
-    size = out_x_ref.shape[0] // tiles
+    size = x_ref.shape[0] // tiles
     for t in range(tiles):
         tile = slice(t * size, (t + 1) * size)
-        turned[:, tile] = jnp.dot(out_x_ref[tile, :], out_w_ref[...], preferred_element_type=F32).T
+        turned[:, tile] = jnp.dot(x_ref[tile, :], w_ref[...], preferred_element_type=F32).T
     features = turned.shape[0] // n
     for slot in range(n):
         chunk = here ^ ungray(reversed_bits(slot, bits))
-        ref = out_keep_ref if slot < n // 2 else out_send_ref
+        ref = keep_ref if slot < n // 2 else send_ref
         place = slot % (n // 2) * features
         ref[place : place + features, :] = turned[pl.ds(pl.multiple_of(chunk * features, features), features), :]
 
 
-def project_rest(in_x, in_w, out_x, out_w, after, tiles, n):
-    rows, width = out_x.shape
-    rank = out_w.shape[1]
-    piece = jax.ShapeDtypeStruct((rows // 4, rank), F32)
+def project_out(x, w, after, tiles, n):
+    rows, width = x.shape
+    rank = w.shape[1]
     out = jax.ShapeDtypeStruct((rank // 2, rows), F32)
     return pl.pallas_call(
-        functools.partial(rest_kernel, n, tiles),
-        in_specs=[in_vmem()] * 4 + [anywhere()],
-        out_specs=[in_vmem()] * 5,
-        out_shape=[piece] * 3 + [out] * 2,
+        functools.partial(out_kernel, n, tiles),
+        in_specs=[in_vmem()] * 2 + [anywhere()],
+        out_specs=[in_vmem()] * 2,
+        out_shape=[out] * 2,
         scratch_shapes=[pltpu.VMEM((rank, rows), F32)],
         compiler_params=params(16),
         cost_estimate=pl.CostEstimate(
-            flops=3 * rows * width * rank, bytes_accessed=3 * rows * width, transcendentals=0
+            flops=int(0.5 * 1e9), bytes_accessed=2 * rows * width, transcendentals=0
         ),
-        name="project_rest",
-    )(in_x, in_w, out_x, out_w, after)
+        name="project_out",
+    )(x, w, after)
 
 
 def add_kernel(parts, a_ref, b_ref, *rest):
@@ -158,11 +170,11 @@
     )(a, b, other)
 
 
-def outer_kernel(tokens, group, *refs):
-    in_refs, (out_ref, grad_ref) = refs[:-2], refs[-2:]
+def outer_kernel(tokens, group, part, *refs):
+    in_refs, (out_ref, grad_ref) = refs[:4], (refs[4], refs[-1])
     width = group * tokens
     rows, rank = in_refs[0].shape
-    features = out_ref.shape[0]
+    features = grad_ref.shape[0]
     mine = gray(lax.axis_index("feat")) & 1
     query = lax.broadcasted_iota(jnp.int32, (group, width), 0)
     token = lax.broadcasted_iota(jnp.int32, (group, width), 1)
@@ -171,7 +183,8 @@
         half = mine ^ (k // 2)
         for g in range(rows // width):
             step = half * (2 * rows // width) + (k % 2) * (rows // width) + g
-            columns = out_ref[:, pl.ds(pl.multiple_of(step * width, width), width)]
+            lines = slice(part * features, (part + 1) * features)
+            columns = out_ref[lines, pl.ds(pl.multiple_of(step * width, width), width)]
             spread = (columns[:, None, :] * own[None, :, :]).reshape(features * group, width)
             left, left_low = split(spread)
             right, right_low = split(in_ref[g * width : (g + 1) * width, :])
@@ -182,13 +195,13 @@
             grad_ref[:, place, :] = total.reshape(features, group, rank)
 
 
-def outer(in_pieces, out_columns, tokens, group):
+def outer(in_pieces, out_columns, tokens, group, part, parts, after=()):
     rank = in_pieces[0].shape[1]
-    features, rows = out_columns.shape
+    features, rows = out_columns.shape[0] // parts, out_columns.shape[1]
     out = jax.ShapeDtypeStruct((features, rows // tokens, rank), F32)
     return pl.pallas_call(
-        functools.partial(outer_kernel, tokens, group),
-        in_specs=[in_vmem()] * (len(in_pieces) + 1),
+        functools.partial(outer_kernel, tokens, group, part),
+        in_specs=[in_vmem()] * (len(in_pieces) + 1) + [anywhere()] * len(after),
         out_specs=in_vmem(),
         out_shape=out,
         compiler_params=params(16),
@@ -196,7 +209,7 @@
             flops=6 * rows * group * features * rank, bytes_accessed=8 * rows * rank, transcendentals=0
         ),
         name="outer",
-    )(*in_pieces, out_columns)
+    )(*in_pieces, out_columns, *after)
 
 
 def split_kernel(first, tiles, x_ref, after_ref, high_ref, low_ref, x_buf, sems):
@@ -230,46 +243,68 @@
     )(store, after)
 
 
-def score_kernel(n, sub, count, *refs):
-    store_refs, out_refs, (both, result) = refs[count : -n - 2], refs[-n - 2 : -2], refs[-2:]
-    grad_refs = refs[:count]
+def products(grad_refs, store_refs, both, part):
     features, queries, rank = grad_refs[0].shape
-    total = count * queries
+    total = len(grad_refs) * queries
     for d, ref in enumerate(grad_refs):
         place = d * queries
         for i in range(features):
             high, low = split(ref[i])
             both[place : place + queries, i * rank : (i + 1) * rank] = high
             both[total + place : total + place + queries, i * rank : (i + 1) * rank] = low
+    columns = slice(part * features * rank, (part + 1) * features * rank)
     first = 0
     for high_ref, low_ref in zip(store_refs[::2], store_refs[1::2]):
-        sums = lax.dot_general(both[...], high_ref[...], NT, preferred_element_type=F32)
-        lows = lax.dot_general(both[:total, :], low_ref[...], NT, preferred_element_type=F32)
-        result[:, first : first + high_ref.shape[0]] = sums[:total] + sums[total:] + lows
+        sums = lax.dot_general(both[...], high_ref[:, columns], NT, preferred_element_type=F32)
+        lows = lax.dot_general(both[:total, :], low_ref[:, columns], NT, preferred_element_type=F32)
+        yield slice(first, first + high_ref.shape[0]), sums[:total] + sums[total:] + lows
         first += high_ref.shape[0]
+
+
+def early_kernel(count, part, *refs):
+    store_refs, (result_ref, both) = refs[count:-2], refs[-2:]
+    for place, value in products(refs[:count], store_refs, both, part):
+        result_ref[:, place] = value
+
+
+def score_kernel(n, sub, count, part, *refs):
+    early_refs, refs = refs[:part], refs[part:]
+    store_refs, out_refs, (both, result) = refs[count : -n - 2], refs[-n - 2 : -2], refs[-2:]
+    queries = refs[0].shape[1]
+    for place, value in products(refs[:count], store_refs, both, part):
+        for early_ref in early_refs:
+            value = value + early_ref[:, place]
+        result[:, place] = value
     own = lax.axis_index("feat") ^ (lax.axis_index("rows") * sub + lax.axis_index("sub"))
-    size = queries
     for slot in range(n):
-        out_refs[slot][...] = result[pl.ds(pl.multiple_of((own ^ slot) * size, size), size), :]
-
-
-def score(grads, stored, n, sub):
+        out_refs[slot][...] = result[pl.ds(pl.multiple_of((own ^ slot) * queries, queries), queries), :]
+
+
+def score(grads, stored, n, sub, part, parts, early):
     features, queries, rank = grads[0].shape
-    examples, width = sum(part.shape[0] for part in stored[::2]), stored[0].shape[1]
+    examples, width = sum(block.shape[0] for block in stored[::2]), features * rank
     total = len(grads) * queries
-    out = jax.ShapeDtypeStruct((total // n, examples), F32)
-    return pl.pallas_call(
-        functools.partial(score_kernel, n, sub, len(grads)),
-        in_specs=[in_vmem()] * (len(grads) + len(stored)),
-        out_specs=[in_vmem()] * n,
-        out_shape=[out] * n,
-        scratch_shapes=[pltpu.VMEM((2 * total, width), BF16), pltpu.VMEM((total, examples), F32)],
+    last = part == parts - 1
+    if last:
+        kernel = functools.partial(score_kernel, n, sub, len(grads), part)
+        outs = [jax.ShapeDtypeStruct((total // n, examples), F32)] * n
+        scratch = [pltpu.VMEM((total, examples), F32)]
+    else:
+        kernel = functools.partial(early_kernel, len(grads), part)
+        outs, scratch = [jax.ShapeDtypeStruct((total, examples), F32)], []
+        early = []
+    return pl.pallas_call(
+        kernel,
+        in_specs=[in_vmem()] * (len(early) + len(grads) + len(stored)),
+        out_specs=[in_vmem()] * len(outs),
+        out_shape=outs,
+        scratch_shapes=[pltpu.VMEM((2 * total, width), BF16), *scratch],
         compiler_params=params(24),
         cost_estimate=pl.CostEstimate(
             flops=6 * total * examples * width, bytes_accessed=4 * examples * width, transcendentals=0
         ),
         name="score",
-    )(*grads, *stored)
+    )(*early, *grads, *stored)
 
 
 def tile_count(extent, unit, most):
@@ -286,7 +321,8 @@
 
     in_send = project_sent(acts, proj_in)
     in_recv = exchange(in_send, "feat", n, 1)
-    in_send, *in_keep, out_keep, out_send = project_rest(acts, proj_in, out_grads, proj_out, in_send, 4, n)
+    in_send, *in_keep = project_rest(acts, proj_in, in_send)
+    out_keep, out_send = project_out(out_grads, proj_out, in_send, 4, n)
     piece, out_send = add_beside(in_keep[0], in_recv, out_send, 2)
     pieces = [piece, *add(in_keep[1], exchange(in_send, "feat", n, 1), 1, (piece,), 1)]
     examples = store.shape[0]
@@ -310,18 +346,26 @@
             parts = [exchange(part, "rows", rows, mask) for part in (*block, out)]
             blocks.append((d ^ (mask * sub), parts[:-1], parts[-1]))
         mask *= 2
-    grads = {d: outer(block, out, tokens, 8) for d, block, out in blocks}
-    mask = 1
-    while mask < sub:
-        for d, grad in list(grads.items()):
-            grads[d ^ mask] = exchange(grad, "sub", sub, mask)
-        mask *= 2
-    grads = [grads[d] for d in range(len(grads))]
-    parts = score(grads, stored, n, sub)
-    moved = [exchange(parts[mask], "feat", n, mask) for mask in reversed(range(1, n))]
-    total = parts[0]
-    for part in reversed(moved):
-        total = total + part
+    parts = 2 if out_sum.shape[0] % 16 == 0 else 1
+    grads = [{} for _ in range(parts)]
+    after = ()
+    for d, block, out in blocks:
+        for part in range(parts):
+            grads[part][d] = outer(block, out, tokens, 8, part, parts, after)
+        after = (grads[-1][d],)
+    early = []
+    for part in range(parts):
+        mask = 1
+        while mask < sub:
+            for d, grad in list(grads[part].items()):
+                grads[part][d ^ mask] = exchange(grad, "sub", sub, mask)
+            mask *= 2
+        ordered = [grads[part][d] for d in range(len(grads[part]))]
+        scores = score(ordered, stored, n, sub, part, parts, early)
+        early = early + list(scores)
+    total = scores[0]
+    for mask in reversed(range(1, n)):
+        (total,) = add(total, exchange(scores[mask], "feat", n, mask), 1, (), 1)
     return total
 
 

time: 58.9 us -> 58 us (0.985)
  starting transfers between devices: 30.3 us -> 25.5 us
  waiting for transfers between devices: 14.8 us -> 18 us
  Pallas kernels: 9.52 us -> 10.8 us
  other arithmetic: 0.65 us -> 0.01 us
    ppermute x18 -> x20, starting transfers between devices: 30.3 us -> 25.5 us  [exchange(): return lax.ppermute(x, axis, [(k, k ^ mask) for k in range(count)])]
    ppermute x18 -> x20, waiting for transfers between devices: 14.8 us -> 18 us  [exchange(): return lax.ppermute(x, axis, [(k, k ^ mask) for k in range(count)])]
    pallas_call x5 -> x8, Pallas kernels: 0.09 us -> 0.76 us  [add(): pl.pallas_call(functools.partial(add_kernel, parts), in_specs=[in_vmem()]...]
    add x1 -> x0, other arithmetic: 0.65 us -> none  [local(): total = total + part]
    pallas_call x4 -> x8, Pallas kernels: 6.7 us -> 7.32 us  [the longest x2 3.52 us: score(): pl.pallas_call(kernel, in_specs=[in_vmem()] * (len(early) + len(grads) +...]
  transfers between devices with their start and end apart: 18 -> 20, of which waited for: 11 -> 10; matrix products, arithmetic and copies ran while one was open for 0% -> 0% of each run, Pallas kernels for 10% -> 14%
where the time goes in v4:
time: 58 us; the launch traced here: 57.8 us
  starting transfers between devices  25.5 us (44%)
  waiting for transfers between devices  18 us (31%)
  Pallas kernels  10.8 us (19%)
  local copies, waits for them, and re-layouts  3.26 us (6%)
    ppermute x20, starting transfers between devices, exchange(): return lax.ppermute(x, axis, [(k, k ^ mask) for k in range(count)])  25.5 us
    ppermute x20, waiting for transfers between devices, exchange(): return lax.ppermute(x, axis, [(k, k ^ mask) for k in range(count)])  18 us
    pallas_call x2, Pallas kernels, score(): pl.pallas_call(kernel, in_specs=[in_vmem()] * (len(early) + len(grads) +...  3.52 us
    unnamed x14, local copies, waits for them, and re-layouts  3.26 us
    pallas_call x2, Pallas kernels, split_store(): pl.pallas_call(functools.partial(split_kernel, start, tiles), in_specs=[i...  2.28 us
    pallas_call x4, Pallas kernels, outer(): pl.pallas_call(functools.partial(outer_kernel, tokens, group, part), in_s...  1.5 us
    pallas_call x1, Pallas kernels, project_out(): pl.pallas_call(functools.partial(out_kernel, n, tiles), in_specs=[in_vmem...  1.34 us
  transfers between devices with their start and end apart: 20, of which 10 were waited for; matrix products, arithmetic and copies ran while one was open for 0% of the time, Pallas kernels for 14%

profile of v4, /device:TPU:0, one launch (start us, length us, event | category | flops | bytes accessed | tf_op | source)
XLA Modules:
  0.0 57.8 jit_solution(1564039256286995255)
XLA Ops:
  0.0 2.2 %copy-done = bf16[32,32,2048]{2,1,0:T(8,128)(2,1)S(1)} copy-done((bf16[32,32,2048]{2,1,0:T(8,128)(2,1)S(1)}, bf16[32,32,2048]{2,1,0:T(8,128)(2,1)}, u32[]{:S(2)}) %copy-start) | copy-done | bytes 4194328
  2.2 1.0 %copy-done.2 = bf16[2048,128]{1,0:T(8,128)(2,1)S(1)} copy-done((bf16[2048,128]{1,0:T(8,128)(2,1)S(1)}, bf16[2048,128]{1,0:T(8,128)(2,1)}, u32[]{:S(2)}) %copy-start.2) | copy-done | bytes 524312
  3.2 0.4 project_sent.1.after_ref
  3.7 0.0 copy-start.1
  3.7 0.0 copy-start.3
  3.7 3.1 %collective-permute-start = (f32[256,128]{1,0:T(8,128)S(1)}, f32[256,128]{1,0:T(8,128)S(1)}, u32[]{:S(2)}, u32[]{:S(2)}) collective-permute-start(f32[256,128]{1,0:T(8,128)S(1)} %project_sent.1.after_ref), channel_id=1, source_target_pairs={{0,4},{4,0},{8,12},{12,8},{1,5},{5,1},{9,13},{13,9},{2,6},{6,2},{1... | collective-permute-start | bytes 393224 | tf_op jit(solution)/shard_map/ppermute | solution.py:49
  6.8 1.0 %project_rest.1 = (f32[256,128]{1,0:T(8,128)S(1)}, f32[256,128]{1,0:T(8,128)S(1)}, f32[256,128]{1,0:T(8,128)S(1)}) custom-call(bf16[1024,2048]{1,0:T(8,128)(2,1)S(1)} %bitcast.5, bf16[2048,128]{1,0:T(8,128)(2,1)S(1)} %copy-done.2, f32[256,128]{1,0:T(8,128)S(1)} %project_sent.1.after_ref), custom_call_target="tpu_custom_call" | custom-call | flops 268435456 | bytes 2097152 | tf_op jit(solution)/shard_map/project_rest/pallas_call | solution.py:90
  7.7 0.1 collective-permute-start.2
  7.8 0.0 slice-start.1
  7.9 1.3 %project_out.1 = (f32[64,1024]{1,0:T(8,128)S(1)}, f32[64,1024]{1,0:T(8,128)S(1)}) custom-call(bf16[1024,2048]{1,0:T(8,128)(2,1)S(1)} %bitcast.6, bf16[2048,128]{1,0:T(8,128)(2,1)S(1)} %copy-done.3, f32[256,128]{1,0:T(8,128)S(1)} %get-tuple-element.23.after_ref), custom_call_target="tpu_custom_call" | custom-call | flops 500000000 | bytes 4194304 | tf_op jit(solution)/shard_map/project_out/pallas_call | solution.py:121
  9.2 1.5 %collective-permute-done.b_ref = f32[256,128]{1,0:T(8,128)S(1)} collective-permute-done((f32[256,128]{1,0:T(8,128)S(1)}, f32[256,128]{1,0:T(8,128)S(1)}, u32[]{:S(2)}, u32[]{:S(2)}) %collective-permute-start) | collective-permute-done | bytes 131104 | tf_op jit(solution)/shard_map/ppermute | solution.py:49
  10.7 4.6 %collective-permute-start.1 = (f32[256,128]{1,0:T(8,128)S(1)}, f32[256,128]{1,0:T(8,128)S(1)}, u32[]{:S(2)}, u32[]{:S(2)}) collective-permute-start(f32[256,128]{1,0:T(8,128)S(1)} %get-tuple-element.25.a_ref.rest_0_), channel_id=1, source_target_pairs={{0,12},{4,8},{8,4},{12,0},{1,13},{5,9},{9,5},{13,1},{2,14},{6,10},... | collective-permute-start | bytes 393224 | tf_op jit(solution)/shard_map/ppermute | solution.py:49
  15.3 1.6 %collective-permute-start.3 = (f32[256,128]{1,0:T(8,128)S(1)}, f32[256,128]{1,0:T(8,128)S(1)}, u32[]{:S(2)}, u32[]{:S(2)}) collective-permute-start(f32[256,128]{1,0:T(8,128)S(1)} %add.9.a_ref.after_ref), channel_id=1, source_target_pairs={{0,12},{4,8},{8,4},{12,0},{1,13},{5,9},{9,5},{13,1},{2,14},{6,10},... | collective-permute-start | bytes 393224 | tf_op jit(solution)/shard_map/ppermute | solution.py:49
  16.9 0.5 collective-permute-start.6
  17.5 0.9 %split_store.2 = (bf16[256,4096]{1,0:T(8,128)(2,1)S(1)}, bf16[256,4096]{1,0:T(8,128)(2,1)S(1)}) custom-call(f32[640,4096]{1,0:T(8,128)S(1)} %bitcast.3, f32[256,128]{1,0:T(8,128)S(1)} %add.9.a_ref.after_ref), custom_call_target="tpu_custom_call" | custom-call | flops 1048576000 | tf_op jit(solution)/shard_map/split_store/pallas_call | solution.py:234
  18.4 1.0 %collective-permute-done.1.b_ref = f32[256,128]{1,0:T(8,128)S(1)} collective-permute-done((f32[256,128]{1,0:T(8,128)S(1)}, f32[256,128]{1,0:T(8,128)S(1)}, u32[]{:S(2)}, u32[]{:S(2)}) %collective-permute-start.1) | collective-permute-done | bytes 131104 | tf_op jit(solution)/shard_map/ppermute | solution.py:49
  19.4 4.2 %collective-permute-done.3.b_ref = f32[256,128]{1,0:T(8,128)S(1)} collective-permute-done((f32[256,128]{1,0:T(8,128)S(1)}, f32[256,128]{1,0:T(8,128)S(1)}, u32[]{:S(2)}, u32[]{:S(2)}) %collective-permute-start.3) | collective-permute-done | bytes 131104 | tf_op jit(solution)/shard_map/ppermute | solution.py:49
  23.6 1.6 %collective-permute-start.10 = (f32[256,128]{1,0:T(8,128)S(1)}, f32[256,128]{1,0:T(8,128)S(1)}, u32[]{:S(2)}, u32[]{:S(2)}) collective-permute-start(f32[256,128]{1,0:T(8,128)S(1)} %add.10.after_ref.refs_1_), channel_id=1, source_target_pairs={{0,2},{2,0},{1,3},{3,1},{4,6},{6,4},{5,7},{7,5},{8,10},{10,8},{9,1... | collective-permute-start | bytes 393224 | tf_op jit(solution)/shard_map/ppermute | solution.py:49
  25.2 1.9 %collective-permute-start.5 = (f32[256,128]{1,0:T(8,128)S(1)}, f32[256,128]{1,0:T(8,128)S(1)}, u32[]{:S(2)}, u32[]{:S(2)}) collective-permute-start(f32[256,128]{1,0:T(8,128)S(1)} %add.10.after_ref.refs_1_), channel_id=1, source_target_pairs={{0,4},{4,0},{8,12},{12,8},{1,5},{5,1},{9,13},{13,9},{2,6},{6,2},{1... | collective-permute-start | bytes 393224 | tf_op jit(solution)/shard_map/ppermute | solution.py:49
  27.0 0.5 collective-permute-start.9
  27.6 0.2 collective-permute-start.4
  27.7 0.0 collective-permute-done.6.b_ref
  27.8 2.7 %collective-permute-start.7 = (f32[32,1024]{1,0:T(8,128)S(1)}, f32[32,1024]{1,0:T(8,128)S(1)}, u32[]{:S(2)}, u32[]{:S(2)}) collective-permute-start(f32[32,1024]{1,0:T(8,128)S(1)} %get-tuple-element.31), channel_id=1, source_target_pairs={{0,12},{4,8},{8,4},{12,0},{1,13},{5,9},{9,5},{13,1},{2,14},{6,10},... | collective-permute-start | bytes 393224 | tf_op jit(solution)/shard_map/ppermute | solution.py:49
  30.5 1.4 %split_store.3 = (bf16[384,4096]{1,0:T(8,128)(2,1)S(1)}, bf16[384,4096]{1,0:T(8,128)(2,1)S(1)}) custom-call(f32[640,4096]{1,0:T(8,128)S(1)} %bitcast.3, f32[256,128]{1,0:T(8,128)S(1)} %add.10.after_ref.refs_1_), custom_call_target="tpu_custom_call" | custom-call | flops 1572864000 | tf_op jit(solution)/shard_map/split_store/pallas_call | solution.py:234
  31.8 1.6 %collective-permute-start.12 = (f32[256,128]{1,0:T(8,128)S(1)}, f32[256,128]{1,0:T(8,128)S(1)}, u32[]{:S(2)}, u32[]{:S(2)}) collective-permute-start(f32[256,128]{1,0:T(8,128)S(1)} %collective-permute-done.5.refs_3_), channel_id=1, source_target_pairs={{0,2},{2,0},{1,3},{3,1},{4,6},{6,4},{5,7},{7,5},{8,10},{10,8},{9,1... | collective-permute-start | bytes 393224 | tf_op jit(solution)/shard_map/ppermute | solution.py:49
  33.4 0.5 collective-permute-done.4.refs_2_
  33.9 1.3 %collective-permute-start.11 = (f32[256,128]{1,0:T(8,128)S(1)}, f32[256,128]{1,0:T(8,128)S(1)}, u32[]{:S(2)}, u32[]{:S(2)}) collective-permute-start(f32[256,128]{1,0:T(8,128)S(1)} %collective-permute-done.4.refs_2_), channel_id=1, source_target_pairs={{0,2},{2,0},{1,3},{3,1},{4,6},{6,4},{5,7},{7,5},{8,10},{10,8},{9,1... | collective-permute-start | bytes 393224 | tf_op jit(solution)/shard_map/ppermute | solution.py:49
  35.2 1.4 %collective-permute-done.7.b_ref = f32[32,1024]{1,0:T(8,128)S(1)} collective-permute-done((f32[32,1024]{1,0:T(8,128)S(1)}, f32[32,1024]{1,0:T(8,128)S(1)}, u32[]{:S(2)}, u32[]{:S(2)}) %collective-permute-start.7) | collective-permute-done | bytes 131104 | tf_op jit(solution)/shard_map/ppermute | solution.py:49
  36.7 0.7 %collective-permute-start.13 = (f32[32,1024]{1,0:T(8,128)S(1)}, f32[32,1024]{1,0:T(8,128)S(1)}, u32[]{:S(2)}, u32[]{:S(2)}) collective-permute-start(f32[32,1024]{1,0:T(8,128)S(1)} %add.12.refs_4_), channel_id=1, source_target_pairs={{0,2},{2,0},{1,3},{3,1},{4,6},{6,4},{5,7},{7,5},{8,10},{10,8},{9,1... | collective-permute-start | bytes 393224 | tf_op jit(solution)/shard_map/ppermute | solution.py:49
  37.4 0.4 outer.5.refs_5_.refs_1_
  37.8 0.4 outer.4.refs_0_
  38.2 0.1 collective-permute-start.8
  38.2 0.0 collective-permute-done.9.refs_0_
  38.3 1.5 %collective-permute-done.11.refs_2_ = f32[256,128]{1,0:T(8,128)S(1)} collective-permute-done((f32[256,128]{1,0:T(8,128)S(1)}, f32[256,128]{1,0:T(8,128)S(1)}, u32[]{:S(2)}, u32[]{:S(2)}) %collective-permute-start.11) | collective-permute-done | bytes 131104 | tf_op jit(solution)/shard_map/ppermute | solution.py:49
  39.8 2.0 %collective-permute-done.13.refs_4_ = f32[32,1024]{1,0:T(8,128)S(1)} collective-permute-done((f32[32,1024]{1,0:T(8,128)S(1)}, f32[32,1024]{1,0:T(8,128)S(1)}, u32[]{:S(2)}, u32[]{:S(2)}) %collective-permute-start.13) | collective-permute-done | bytes 131104 | tf_op jit(solution)/shard_map/ppermute | solution.py:49
  41.7 0.4 outer.6.refs_2_
  42.1 0.1 collective-permute-start.14
  42.2 0.5 collective-permute-start.15
  42.7 0.4 outer.7.refs_3_
  43.0 0.1 collective-permute-start.16
  43.2 0.5 collective-permute-done.14.refs_3_
  43.7 1.8 %score.2.refs_0_ = f32[128,640]{1,0:T(8,128)S(1)} custom-call(f32[16,32,128]{2,1,0:T(8,128)S(1)} %outer.4.refs_0_, f32[16,32,128]{2,1,0:T(8,128)S(1)} %collective-permute-done.8.refs_1_, f32[16,32,128]{2,1,0:T(8,128)S(1)} %outer.6.refs_2_, f32[16,32,128]{2,1,0:T(8,128)S(1)} %collective-permute-done.14.refs_3_, ...), custom_call_target="tpu_custom_call" | custom-call | flops 1006632960 | bytes 5242880 | tf_op jit(solution)/shard_map/score/pallas_call | solution.py:296
  45.5 1.8 %score.3 = (f32[32,640]{1,0:T(8,128)S(1)}, f32[32,640]{1,0:T(8,128)S(1)}, f32[32,640]{1,0:T(8,128)S(1)}, f32[32,640]{1,0:T(8,128)S(1)}) custom-call(f32[128,640]{1,0:T(8,128)S(1)} %score.2.refs_0_, f32[16,32,128]{2,1,0:T(8,128)S(1)} %outer.5.refs_5_.refs_1_, f32[16,32,128]{2,1,0:T(8,128)S(1)} %collective-permute-done.15.refs_2_, ...), custom_call_target="tpu_custom_call" | custom-call | flops 1006632960 | bytes 5242880 | tf_op jit(solution)/shard_map/score/pallas_call | solution.py:296
  47.2 2.0 %collective-permute-start.17 = (f32[32,640]{1,0:T(8,128)S(1)}, f32[32,640]{1,0:T(8,128)S(1)}, u32[]{:S(2)}, u32[]{:S(2)}) collective-permute-start(f32[32,640]{1,0:T(8,128)S(1)} %get-tuple-element.36), channel_id=1, source_target_pairs={{0,12},{4,8},{8,4},{12,0},{1,13},{5,9},{9,5},{13,1},{2,14},{6,10},... | collective-permute-start | bytes 245768 | tf_op jit(solution)/shard_map/ppermute | solution.py:49
  49.2 2.5 %collective-permute-start.19 = (f32[32,640]{1,0:T(8,128)S(1)}, f32[32,640]{1,0:T(8,128)S(1)}, u32[]{:S(2)}, u32[]{:S(2)}) collective-permute-start(f32[32,640]{1,0:T(8,128)S(1)} %get-tuple-element.38), channel_id=1, source_target_pairs={{0,4},{4,0},{8,12},{12,8},{1,5},{5,1},{9,13},{13,9},{2,6},{6,2},{1... | collective-permute-start | bytes 245768 | tf_op jit(solution)/shard_map/ppermute | solution.py:49
  51.7 2.8 %collective-permute-done.17.b_ref = f32[32,640]{1,0:T(8,128)S(1)} collective-permute-done((f32[32,640]{1,0:T(8,128)S(1)}, f32[32,640]{1,0:T(8,128)S(1)}, u32[]{:S(2)}, u32[]{:S(2)}) %collective-permute-start.17) | collective-permute-done | bytes 81952 | tf_op jit(solution)/shard_map/ppermute | solution.py:49
  54.5 2.6 %collective-permute-done.18.b_ref = f32[32,640]{1,0:T(8,128)S(1)} collective-permute-done((f32[32,640]{1,0:T(8,128)S(1)}, f32[32,640]{1,0:T(8,128)S(1)}, u32[]{:S(2)}, u32[]{:S(2)}) %collective-permute-start.18) | collective-permute-done | bytes 81952 | tf_op jit(solution)/shard_map/ppermute | solution.py:49
  57.1 0.6 %add.15 = f32[32,640]{1,0:T(8,128)} custom-call(f32[32,640]{1,0:T(8,128)S(1)} %add.14.a_ref, f32[32,640]{1,0:T(8,128)S(1)} %collective-permute-done.19.b_ref), custom_call_target="tpu_custom_call" | custom-call | flops 1000000000 | bytes 245760 | tf_op jit(solution)/shard_map/add/pallas_call | solution.py:145
  (27 shorter events, 0.2 us)
Async XLA Ops:
  0.0 2.2 %copy-start = (bf16[32,32,2048]{2,1,0:T(8,128)(2,1)S(1)}, bf16[32,32,2048]{2,1,0:T(8,128)(2,1)}, u32[]{:S(2)}) copy-start(bf16[32,32,2048]{2,1,0:T(8,128)(2,1)} %param.5) | copy-start | bytes 12582916
  2.2 1.0 %copy-start.2 = (bf16[2048,128]{1,0:T(8,128)(2,1)S(1)}, bf16[2048,128]{1,0:T(8,128)(2,1)}, u32[]{:S(2)}) copy-start(bf16[2048,128]{1,0:T(8,128)(2,1)} %w_ref.4) | copy-start | bytes 1572868
  3.7 4.2 %copy-start.1 = (bf16[32,32,2048]{2,1,0:T(8,128)(2,1)S(1)}, bf16[32,32,2048]{2,1,0:T(8,128)(2,1)}, u32[]{:S(2)}) copy-start(bf16[32,32,2048]{2,1,0:T(8,128)(2,1)} %param.6) | copy-start | bytes 12582916
  3.7 4.2 %copy-start.3 = (bf16[2048,128]{1,0:T(8,128)(2,1)S(1)}, bf16[2048,128]{1,0:T(8,128)(2,1)}, u32[]{:S(2)}) copy-start(bf16[2048,128]{1,0:T(8,128)(2,1)} %w_ref.5) | copy-start | bytes 1572868
  3.7 7.0 %collective-permute-start = (f32[256,128]{1,0:T(8,128)S(1)}, f32[256,128]{1,0:T(8,128)S(1)}, u32[]{:S(2)}, u32[]{:S(2)}) collective-permute-start(f32[256,128]{1,0:T(8,128)S(1)} %project_sent.1.after_ref), channel_id=1, source_target_pairs={{0,4},{4,0},{8,12},{12,8},{1,5},{5,1},{9,13},{13,9},{2,6},{6,2},{1... | collective-permute-start | bytes 393224 | tf_op jit(solution)/shard_map/ppermute | solution.py:49
  6.8 10.7 %slice-start = ((s8[10485760]{0:T(1024)(128)(4,1)}), s8[4194304]{0:T(1024)(128)(4,1)S(1)}, s32[]{:S(2)}) async-start(s8[10485760]{0:T(1024)(128)(4,1)} %bitcast.2), calls=%async_computation | async-start | bytes 8388608
  7.7 7.5 %collective-permute-start.2 = (f32[256,128]{1,0:T(8,128)S(1)}, f32[256,128]{1,0:T(8,128)S(1)}, u32[]{:S(2)}, u32[]{:S(2)}) collective-permute-start(f32[256,128]{1,0:T(8,128)S(1)} %get-tuple-element.23.after_ref), channel_id=1, source_target_pairs={{0,4},{4,0},{8,12},{12,8},{1,5},{5,1},{9,13},{13,9},{2,6},{6,2},{1... | collective-permute-start | bytes 393224 | tf_op jit(solution)/shard_map/ppermute | solution.py:49
  7.8 9.6 %slice-start.1 = ((s8[10485760]{0:T(1024)(128)(4,1)}), s8[4194304]{0:T(1024)(128)(4,1)S(1)}, s32[]{:S(2)}) async-start(s8[10485760]{0:T(1024)(128)(4,1)} %bitcast.2), calls=%async_computation.1 | async-start | bytes 8388608
  10.7 6.8 %slice-start.2 = ((s8[10485760]{0:T(1024)(128)(4,1)}), s8[2097152]{0:T(1024)(128)(4,1)S(1)}, s32[]{:S(2)}) async-start(s8[10485760]{0:T(1024)(128)(4,1)} %bitcast.2), calls=%async_computation.2 | async-start | bytes 4194304
  10.7 8.7 %collective-permute-start.1 = (f32[256,128]{1,0:T(8,128)S(1)}, f32[256,128]{1,0:T(8,128)S(1)}, u32[]{:S(2)}, u32[]{:S(2)}) collective-permute-start(f32[256,128]{1,0:T(8,128)S(1)} %get-tuple-element.25.a_ref.rest_0_), channel_id=1, source_target_pairs={{0,12},{4,8},{8,4},{12,0},{1,13},{5,9},{9,5},{13,1},{2,14},{6,10},... | collective-permute-start | bytes 393224 | tf_op jit(solution)/shard_map/ppermute | solution.py:49
  15.3 8.3 %collective-permute-start.3 = (f32[256,128]{1,0:T(8,128)S(1)}, f32[256,128]{1,0:T(8,128)S(1)}, u32[]{:S(2)}, u32[]{:S(2)}) collective-permute-start(f32[256,128]{1,0:T(8,128)S(1)} %add.9.a_ref.after_ref), channel_id=1, source_target_pairs={{0,12},{4,8},{8,4},{12,0},{1,13},{5,9},{9,5},{13,1},{2,14},{6,10},... | collective-permute-start | bytes 393224 | tf_op jit(solution)/shard_map/ppermute | solution.py:49
  16.9 10.8 %collective-permute-start.6 = (f32[64,1024]{1,0:T(8,128)S(1)}, f32[64,1024]{1,0:T(8,128)S(1)}, u32[]{:S(2)}, u32[]{:S(2)}) collective-permute-start(f32[64,1024]{1,0:T(8,128)S(1)} %get-tuple-element.28), channel_id=1, source_target_pairs={{0,4},{4,0},{8,12},{12,8},{1,5},{5,1},{9,13},{13,9},{2,6},{6,2},{1... | collective-permute-start | bytes 786440 | tf_op jit(solution)/shard_map/ppermute | solution.py:49
  23.6 14.5 %collective-permute-start.10 = (f32[256,128]{1,0:T(8,128)S(1)}, f32[256,128]{1,0:T(8,128)S(1)}, u32[]{:S(2)}, u32[]{:S(2)}) collective-permute-start(f32[256,128]{1,0:T(8,128)S(1)} %add.10.after_ref.refs_1_), channel_id=1, source_target_pairs={{0,2},{2,0},{1,3},{3,1},{4,6},{6,4},{5,7},{7,5},{8,10},{10,8},{9,1... | collective-permute-start | bytes 393224 | tf_op jit(solution)/shard_map/ppermute | solution.py:49
  25.2 6.6 %collective-permute-start.5 = (f32[256,128]{1,0:T(8,128)S(1)}, f32[256,128]{1,0:T(8,128)S(1)}, u32[]{:S(2)}, u32[]{:S(2)}) collective-permute-start(f32[256,128]{1,0:T(8,128)S(1)} %add.10.after_ref.refs_1_), channel_id=1, source_target_pairs={{0,4},{4,0},{8,12},{12,8},{1,5},{5,1},{9,13},{13,9},{2,6},{6,2},{1... | collective-permute-start | bytes 393224 | tf_op jit(solution)/shard_map/ppermute | solution.py:49
  27.0 11.2 %collective-permute-start.9 = (f32[256,128]{1,0:T(8,128)S(1)}, f32[256,128]{1,0:T(8,128)S(1)}, u32[]{:S(2)}, u32[]{:S(2)}) collective-permute-start(f32[256,128]{1,0:T(8,128)S(1)} %add.8.rest_0_.refs_0_), channel_id=1, source_target_pairs={{0,2},{2,0},{1,3},{3,1},{4,6},{6,4},{5,7},{7,5},{8,10},{10,8},{9,1... | collective-permute-start | bytes 393224 | tf_op jit(solution)/shard_map/ppermute | solution.py:49
  27.6 6.3 %collective-permute-start.4 = (f32[256,128]{1,0:T(8,128)S(1)}, f32[256,128]{1,0:T(8,128)S(1)}, u32[]{:S(2)}, u32[]{:S(2)}) collective-permute-start(f32[256,128]{1,0:T(8,128)S(1)} %add.8.rest_0_.refs_0_), channel_id=1, source_target_pairs={{0,4},{4,0},{8,12},{12,8},{1,5},{5,1},{9,13},{13,9},{2,6},{6,2},{1... | collective-permute-start | bytes 393224 | tf_op jit(solution)/shard_map/ppermute | solution.py:49
  27.8 8.9 %collective-permute-start.7 = (f32[32,1024]{1,0:T(8,128)S(1)}, f32[32,1024]{1,0:T(8,128)S(1)}, u32[]{:S(2)}, u32[]{:S(2)}) collective-permute-start(f32[32,1024]{1,0:T(8,128)S(1)} %get-tuple-element.31), channel_id=1, source_target_pairs={{0,12},{4,8},{8,4},{12,0},{1,13},{5,9},{9,5},{13,1},{2,14},{6,10},... | collective-permute-start | bytes 393224 | tf_op jit(solution)/shard_map/ppermute | solution.py:49
  31.8 6.4 %collective-permute-start.12 = (f32[256,128]{1,0:T(8,128)S(1)}, f32[256,128]{1,0:T(8,128)S(1)}, u32[]{:S(2)}, u32[]{:S(2)}) collective-permute-start(f32[256,128]{1,0:T(8,128)S(1)} %collective-permute-done.5.refs_3_), channel_id=1, source_target_pairs={{0,2},{2,0},{1,3},{3,1},{4,6},{6,4},{5,7},{7,5},{8,10},{10,8},{9,1... | collective-permute-start | bytes 393224 | tf_op jit(solution)/shard_map/ppermute | solution.py:49
  33.9 5.9 %collective-permute-start.11 = (f32[256,128]{1,0:T(8,128)S(1)}, f32[256,128]{1,0:T(8,128)S(1)}, u32[]{:S(2)}, u32[]{:S(2)}) collective-permute-start(f32[256,128]{1,0:T(8,128)S(1)} %collective-permute-done.4.refs_2_), channel_id=1, source_target_pairs={{0,2},{2,0},{1,3},{3,1},{4,6},{6,4},{5,7},{7,5},{8,10},{10,8},{9,1... | collective-permute-start | bytes 393224 | tf_op jit(solution)/shard_map/ppermute | solution.py:49
  36.7 5.0 %collective-permute-start.13 = (f32[32,1024]{1,0:T(8,128)S(1)}, f32[32,1024]{1,0:T(8,128)S(1)}, u32[]{:S(2)}, u32[]{:S(2)}) collective-permute-start(f32[32,1024]{1,0:T(8,128)S(1)} %add.12.refs_4_), channel_id=1, source_target_pairs={{0,2},{2,0},{1,3},{3,1},{4,6},{6,4},{5,7},{7,5},{8,10},{10,8},{9,1... | collective-permute-start | bytes 393224 | tf_op jit(solution)/shard_map/ppermute | solution.py:49
  38.2 5.0 %collective-permute-start.8 = (f32[16,32,128]{2,1,0:T(8,128)S(1)}, f32[16,32,128]{2,1,0:T(8,128)S(1)}, u32[]{:S(2)}, u32[]{:S(2)}) collective-permute-start(f32[16,32,128]{2,1,0:T(8,128)S(1)} %outer.4.refs_0_), channel_id=1, source_target_pairs={{0,1},{1,0},{2,3},{3,2},{4,5},{5,4},{6,7},{7,6},{8,9},{9,8},{10,11... | collective-permute-start | bytes 786440 | tf_op jit(solution)/shard_map/ppermute | solution.py:49
  42.1 1.6 %collective-permute-start.14 = (f32[16,32,128]{2,1,0:T(8,128)S(1)}, f32[16,32,128]{2,1,0:T(8,128)S(1)}, u32[]{:S(2)}, u32[]{:S(2)}) collective-permute-start(f32[16,32,128]{2,1,0:T(8,128)S(1)} %outer.6.refs_2_), channel_id=1, source_target_pairs={{0,1},{1,0},{2,3},{3,2},{4,5},{5,4},{6,7},{7,6},{8,9},{9,8},{10,11... | collective-permute-start | bytes 786440 | tf_op jit(solution)/shard_map/ppermute | solution.py:49
  42.2 3.3 %collective-permute-start.15 = (f32[16,32,128]{2,1,0:T(8,128)S(1)}, f32[16,32,128]{2,1,0:T(8,128)S(1)}, u32[]{:S(2)}, u32[]{:S(2)}) collective-permute-start(f32[16,32,128]{2,1,0:T(8,128)S(1)} %outer.5.refs_5_.refs_1_), channel_id=1, source_target_pairs={{0,1},{1,0},{2,3},{3,2},{4,5},{5,4},{6,7},{7,6},{8,9},{9,8},{10,11... | collective-permute-start | bytes 786440 | tf_op jit(solution)/shard_map/ppermute | solution.py:49
  43.0 2.4 %collective-permute-start.16 = (f32[16,32,128]{2,1,0:T(8,128)S(1)}, f32[16,32,128]{2,1,0:T(8,128)S(1)}, u32[]{:S(2)}, u32[]{:S(2)}) collective-permute-start(f32[16,32,128]{2,1,0:T(8,128)S(1)} %outer.7.refs_3_), channel_id=1, source_target_pairs={{0,1},{1,0},{2,3},{3,2},{4,5},{5,4},{6,7},{7,6},{8,9},{9,8},{10,11... | collective-permute-start | bytes 786440 | tf_op jit(solution)/shard_map/ppermute | solution.py:49
  47.2 7.3 %collective-permute-start.17 = (f32[32,640]{1,0:T(8,128)S(1)}, f32[32,640]{1,0:T(8,128)S(1)}, u32[]{:S(2)}, u32[]{:S(2)}) collective-permute-start(f32[32,640]{1,0:T(8,128)S(1)} %get-tuple-element.36), channel_id=1, source_target_pairs={{0,12},{4,8},{8,4},{12,0},{1,13},{5,9},{9,5},{13,1},{2,14},{6,10},... | collective-permute-start | bytes 245768 | tf_op jit(solution)/shard_map/ppermute | solution.py:49
  49.2 7.9 %collective-permute-start.18 = (f32[32,640]{1,0:T(8,128)S(1)}, f32[32,640]{1,0:T(8,128)S(1)}, u32[]{:S(2)}, u32[]{:S(2)}) collective-permute-start(f32[32,640]{1,0:T(8,128)S(1)} %get-tuple-element.37), channel_id=1, source_target_pairs={{0,8},{4,12},{8,0},{12,4},{1,9},{5,13},{9,1},{13,5},{2,10},{6,14},... | collective-permute-start | bytes 245768 | tf_op jit(solution)/shard_map/ppermute | solution.py:49
  49.2 7.9 %collective-permute-start.19 = (f32[32,640]{1,0:T(8,128)S(1)}, f32[32,640]{1,0:T(8,128)S(1)}, u32[]{:S(2)}, u32[]{:S(2)}) collective-permute-start(f32[32,640]{1,0:T(8,128)S(1)} %get-tuple-element.38), channel_id=1, source_target_pairs={{0,4},{4,0},{8,12},{12,8},{1,5},{5,1},{9,13},{13,9},{2,6},{6,2},{1... | collective-permute-start | bytes 245768 | tf_op jit(solution)/shard_map/ppermute | solution.py:49

commit v5 on v4

--- a/solution.py
+++ b/solution.py
@@ -364,7 +364,7 @@
         scores = score(ordered, stored, n, sub, part, parts, early)
         early = early + list(scores)
     total = scores[0]
-    for mask in reversed(range(1, n)):
+    for mask in sorted(range(1, n), key=lambda m: -(m & -m)):
         (total,) = add(total, exchange(scores[mask], "feat", n, mask), 1, (), 1)
     return total
 

time: 58 us -> 56.9 us (0.981)
  waiting for transfers between devices: 18 us -> 16.9 us
    ppermute x20, waiting for transfers between devices: 18 us -> 16.9 us  [exchange(): return lax.ppermute(x, axis, [(k, k ^ mask) for k in range(count)])]
where the time goes in v5:
time: 56.9 us; the launch traced here: 56.7 us
  starting transfers between devices  25.5 us (45%)
  waiting for transfers between devices  16.9 us (30%)
  Pallas kernels  10.8 us (19%)
  local copies, waits for them, and re-layouts  3.26 us (6%)
    ppermute x20, starting transfers between devices, exchange(): return lax.ppermute(x, axis, [(k, k ^ mask) for k in range(count)])  25.5 us
    ppermute x20, waiting for transfers between devices, exchange(): return lax.ppermute(x, axis, [(k, k ^ mask) for k in range(count)])  16.9 us
    pallas_call x2, Pallas kernels, score(): pl.pallas_call(kernel, in_specs=[in_vmem()] * (len(early) + len(grads) +...  3.52 us
    unnamed x14, local copies, waits for them, and re-layouts  3.26 us
    pallas_call x2, Pallas kernels, split_store(): pl.pallas_call(functools.partial(split_kernel, start, tiles), in_specs=[i...  2.28 us
    pallas_call x4, Pallas kernels, outer(): pl.pallas_call(functools.partial(outer_kernel, tokens, group, part), in_s...  1.5 us
    pallas_call x1, Pallas kernels, project_out(): pl.pallas_call(functools.partial(out_kernel, n, tiles), in_specs=[in_vmem...  1.34 us
  transfers between devices with their start and end apart: 20, of which 10 were waited for; matrix products, arithmetic and copies ran while one was open for 0% of the time, Pallas kernels for 14%

profile of v5, /device:TPU:0, one launch (start us, length us, event | category | flops | bytes accessed | tf_op | source)
XLA Modules:
  0.0 56.7 jit_solution(17587760073974993540)
XLA Ops:
  0.0 2.2 %copy-done = bf16[32,32,2048]{2,1,0:T(8,128)(2,1)S(1)} copy-done((bf16[32,32,2048]{2,1,0:T(8,128)(2,1)S(1)}, bf16[32,32,2048]{2,1,0:T(8,128)(2,1)}, u32[]{:S(2)}) %copy-start) | copy-done | bytes 4194328
  2.2 1.0 %copy-done.2 = bf16[2048,128]{1,0:T(8,128)(2,1)S(1)} copy-done((bf16[2048,128]{1,0:T(8,128)(2,1)S(1)}, bf16[2048,128]{1,0:T(8,128)(2,1)}, u32[]{:S(2)}) %copy-start.2) | copy-done | bytes 524312
  3.2 0.4 project_sent.1.after_ref
  3.7 0.0 copy-start.1
  3.7 0.0 copy-start.3
  3.7 3.1 %collective-permute-start = (f32[256,128]{1,0:T(8,128)S(1)}, f32[256,128]{1,0:T(8,128)S(1)}, u32[]{:S(2)}, u32[]{:S(2)}) collective-permute-start(f32[256,128]{1,0:T(8,128)S(1)} %project_sent.1.after_ref), channel_id=1, source_target_pairs={{0,4},{4,0},{8,12},{12,8},{1,5},{5,1},{9,13},{13,9},{2,6},{6,2},{1... | collective-permute-start | bytes 393224 | tf_op jit(solution)/shard_map/ppermute | solution.py:49
  6.8 1.0 %project_rest.1 = (f32[256,128]{1,0:T(8,128)S(1)}, f32[256,128]{1,0:T(8,128)S(1)}, f32[256,128]{1,0:T(8,128)S(1)}) custom-call(bf16[1024,2048]{1,0:T(8,128)(2,1)S(1)} %bitcast.5, bf16[2048,128]{1,0:T(8,128)(2,1)S(1)} %copy-done.2, f32[256,128]{1,0:T(8,128)S(1)} %project_sent.1.after_ref), custom_call_target="tpu_custom_call" | custom-call | flops 268435456 | bytes 2097152 | tf_op jit(solution)/shard_map/project_rest/pallas_call | solution.py:90
  7.7 0.1 collective-permute-start.2
  7.8 0.0 slice-start.1
  7.9 1.3 %project_out.1 = (f32[64,1024]{1,0:T(8,128)S(1)}, f32[64,1024]{1,0:T(8,128)S(1)}) custom-call(bf16[1024,2048]{1,0:T(8,128)(2,1)S(1)} %bitcast.6, bf16[2048,128]{1,0:T(8,128)(2,1)S(1)} %copy-done.3, f32[256,128]{1,0:T(8,128)S(1)} %get-tuple-element.23.after_ref), custom_call_target="tpu_custom_call" | custom-call | flops 500000000 | bytes 4194304 | tf_op jit(solution)/shard_map/project_out/pallas_call | solution.py:121
  9.2 1.5 %collective-permute-done.b_ref = f32[256,128]{1,0:T(8,128)S(1)} collective-permute-done((f32[256,128]{1,0:T(8,128)S(1)}, f32[256,128]{1,0:T(8,128)S(1)}, u32[]{:S(2)}, u32[]{:S(2)}) %collective-permute-start) | collective-permute-done | bytes 131104 | tf_op jit(solution)/shard_map/ppermute | solution.py:49
  10.7 4.6 %collective-permute-start.1 = (f32[256,128]{1,0:T(8,128)S(1)}, f32[256,128]{1,0:T(8,128)S(1)}, u32[]{:S(2)}, u32[]{:S(2)}) collective-permute-start(f32[256,128]{1,0:T(8,128)S(1)} %get-tuple-element.25.a_ref.rest_0_), channel_id=1, source_target_pairs={{0,12},{4,8},{8,4},{12,0},{1,13},{5,9},{9,5},{13,1},{2,14},{6,10},... | collective-permute-start | bytes 393224 | tf_op jit(solution)/shard_map/ppermute | solution.py:49
  15.3 0.0 collective-permute-done.2.b_ref
  15.3 1.6 %collective-permute-start.3 = (f32[256,128]{1,0:T(8,128)S(1)}, f32[256,128]{1,0:T(8,128)S(1)}, u32[]{:S(2)}, u32[]{:S(2)}) collective-permute-start(f32[256,128]{1,0:T(8,128)S(1)} %add.9.a_ref.after_ref), channel_id=1, source_target_pairs={{0,12},{4,8},{8,4},{12,0},{1,13},{5,9},{9,5},{13,1},{2,14},{6,10},... | collective-permute-start | bytes 393224 | tf_op jit(solution)/shard_map/ppermute | solution.py:49
  16.9 0.5 collective-permute-start.6
  17.5 0.9 %split_store.2 = (bf16[256,4096]{1,0:T(8,128)(2,1)S(1)}, bf16[256,4096]{1,0:T(8,128)(2,1)S(1)}) custom-call(f32[640,4096]{1,0:T(8,128)S(1)} %bitcast.3, f32[256,128]{1,0:T(8,128)S(1)} %add.9.a_ref.after_ref), custom_call_target="tpu_custom_call" | custom-call | flops 1048576000 | tf_op jit(solution)/shard_map/split_store/pallas_call | solution.py:234
  18.4 1.0 %collective-permute-done.1.b_ref = f32[256,128]{1,0:T(8,128)S(1)} collective-permute-done((f32[256,128]{1,0:T(8,128)S(1)}, f32[256,128]{1,0:T(8,128)S(1)}, u32[]{:S(2)}, u32[]{:S(2)}) %collective-permute-start.1) | collective-permute-done | bytes 131104 | tf_op jit(solution)/shard_map/ppermute | solution.py:49
  19.4 4.2 %collective-permute-done.3.b_ref = f32[256,128]{1,0:T(8,128)S(1)} collective-permute-done((f32[256,128]{1,0:T(8,128)S(1)}, f32[256,128]{1,0:T(8,128)S(1)}, u32[]{:S(2)}, u32[]{:S(2)}) %collective-permute-start.3) | collective-permute-done | bytes 131104 | tf_op jit(solution)/shard_map/ppermute | solution.py:49
  23.6 1.6 %collective-permute-start.10 = (f32[256,128]{1,0:T(8,128)S(1)}, f32[256,128]{1,0:T(8,128)S(1)}, u32[]{:S(2)}, u32[]{:S(2)}) collective-permute-start(f32[256,128]{1,0:T(8,128)S(1)} %add.10.after_ref.refs_1_), channel_id=1, source_target_pairs={{0,2},{2,0},{1,3},{3,1},{4,6},{6,4},{5,7},{7,5},{8,10},{10,8},{9,1... | collective-permute-start | bytes 393224 | tf_op jit(solution)/shard_map/ppermute | solution.py:49
  25.2 1.9 %collective-permute-start.5 = (f32[256,128]{1,0:T(8,128)S(1)}, f32[256,128]{1,0:T(8,128)S(1)}, u32[]{:S(2)}, u32[]{:S(2)}) collective-permute-start(f32[256,128]{1,0:T(8,128)S(1)} %add.10.after_ref.refs_1_), channel_id=1, source_target_pairs={{0,4},{4,0},{8,12},{12,8},{1,5},{5,1},{9,13},{13,9},{2,6},{6,2},{1... | collective-permute-start | bytes 393224 | tf_op jit(solution)/shard_map/ppermute | solution.py:49
  27.0 0.5 collective-permute-start.9
  27.6 0.2 collective-permute-start.4
  27.8 2.7 %collective-permute-start.7 = (f32[32,1024]{1,0:T(8,128)S(1)}, f32[32,1024]{1,0:T(8,128)S(1)}, u32[]{:S(2)}, u32[]{:S(2)}) collective-permute-start(f32[32,1024]{1,0:T(8,128)S(1)} %get-tuple-element.31), channel_id=1, source_target_pairs={{0,12},{4,8},{8,4},{12,0},{1,13},{5,9},{9,5},{13,1},{2,14},{6,10},... | collective-permute-start | bytes 393224 | tf_op jit(solution)/shard_map/ppermute | solution.py:49
  30.5 1.4 %split_store.3 = (bf16[384,4096]{1,0:T(8,128)(2,1)S(1)}, bf16[384,4096]{1,0:T(8,128)(2,1)S(1)}) custom-call(f32[640,4096]{1,0:T(8,128)S(1)} %bitcast.3, f32[256,128]{1,0:T(8,128)S(1)} %add.10.after_ref.refs_1_), custom_call_target="tpu_custom_call" | custom-call | flops 1572864000 | tf_op jit(solution)/shard_map/split_store/pallas_call | solution.py:234
  31.8 1.6 %collective-permute-start.12 = (f32[256,128]{1,0:T(8,128)S(1)}, f32[256,128]{1,0:T(8,128)S(1)}, u32[]{:S(2)}, u32[]{:S(2)}) collective-permute-start(f32[256,128]{1,0:T(8,128)S(1)} %collective-permute-done.5.refs_3_), channel_id=1, source_target_pairs={{0,2},{2,0},{1,3},{3,1},{4,6},{6,4},{5,7},{7,5},{8,10},{10,8},{9,1... | collective-permute-start | bytes 393224 | tf_op jit(solution)/shard_map/ppermute | solution.py:49
  33.4 0.5 collective-permute-done.4.refs_2_
  33.9 1.3 %collective-permute-start.11 = (f32[256,128]{1,0:T(8,128)S(1)}, f32[256,128]{1,0:T(8,128)S(1)}, u32[]{:S(2)}, u32[]{:S(2)}) collective-permute-start(f32[256,128]{1,0:T(8,128)S(1)} %collective-permute-done.4.refs_2_), channel_id=1, source_target_pairs={{0,2},{2,0},{1,3},{3,1},{4,6},{6,4},{5,7},{7,5},{8,10},{10,8},{9,1... | collective-permute-start | bytes 393224 | tf_op jit(solution)/shard_map/ppermute | solution.py:49
  35.2 1.4 %collective-permute-done.7.b_ref = f32[32,1024]{1,0:T(8,128)S(1)} collective-permute-done((f32[32,1024]{1,0:T(8,128)S(1)}, f32[32,1024]{1,0:T(8,128)S(1)}, u32[]{:S(2)}, u32[]{:S(2)}) %collective-permute-start.7) | collective-permute-done | bytes 131104 | tf_op jit(solution)/shard_map/ppermute | solution.py:49
  36.7 0.7 %collective-permute-start.13 = (f32[32,1024]{1,0:T(8,128)S(1)}, f32[32,1024]{1,0:T(8,128)S(1)}, u32[]{:S(2)}, u32[]{:S(2)}) collective-permute-start(f32[32,1024]{1,0:T(8,128)S(1)} %add.12.refs_4_), channel_id=1, source_target_pairs={{0,2},{2,0},{1,3},{3,1},{4,6},{6,4},{5,7},{7,5},{8,10},{10,8},{9,1... | collective-permute-start | bytes 393224 | tf_op jit(solution)/shard_map/ppermute | solution.py:49
  37.4 0.4 outer.5.refs_5_.refs_1_
  37.8 0.4 outer.4.refs_0_
  38.2 0.1 collective-permute-start.8
  38.3 1.5 %collective-permute-done.11.refs_2_ = f32[256,128]{1,0:T(8,128)S(1)} collective-permute-done((f32[256,128]{1,0:T(8,128)S(1)}, f32[256,128]{1,0:T(8,128)S(1)}, u32[]{:S(2)}, u32[]{:S(2)}) %collective-permute-start.11) | collective-permute-done | bytes 131104 | tf_op jit(solution)/shard_map/ppermute | solution.py:49
  39.8 2.0 %collective-permute-done.13.refs_4_ = f32[32,1024]{1,0:T(8,128)S(1)} collective-permute-done((f32[32,1024]{1,0:T(8,128)S(1)}, f32[32,1024]{1,0:T(8,128)S(1)}, u32[]{:S(2)}, u32[]{:S(2)}) %collective-permute-start.13) | collective-permute-done | bytes 131104 | tf_op jit(solution)/shard_map/ppermute | solution.py:49
  41.7 0.4 outer.6.refs_2_
  42.1 0.1 collective-permute-start.14
  42.2 0.5 collective-permute-start.15
  42.7 0.4 outer.7.refs_3_
  43.0 0.1 collective-permute-start.16
  43.2 0.5 collective-permute-done.14.refs_3_
  43.7 1.8 %score.2.refs_0_ = f32[128,640]{1,0:T(8,128)S(1)} custom-call(f32[16,32,128]{2,1,0:T(8,128)S(1)} %outer.4.refs_0_, f32[16,32,128]{2,1,0:T(8,128)S(1)} %collective-permute-done.8.refs_1_, f32[16,32,128]{2,1,0:T(8,128)S(1)} %outer.6.refs_2_, f32[16,32,128]{2,1,0:T(8,128)S(1)} %collective-permute-done.14.refs_3_, ...), custom_call_target="tpu_custom_call" | custom-call | flops 1006632960 | bytes 5242880 | tf_op jit(solution)/shard_map/score/pallas_call | solution.py:296
  45.5 1.8 %score.3 = (f32[32,640]{1,0:T(8,128)S(1)}, f32[32,640]{1,0:T(8,128)S(1)}, f32[32,640]{1,0:T(8,128)S(1)}, f32[32,640]{1,0:T(8,128)S(1)}) custom-call(f32[128,640]{1,0:T(8,128)S(1)} %score.2.refs_0_, f32[16,32,128]{2,1,0:T(8,128)S(1)} %outer.5.refs_5_.refs_1_, f32[16,32,128]{2,1,0:T(8,128)S(1)} %collective-permute-done.15.refs_2_, ...), custom_call_target="tpu_custom_call" | custom-call | flops 1006632960 | bytes 5242880 | tf_op jit(solution)/shard_map/score/pallas_call | solution.py:296
  47.2 0.8 %collective-permute-start.17 = (f32[32,640]{1,0:T(8,128)S(1)}, f32[32,640]{1,0:T(8,128)S(1)}, u32[]{:S(2)}, u32[]{:S(2)}) collective-permute-start(f32[32,640]{1,0:T(8,128)S(1)} %get-tuple-element.36), channel_id=1, source_target_pairs={{0,8},{4,12},{8,0},{12,4},{1,9},{5,13},{9,1},{13,5},{2,10},{6,14},... | collective-permute-start | bytes 245768 | tf_op jit(solution)/shard_map/ppermute | solution.py:49
  48.1 1.8 %collective-permute-start.18 = (f32[32,640]{1,0:T(8,128)S(1)}, f32[32,640]{1,0:T(8,128)S(1)}, u32[]{:S(2)}, u32[]{:S(2)}) collective-permute-start(f32[32,640]{1,0:T(8,128)S(1)} %get-tuple-element.37), channel_id=1, source_target_pairs={{0,4},{4,0},{8,12},{12,8},{1,5},{5,1},{9,13},{13,9},{2,6},{6,2},{1... | collective-permute-start | bytes 245768 | tf_op jit(solution)/shard_map/ppermute | solution.py:49
  49.8 1.9 %collective-permute-start.19 = (f32[32,640]{1,0:T(8,128)S(1)}, f32[32,640]{1,0:T(8,128)S(1)}, u32[]{:S(2)}, u32[]{:S(2)}) collective-permute-start(f32[32,640]{1,0:T(8,128)S(1)} %get-tuple-element.38), channel_id=1, source_target_pairs={{0,12},{4,8},{8,4},{12,0},{1,13},{5,9},{9,5},{13,1},{2,14},{6,10},... | collective-permute-start | bytes 245768 | tf_op jit(solution)/shard_map/ppermute | solution.py:49
  51.7 3.4 %collective-permute-done.17.b_ref = f32[32,640]{1,0:T(8,128)S(1)} collective-permute-done((f32[32,640]{1,0:T(8,128)S(1)}, f32[32,640]{1,0:T(8,128)S(1)}, u32[]{:S(2)}, u32[]{:S(2)}) %collective-permute-start.17) | collective-permute-done | bytes 81952 | tf_op jit(solution)/shard_map/ppermute | solution.py:49
  55.1 1.0 %collective-permute-done.19.b_ref = f32[32,640]{1,0:T(8,128)S(1)} collective-permute-done((f32[32,640]{1,0:T(8,128)S(1)}, f32[32,640]{1,0:T(8,128)S(1)}, u32[]{:S(2)}, u32[]{:S(2)}) %collective-permute-start.19) | collective-permute-done | bytes 81952 | tf_op jit(solution)/shard_map/ppermute | solution.py:49
  56.1 0.6 %add.15 = f32[32,640]{1,0:T(8,128)} custom-call(f32[32,640]{1,0:T(8,128)S(1)} %add.14.a_ref, f32[32,640]{1,0:T(8,128)S(1)} %collective-permute-done.19.b_ref), custom_call_target="tpu_custom_call" | custom-call | flops 1000000000 | bytes 245760 | tf_op jit(solution)/shard_map/add/pallas_call | solution.py:145
  (27 shorter events, 0.2 us)
Async XLA Ops:
  0.0 2.2 %copy-start = (bf16[32,32,2048]{2,1,0:T(8,128)(2,1)S(1)}, bf16[32,32,2048]{2,1,0:T(8,128)(2,1)}, u32[]{:S(2)}) copy-start(bf16[32,32,2048]{2,1,0:T(8,128)(2,1)} %param.5) | copy-start | bytes 12582916
  2.2 1.0 %copy-start.2 = (bf16[2048,128]{1,0:T(8,128)(2,1)S(1)}, bf16[2048,128]{1,0:T(8,128)(2,1)}, u32[]{:S(2)}) copy-start(bf16[2048,128]{1,0:T(8,128)(2,1)} %w_ref.4) | copy-start | bytes 1572868
  3.7 4.2 %copy-start.1 = (bf16[32,32,2048]{2,1,0:T(8,128)(2,1)S(1)}, bf16[32,32,2048]{2,1,0:T(8,128)(2,1)}, u32[]{:S(2)}) copy-start(bf16[32,32,2048]{2,1,0:T(8,128)(2,1)} %param.6) | copy-start | bytes 12582916
  3.7 4.2 %copy-start.3 = (bf16[2048,128]{1,0:T(8,128)(2,1)S(1)}, bf16[2048,128]{1,0:T(8,128)(2,1)}, u32[]{:S(2)}) copy-start(bf16[2048,128]{1,0:T(8,128)(2,1)} %w_ref.5) | copy-start | bytes 1572868
  3.7 7.0 %collective-permute-start = (f32[256,128]{1,0:T(8,128)S(1)}, f32[256,128]{1,0:T(8,128)S(1)}, u32[]{:S(2)}, u32[]{:S(2)}) collective-permute-start(f32[256,128]{1,0:T(8,128)S(1)} %project_sent.1.after_ref), channel_id=1, source_target_pairs={{0,4},{4,0},{8,12},{12,8},{1,5},{5,1},{9,13},{13,9},{2,6},{6,2},{1... | collective-permute-start | bytes 393224 | tf_op jit(solution)/shard_map/ppermute | solution.py:49
  6.8 10.7 %slice-start = ((s8[10485760]{0:T(1024)(128)(4,1)}), s8[4194304]{0:T(1024)(128)(4,1)S(1)}, s32[]{:S(2)}) async-start(s8[10485760]{0:T(1024)(128)(4,1)} %bitcast.2), calls=%async_computation | async-start | bytes 8388608
  7.7 7.5 %collective-permute-start.2 = (f32[256,128]{1,0:T(8,128)S(1)}, f32[256,128]{1,0:T(8,128)S(1)}, u32[]{:S(2)}, u32[]{:S(2)}) collective-permute-start(f32[256,128]{1,0:T(8,128)S(1)} %get-tuple-element.23.after_ref), channel_id=1, source_target_pairs={{0,4},{4,0},{8,12},{12,8},{1,5},{5,1},{9,13},{13,9},{2,6},{6,2},{1... | collective-permute-start | bytes 393224 | tf_op jit(solution)/shard_map/ppermute | solution.py:49
  7.8 9.6 %slice-start.1 = ((s8[10485760]{0:T(1024)(128)(4,1)}), s8[4194304]{0:T(1024)(128)(4,1)S(1)}, s32[]{:S(2)}) async-start(s8[10485760]{0:T(1024)(128)(4,1)} %bitcast.2), calls=%async_computation.1 | async-start | bytes 8388608
  10.7 6.8 %slice-start.2 = ((s8[10485760]{0:T(1024)(128)(4,1)}), s8[2097152]{0:T(1024)(128)(4,1)S(1)}, s32[]{:S(2)}) async-start(s8[10485760]{0:T(1024)(128)(4,1)} %bitcast.2), calls=%async_computation.2 | async-start | bytes 4194304
  10.7 8.7 %collective-permute-start.1 = (f32[256,128]{1,0:T(8,128)S(1)}, f32[256,128]{1,0:T(8,128)S(1)}, u32[]{:S(2)}, u32[]{:S(2)}) collective-permute-start(f32[256,128]{1,0:T(8,128)S(1)} %get-tuple-element.25.a_ref.rest_0_), channel_id=1, source_target_pairs={{0,12},{4,8},{8,4},{12,0},{1,13},{5,9},{9,5},{13,1},{2,14},{6,10},... | collective-permute-start | bytes 393224 | tf_op jit(solution)/shard_map/ppermute | solution.py:49
  15.3 8.3 %collective-permute-start.3 = (f32[256,128]{1,0:T(8,128)S(1)}, f32[256,128]{1,0:T(8,128)S(1)}, u32[]{:S(2)}, u32[]{:S(2)}) collective-permute-start(f32[256,128]{1,0:T(8,128)S(1)} %add.9.a_ref.after_ref), channel_id=1, source_target_pairs={{0,12},{4,8},{8,4},{12,0},{1,13},{5,9},{9,5},{13,1},{2,14},{6,10},... | collective-permute-start | bytes 393224 | tf_op jit(solution)/shard_map/ppermute | solution.py:49
  16.9 10.8 %collective-permute-start.6 = (f32[64,1024]{1,0:T(8,128)S(1)}, f32[64,1024]{1,0:T(8,128)S(1)}, u32[]{:S(2)}, u32[]{:S(2)}) collective-permute-start(f32[64,1024]{1,0:T(8,128)S(1)} %get-tuple-element.28), channel_id=1, source_target_pairs={{0,4},{4,0},{8,12},{12,8},{1,5},{5,1},{9,13},{13,9},{2,6},{6,2},{1... | collective-permute-start | bytes 786440 | tf_op jit(solution)/shard_map/ppermute | solution.py:49
  23.6 14.5 %collective-permute-start.10 = (f32[256,128]{1,0:T(8,128)S(1)}, f32[256,128]{1,0:T(8,128)S(1)}, u32[]{:S(2)}, u32[]{:S(2)}) collective-permute-start(f32[256,128]{1,0:T(8,128)S(1)} %add.10.after_ref.refs_1_), channel_id=1, source_target_pairs={{0,2},{2,0},{1,3},{3,1},{4,6},{6,4},{5,7},{7,5},{8,10},{10,8},{9,1... | collective-permute-start | bytes 393224 | tf_op jit(solution)/shard_map/ppermute | solution.py:49
  25.2 6.6 %collective-permute-start.5 = (f32[256,128]{1,0:T(8,128)S(1)}, f32[256,128]{1,0:T(8,128)S(1)}, u32[]{:S(2)}, u32[]{:S(2)}) collective-permute-start(f32[256,128]{1,0:T(8,128)S(1)} %add.10.after_ref.refs_1_), channel_id=1, source_target_pairs={{0,4},{4,0},{8,12},{12,8},{1,5},{5,1},{9,13},{13,9},{2,6},{6,2},{1... | collective-permute-start | bytes 393224 | tf_op jit(solution)/shard_map/ppermute | solution.py:49
  27.0 11.2 %collective-permute-start.9 = (f32[256,128]{1,0:T(8,128)S(1)}, f32[256,128]{1,0:T(8,128)S(1)}, u32[]{:S(2)}, u32[]{:S(2)}) collective-permute-start(f32[256,128]{1,0:T(8,128)S(1)} %add.8.rest_0_.refs_0_), channel_id=1, source_target_pairs={{0,2},{2,0},{1,3},{3,1},{4,6},{6,4},{5,7},{7,5},{8,10},{10,8},{9,1... | collective-permute-start | bytes 393224 | tf_op jit(solution)/shard_map/ppermute | solution.py:49
  27.6 6.3 %collective-permute-start.4 = (f32[256,128]{1,0:T(8,128)S(1)}, f32[256,128]{1,0:T(8,128)S(1)}, u32[]{:S(2)}, u32[]{:S(2)}) collective-permute-start(f32[256,128]{1,0:T(8,128)S(1)} %add.8.rest_0_.refs_0_), channel_id=1, source_target_pairs={{0,4},{4,0},{8,12},{12,8},{1,5},{5,1},{9,13},{13,9},{2,6},{6,2},{1... | collective-permute-start | bytes 393224 | tf_op jit(solution)/shard_map/ppermute | solution.py:49
  27.8 8.9 %collective-permute-start.7 = (f32[32,1024]{1,0:T(8,128)S(1)}, f32[32,1024]{1,0:T(8,128)S(1)}, u32[]{:S(2)}, u32[]{:S(2)}) collective-permute-start(f32[32,1024]{1,0:T(8,128)S(1)} %get-tuple-element.31), channel_id=1, source_target_pairs={{0,12},{4,8},{8,4},{12,0},{1,13},{5,9},{9,5},{13,1},{2,14},{6,10},... | collective-permute-start | bytes 393224 | tf_op jit(solution)/shard_map/ppermute | solution.py:49
  31.8 6.4 %collective-permute-start.12 = (f32[256,128]{1,0:T(8,128)S(1)}, f32[256,128]{1,0:T(8,128)S(1)}, u32[]{:S(2)}, u32[]{:S(2)}) collective-permute-start(f32[256,128]{1,0:T(8,128)S(1)} %collective-permute-done.5.refs_3_), channel_id=1, source_target_pairs={{0,2},{2,0},{1,3},{3,1},{4,6},{6,4},{5,7},{7,5},{8,10},{10,8},{9,1... | collective-permute-start | bytes 393224 | tf_op jit(solution)/shard_map/ppermute | solution.py:49
  33.9 5.9 %collective-permute-start.11 = (f32[256,128]{1,0:T(8,128)S(1)}, f32[256,128]{1,0:T(8,128)S(1)}, u32[]{:S(2)}, u32[]{:S(2)}) collective-permute-start(f32[256,128]{1,0:T(8,128)S(1)} %collective-permute-done.4.refs_2_), channel_id=1, source_target_pairs={{0,2},{2,0},{1,3},{3,1},{4,6},{6,4},{5,7},{7,5},{8,10},{10,8},{9,1... | collective-permute-start | bytes 393224 | tf_op jit(solution)/shard_map/ppermute | solution.py:49
  36.7 5.0 %collective-permute-start.13 = (f32[32,1024]{1,0:T(8,128)S(1)}, f32[32,1024]{1,0:T(8,128)S(1)}, u32[]{:S(2)}, u32[]{:S(2)}) collective-permute-start(f32[32,1024]{1,0:T(8,128)S(1)} %add.12.refs_4_), channel_id=1, source_target_pairs={{0,2},{2,0},{1,3},{3,1},{4,6},{6,4},{5,7},{7,5},{8,10},{10,8},{9,1... | collective-permute-start | bytes 393224 | tf_op jit(solution)/shard_map/ppermute | solution.py:49
  38.2 5.0 %collective-permute-start.8 = (f32[16,32,128]{2,1,0:T(8,128)S(1)}, f32[16,32,128]{2,1,0:T(8,128)S(1)}, u32[]{:S(2)}, u32[]{:S(2)}) collective-permute-start(f32[16,32,128]{2,1,0:T(8,128)S(1)} %outer.4.refs_0_), channel_id=1, source_target_pairs={{0,1},{1,0},{2,3},{3,2},{4,5},{5,4},{6,7},{7,6},{8,9},{9,8},{10,11... | collective-permute-start | bytes 786440 | tf_op jit(solution)/shard_map/ppermute | solution.py:49
  42.1 1.6 %collective-permute-start.14 = (f32[16,32,128]{2,1,0:T(8,128)S(1)}, f32[16,32,128]{2,1,0:T(8,128)S(1)}, u32[]{:S(2)}, u32[]{:S(2)}) collective-permute-start(f32[16,32,128]{2,1,0:T(8,128)S(1)} %outer.6.refs_2_), channel_id=1, source_target_pairs={{0,1},{1,0},{2,3},{3,2},{4,5},{5,4},{6,7},{7,6},{8,9},{9,8},{10,11... | collective-permute-start | bytes 786440 | tf_op jit(solution)/shard_map/ppermute | solution.py:49
  42.2 3.3 %collective-permute-start.15 = (f32[16,32,128]{2,1,0:T(8,128)S(1)}, f32[16,32,128]{2,1,0:T(8,128)S(1)}, u32[]{:S(2)}, u32[]{:S(2)}) collective-permute-start(f32[16,32,128]{2,1,0:T(8,128)S(1)} %outer.5.refs_5_.refs_1_), channel_id=1, source_target_pairs={{0,1},{1,0},{2,3},{3,2},{4,5},{5,4},{6,7},{7,6},{8,9},{9,8},{10,11... | collective-permute-start | bytes 786440 | tf_op jit(solution)/shard_map/ppermute | solution.py:49
  43.0 2.4 %collective-permute-start.16 = (f32[16,32,128]{2,1,0:T(8,128)S(1)}, f32[16,32,128]{2,1,0:T(8,128)S(1)}, u32[]{:S(2)}, u32[]{:S(2)}) collective-permute-start(f32[16,32,128]{2,1,0:T(8,128)S(1)} %outer.7.refs_3_), channel_id=1, source_target_pairs={{0,1},{1,0},{2,3},{3,2},{4,5},{5,4},{6,7},{7,6},{8,9},{9,8},{10,11... | collective-permute-start | bytes 786440 | tf_op jit(solution)/shard_map/ppermute | solution.py:49
  47.2 7.8 %collective-permute-start.17 = (f32[32,640]{1,0:T(8,128)S(1)}, f32[32,640]{1,0:T(8,128)S(1)}, u32[]{:S(2)}, u32[]{:S(2)}) collective-permute-start(f32[32,640]{1,0:T(8,128)S(1)} %get-tuple-element.36), channel_id=1, source_target_pairs={{0,8},{4,12},{8,0},{12,4},{1,9},{5,13},{9,1},{13,5},{2,10},{6,14},... | collective-permute-start | bytes 245768 | tf_op jit(solution)/shard_map/ppermute | solution.py:49
  48.1 7.0 %collective-permute-start.18 = (f32[32,640]{1,0:T(8,128)S(1)}, f32[32,640]{1,0:T(8,128)S(1)}, u32[]{:S(2)}, u32[]{:S(2)}) collective-permute-start(f32[32,640]{1,0:T(8,128)S(1)} %get-tuple-element.37), channel_id=1, source_target_pairs={{0,4},{4,0},{8,12},{12,8},{1,5},{5,1},{9,13},{13,9},{2,6},{6,2},{1... | collective-permute-start | bytes 245768 | tf_op jit(solution)/shard_map/ppermute | solution.py:49
  49.8 6.3 %collective-permute-start.19 = (f32[32,640]{1,0:T(8,128)S(1)}, f32[32,640]{1,0:T(8,128)S(1)}, u32[]{:S(2)}, u32[]{:S(2)}) collective-permute-start(f32[32,640]{1,0:T(8,128)S(1)} %get-tuple-element.38), channel_id=1, source_target_pairs={{0,12},{4,8},{8,4},{12,0},{1,13},{5,9},{9,5},{13,1},{2,14},{6,10},... | collective-permute-start | bytes 245768 | tf_op jit(solution)/shard_map/ppermute | solution.py:49
